TPU v7x, 32 devices: a whole 2x2x4 slice. The times are simulated.
32 devices in a mesh: tm: 8 (over y, x, core), ens: 4 (over z).
Axes of the slice: x: 2, y: 2, z: 4, core: 2. Of those that a mesh axis runs over, the one named last changes fastest.
Arguments:
- propagators: float32 [4, 8, 512, 512], P('ens', 'tm'), may hold values from -1 to 1, as said below
- weights: float32 [4], P('ens'), may hold values from 2 to 8
- target: float32 [512, 512], replicated, may hold values from -1 to 1, as said below
Outputs:
- gradient: float32 [512, 8, 512], P('ens', 'tm')
Inputs may be any that keep to these rules, and one draw needn't show every extreme that they name: Every propagators[m, t] is an orthogonal 512 x 512 matrix up to float32 rounding. target is an orthogonal 512 x 512 matrix up to float32 rounding.
All inputs are finite; a program needn't handle non-finite values.
Results may differ from a plain program's by a relative error of at most 0.0003.
Values sent between devices are 32-bit elements; how exact they have to be, the bound alone decides.
No kernel may reach another device: no remote copies, remote signals or barrier semaphores. Data moves between devices by JAX's collectives and lax.ppermute only.
A program may use at most 128 MiB of HBM per device.

v0:
```python
import jax
import jax.numpy as jnp
from jax import lax
from jax.sharding import PartitionSpec as P

highest = lax.Precision.HIGHEST


def carried_in(part, axis, combine, identity, reverse):
    count = lax.axis_size(axis)
    place = lax.axis_index(axis)
    ahead = count - 1 - place if reverse else place
    gathered = lax.all_gather(part, axis)
    state = jnp.zeros_like(part) + jnp.asarray(identity, part.dtype)

    def one(lap, state):
        source = count - 1 - lap if reverse else lap
        return combine(state, lax.dynamic_index_in_dim(gathered, source, 0, False))

    return lax.fori_loop(0, ahead, one, state)


def multiply(left_side, right_side):
    return jnp.einsum("mij,mjk->mik", left_side, right_side, precision=highest)


def compose_forward(earlier, later):
    return multiply(later, earlier)


def compose_backward(earlier, later):
    return multiply(earlier, later)


def shards(propagators, weights, target):
    slices = propagators.shape[1]
    order = target.shape[0]
    block_product = propagators[:, 0]
    identity = jnp.broadcast_to(jnp.eye(order, dtype=jnp.float32), block_product.shape)
    before = carried_in(block_product, "tm", compose_forward, identity, False)
    running = before
    running = multiply(propagators[:, 0], running)
    collected = [running]
    stacked = jnp.stack(collected, axis=1)
    last_prefix = stacked[:, slices - 1]
    after = carried_in(block_product, "tm", compose_backward, identity, True)
    final_product = multiply(after, last_prefix)
    twisted = jnp.einsum("ki,mkj->mij", target, final_product, precision=highest)
    skew_part = weights[:, None, None] * (twisted - jnp.swapaxes(twisted, 1, 2)) * 0.5
    right_factor = jnp.einsum("mij,mtkj->mtik", skew_part, stacked, precision=highest)
    return lax.psum_scatter(
        jnp.einsum("mtik,mtkj->itj", stacked, right_factor, precision=highest),
        "ens",
        scatter_dimension=0,
        tiled=True,
    )


def solution(mesh):
    placed = (P("ens", "tm", None, None), P("ens"), P())
    return jax.shard_map(
        shards, mesh=mesh, in_specs=placed, out_specs=P("ens", "tm", None), check_vma=False
    )
```

profile of v0, /device:TPU:0, one launch (start us, length us, event | category | flops | bytes accessed | tf_op | source)
XLA Modules:
  0.0 145.6 jit_solution(10854702814904647690)
XLA Ops:
  6.5 0.0 copy-start
  6.5 0.0 all-gather.2.cloned.1.call-start
  6.5 0.7 all-gather.2.cloned.1.call-update
  7.3 0.0 reduce-scatter.2.cloned.1.call-start
  7.3 0.1 fusion.17
  7.4 0.3 copy.7
  8.4 57.9 %all-gather.2.cloned.1.call-done = f32[8,1,512,512]{3,2,1,0:T(8,128)} async-done(((f32[1,1,512,512]{3,2,1,0:T(8,128)}), f32[8,1,512,512]{3,2,1,0:T(8,128)}) %all-gather.2.cloned.1.call-update) | async-done | bytes 8388624 | tf_op jit(solution)/shard_map/all_gather | solution.py:13
  66.4 5.7 %fusion.14 = f32[512,512]{1,0:T(8,128)} fusion(f32[1,1,512,512]{3,2,1,0:T(8,128)} %param.7, f32[1,512,512]{2,1,0:T(8,128)S(1)} %get-tuple-element.84), kind=kOutput, calls=%fused_computation.19 | convolution fusion | flops 1610612736 | bytes 3145728 | tf_op jit(solution)/shard_map/mij,mjk->mik/dot_general | solution.py:24
  72.1 0.0 copy-start.1
  72.1 22.6 %while.23 = (s32[]{:T(128)}, f32[1,512,512]{1,2,0:T(8,128)S(1)}, s32[]{:T(128)}, f32[8,1,512,512]{3,2,1,0:T(8,128)}, s32[]{:T(128)}, /*index=5*/s32[]{:T(128)}, s32[]{:T(128)}, s32[]{:T(128)}) while((s32[]{:T(128)}, f32[1,512,512]{1,2,0:T(8,128)S(1)}, s32[]{:T(128)}, f32[8,1,512,512]{3,2,1,0:T(8,128)}, s32[]{:T(128)}, /*index=5*/s32[]{:T(128)}, ...), condition=%wide.region_3.4_spmd, body=%wide.region_2.3_spmd.sunk | while | flops 1610612736 | bytes 5243015 | solution.py:20
  72.1 0.1 copy.26
  72.2 3.2 %convolution_bitcast_fusion.8 = f32[1,512,512]{1,2,0:T(8,128)S(1)} fusion(f32[1,512,512]{1,2,0:T(8,128)S(1)} %copy.26, f32[8,1,512,512]{3,2,1,0:T(8,128)} %get-tuple-element.202, s32[]{:T(128)S(6)} %select_n.14), kind=kOutput, calls=%fused_computation.5.clone.1 | convolution fusion | flops 1610612736 | bytes 3145732 | tf_op jit(solution)/shard_map/while/body/mij,mjk->mik/dot_general | solution.py:24
  75.4 0.1 copy.26
  75.5 3.1 %convolution_bitcast_fusion.8 = f32[1,512,512]{1,2,0:T(8,128)S(1)} fusion(f32[1,512,512]{1,2,0:T(8,128)S(1)} %copy.26, f32[8,1,512,512]{3,2,1,0:T(8,128)} %get-tuple-element.202, s32[]{:T(128)S(6)} %select_n.14), kind=kOutput, calls=%fused_computation.5.clone.1 | convolution fusion | flops 1610612736 | bytes 3145732 | tf_op jit(solution)/shard_map/while/body/mij,mjk->mik/dot_general | solution.py:24
  78.6 0.1 copy.26
  78.6 3.1 %convolution_bitcast_fusion.8 = f32[1,512,512]{1,2,0:T(8,128)S(1)} fusion(f32[1,512,512]{1,2,0:T(8,128)S(1)} %copy.26, f32[8,1,512,512]{3,2,1,0:T(8,128)} %get-tuple-element.202, s32[]{:T(128)S(6)} %select_n.14), kind=kOutput, calls=%fused_computation.5.clone.1 | convolution fusion | flops 1610612736 | bytes 3145732 | tf_op jit(solution)/shard_map/while/body/mij,mjk->mik/dot_general | solution.py:24
  81.8 0.1 copy.26
  81.8 3.1 %convolution_bitcast_fusion.8 = f32[1,512,512]{1,2,0:T(8,128)S(1)} fusion(f32[1,512,512]{1,2,0:T(8,128)S(1)} %copy.26, f32[8,1,512,512]{3,2,1,0:T(8,128)} %get-tuple-element.202, s32[]{:T(128)S(6)} %select_n.14), kind=kOutput, calls=%fused_computation.5.clone.1 | convolution fusion | flops 1610612736 | bytes 3145732 | tf_op jit(solution)/shard_map/while/body/mij,mjk->mik/dot_general | solution.py:24
  84.9 0.1 copy.26
  85.0 3.1 %convolution_bitcast_fusion.8 = f32[1,512,512]{1,2,0:T(8,128)S(1)} fusion(f32[1,512,512]{1,2,0:T(8,128)S(1)} %copy.26, f32[8,1,512,512]{3,2,1,0:T(8,128)} %get-tuple-element.202, s32[]{:T(128)S(6)} %select_n.14), kind=kOutput, calls=%fused_computation.5.clone.1 | convolution fusion | flops 1610612736 | bytes 3145732 | tf_op jit(solution)/shard_map/while/body/mij,mjk->mik/dot_general | solution.py:24
  88.1 0.1 copy.26
  88.2 3.1 %convolution_bitcast_fusion.8 = f32[1,512,512]{1,2,0:T(8,128)S(1)} fusion(f32[1,512,512]{1,2,0:T(8,128)S(1)} %copy.26, f32[8,1,512,512]{3,2,1,0:T(8,128)} %get-tuple-element.202, s32[]{:T(128)S(6)} %select_n.14), kind=kOutput, calls=%fused_computation.5.clone.1 | convolution fusion | flops 1610612736 | bytes 3145732 | tf_op jit(solution)/shard_map/while/body/mij,mjk->mik/dot_general | solution.py:24
  91.3 0.1 copy.26
  91.4 3.1 %convolution_bitcast_fusion.8 = f32[1,512,512]{1,2,0:T(8,128)S(1)} fusion(f32[1,512,512]{1,2,0:T(8,128)S(1)} %copy.26, f32[8,1,512,512]{3,2,1,0:T(8,128)} %get-tuple-element.202, s32[]{:T(128)S(6)} %select_n.14), kind=kOutput, calls=%fused_computation.5.clone.1 | convolution fusion | flops 1610612736 | bytes 3145732 | tf_op jit(solution)/shard_map/while/body/mij,mjk->mik/dot_general | solution.py:24
  94.7 0.0 copy-done.1
  94.7 3.5 %fusion.12 = f32[512,512]{1,0:T(8,128)S(1)} fusion(f32[512,512]{1,0:T(8,128)S(1)} %copy-done.1, f32[1,512,512]{1,2,0:T(8,128)S(1)} %get-tuple-element.85), kind=kOutput, calls=%fused_computation.17 | convolution fusion | flops 1610612736 | bytes 3145728 | tf_op jit(solution)/shard_map/mij,mjk->mik/dot_general | solution.py:24
  98.2 0.0 copy-done
  98.2 1.9 %convolution_bitcast_fusion.4 = f32[1,512,512]{2,1,0:T(8,128)S(1)} fusion(f32[512,512]{1,0:T(8,128)S(1)} %fusion.12, f32[512,512]{1,0:T(8,128)S(1)} %copy-done), kind=kOutput, calls=%fused_computation.12 | convolution fusion | flops 1610612736 | bytes 3145728 | tf_op jit(solution)/shard_map/ki,mkj->mij/dot_general | solution.py:48
  100.1 1.3 copy.8
  101.4 4.7 %convolution_bitcast_fusion.3 = f32[512,512]{0,1:T(8,128)S(1)} fusion(f32[512,512]{1,0:T(8,128)S(1)} %copy-done.1, f32[1,512,512]{2,1,0:T(8,128)S(1)} %convolution_bitcast_fusion.4, f32[1,512,512]{1,2,0:T(8,128)} %copy.8, f32[]{:T(128)} %bitcast.70), kind=kOutput, calls=%fused_computation.11 | convolution fusion | flops 1611399168 | bytes 4194308 | tf_op jit(solution)/shard_map/mij,mtkj->mtik/dot_general | solution.py:50
  106.1 2.8 %convolution_bitcast_fusion.2 = f32[512,1,512]{0,2,1:T(8,128)} fusion(f32[512,512]{0,1:T(8,128)S(1)} %convolution_bitcast_fusion.3, f32[512,512]{1,0:T(8,128)S(1)} %copy-done.1), kind=kOutput, calls=%fused_computation.10 | convolution fusion | flops 1610612736 | bytes 3145728 | tf_op jit(solution)/shard_map/mtik,mtkj->itj/dot_general | solution.py:52
  108.9 0.0 reduce-scatter.2.cloned.1.call-update
  108.9 28.1 %reduce-scatter.2.cloned.1.call-done = f32[128,1,512]{0,2,1:T(8,128)} async-done(((f32[512,1,512]{0,2,1:T(8,128)}), f32[128,1,512]{0,2,1:T(8,128)}) %reduce-scatter.2.cloned.1.call-update) | async-done | bytes 262160 | tf_op jit(solution)/shard_map/reduce_scatter | solution.py:51
  137.0 1.8 %copy.9 = f32[128,1,512]{2,1,0:T(1,128)} copy(f32[128,1,512]{0,2,1:T(8,128)} %reduce-scatter.2.cloned.1.call-done) | data formatting | bytes 524288 | tf_op jit(solution)/shard_map/reduce_scatter | solution.py:51
  (1 shorter events, 0.0 us)
Async XLA Ops:
  6.5 91.7 %copy-start = (f32[512,512]{1,0:T(8,128)S(1)}, f32[512,512]{1,0:T(8,128)}, u32[]{:S(2)}) copy-start(f32[512,512]{1,0:T(8,128)} %param.9) | copy-start | bytes 3145732
  6.5 59.8 %all-gather.2.cloned.1.call-start = ((), (), s32[]{:S(2)}) async-start(), calls=%async_computation.1 | async-start | bytes 9437184 | tf_op jit(solution)/shard_map/all_gather | solution.py:13
  7.3 129.7 %reduce-scatter.2.cloned.1.call-start = ((), (), s32[]{:S(2)}) async-start(), calls=%async_computation.2 | async-start | bytes 1310720 | tf_op jit(solution)/shard_map/reduce_scatter | solution.py:51
  72.1 22.6 %copy-start.1 = (f32[512,512]{1,0:T(8,128)S(1)}, f32[512,512]{1,0:T(8,128)}, u32[]{:S(2)}) copy-start(f32[512,512]{1,0:T(8,128)} %fusion.14) | copy-start | bytes 3145732
Sparse Core Ops, SparseCore 0:
  9.2 57.0 all-gather.1
  109.0 27.8 reduce-scatter.1
where the time goes:
time: 146 us
  waiting for transfers between devices  86.7 us (59%)
  matrix products  40.2 us (28%)
  between operations  14.1 us (10%)
  local copies, waits for them, and re-layouts  3.92 us (3%)
    all_gather x1, waiting for transfers between devices, carried_in(): gathered = lax.all_gather(part, axis)  57.9 us
    dot_general x9, matrix products, multiply(): return jnp.einsum('mij,mjk->mik', left_side, right_side, precision=highest)  30.9 us
    reduce_scatter x1, waiting for transfers between devices, shards(): lax.psum_scatter(jnp.einsum('mtik,mtkj->itj', stacked, right_factor, prec...  28.1 us
    dot_general x1, matrix products, shards(): jnp.einsum('mij,mtkj->mtik', skew_part, stacked, precision=highest)  4.7 us
  transfers between devices with their start and end apart: 2, of which 2 were waited for; matrix products, arithmetic and copies ran while one was open for 0% of the time, Pallas kernels for 0%

commit v1 on v0

v1 whole, which is shorter than its diff:
```python
import functools

import jax
import jax.numpy as jnp
from jax import lax
from jax.experimental import pallas as pl
from jax.experimental.pallas import tpu as pltpu
from jax.sharding import PartitionSpec as P

LANES = 128
f32, bf16 = jnp.float32, jnp.bfloat16


def split(x):
    high = x.astype(bf16)
    return high, (x - high.astype(f32)).astype(bf16)


def product(a, b):
    (ah, al), (bh, bl) = split(a), split(b)
    dot = functools.partial(jnp.dot, preferred_element_type=f32)
    return dot(ah, bh) + (dot(al, bh) + dot(ah, bl))


def bit(level):
    return lax.rem(lax.div(lax.axis_index("tm"), 1 << level), 2)


def call(kernel, outs, *operands, scratch=()):
    return pl.pallas_call(
        kernel,
        out_shape=[jax.ShapeDtypeStruct(s, f32) for s in outs],
        in_specs=[pl.BlockSpec(memory_space=pltpu.VMEM)] * len(operands),
        out_specs=[pl.BlockSpec(memory_space=pltpu.VMEM)] * len(outs),
        scratch_shapes=[pltpu.VMEM(s, f32) for s in scratch],
        compiler_params=pltpu.CompilerParams(vmem_limit_bytes=48 << 20),
    )(*operands)


def place(full, mine, other):
    half = mine.shape[0]
    core = bit(0)
    full[pl.ds(pl.multiple_of(core * half, half), half), :] = mine[...]
    full[pl.ds(pl.multiple_of((1 - core) * half, half), half), :] = other[...]


def pair_kernel(mine, other, own, send, left, right, lo, hi, whole):
    core, turned = bit(0), bit(1)
    half = send.shape[0]
    order = mine.shape[0]

    @pl.when(core == 0)
    def _():
        lo[...] = mine[...]
        hi[...] = other[...]

    @pl.when(core == 1)
    def _():
        lo[...] = other[...]
        hi[...] = mine[...]

    both = product(hi[...], lo[...])
    identity = (lax.broadcasted_iota(jnp.int32, (order, order), 0) == lax.broadcasted_iota(jnp.int32, (order, order), 1)).astype(f32)
    rows = pl.ds(pl.multiple_of(core * half, half), half)

    @pl.when(turned == 0)
    def _():
        own[...] = both
        whole[...] = both.T

    @pl.when(turned == 1)
    def _():
        own[...] = both.T
        whole[...] = both

    send[...] = whole[rows, :]

    @pl.when((core == 0) & (turned == 0))
    def _():
        left[...] = lo[...]
        right[...] = hi[...]

    @pl.when((core == 0) & (turned == 1))
    def _():
        left[...] = hi[...].T
        right[...] = lo[...].T

    @pl.when((core == 1) & (turned == 0))
    def _():
        left[...] = both
        right[...] = identity

    @pl.when((core == 1) & (turned == 1))
    def _():
        left[...] = identity
        right[...] = both.T


def turn_kernel(level, mine, other, left, right, got, got_other, own, send, left_out, right_out, full):
    core = bit(0)
    half = send.shape[0]
    flip = bit(level) != bit(level + 1)
    place(full, got, got_other)
    new_right = product(full[...], right[...])
    place(full, mine, other)

    @pl.when(flip)
    def _():
        own[...] = full[...].T
        left_out[...] = new_right.T
        right_out[...] = left[...].T

    @pl.when(jnp.logical_not(flip))
    def _():
        own[...] = full[...]
        full[...] = full[...].T
        left_out[...] = left[...]
        right_out[...] = new_right

    send[...] = full[pl.ds(pl.multiple_of(core * half, half), half), :]


def half_kernel(got, own, out):
    out[...] = product(got[...], own[...])


def factor_kernel(top, got, got_other, left, right, target, left_out, right_out, full):
    turned, later = bit(top - 1), bit(top)
    place(full, got, got_other)
    full[...] = product(full[...], right[...])
    left_out[...] = left[...]
    right_out[...] = full[...]

    @pl.when((later == 0) & (turned == 0))
    def _():
        left_out[...] = product(left[...], target[...].T)

    @pl.when((later == 0) & (turned == 1))
    def _():
        right_out[...] = product(target[...], full[...])

    @pl.when((later == 1) & (turned == 0))
    def _():
        right_out[...] = product(target[...].T, full[...])

    @pl.when((later == 1) & (turned == 1))
    def _():
        left_out[...] = product(left[...], target[...])


def gradient_kernel(top, mine, other, left, right, weight, *rest):
    blocks, (full, terms) = rest[:-2], rest[-2:]
    place(full, mine, other)
    turned = bit(top - 1)
    scale = weight[...] * (0.5 - turned.astype(f32))
    cyclic = product(product(left[...], full[...]), right[...])
    terms[...] = scale * (cyclic - cyclic.T)
    count = len(blocks)
    rows = terms.shape[0] // count
    spread = terms.shape[1] // LANES
    place_z = lax.axis_index("ens")
    for step, block in enumerate(blocks):
        which = lax.rem(place_z + step, count)
        part = terms[pl.ds(pl.multiple_of(which * rows, rows), rows), :]
        for j in range(spread):
            block[pl.ds(j, rows, stride=spread), :] = part[:, j * LANES:(j + 1) * LANES]


def sum_kernel(*refs):
    total = refs[0][...]
    for ref in refs[1:-1]:
        total = total + ref[...]
    refs[-1][...] = total


def shards(levels, members, propagators, weights, target):
    order = target.shape[0]
    half, square = (order // 2, order), (order, order)
    slices = 1 << levels

    def swap(x, level):
        return lax.ppermute(x, "tm", [(i, i ^ (1 << level)) for i in range(slices)])

    slice_here = propagators[0, 0]
    other = swap(slice_here, 0)
    own, send, left, right = call(pair_kernel, [square, half, square, square], slice_here, other, scratch=[square] * 3)
    top = levels - 1
    for level in range(1, top):
        got = swap(send, level)
        product_half = call(half_kernel, [half], got, own)[0]
        got_other = swap(got, 0)
        if level + 1 < top:
            own, send, left, right = call(
                functools.partial(turn_kernel, level), [square, half, square, square],
                product_half, swap(product_half, 0), left, right, got, got_other, scratch=[square])
    far = swap(product_half, top)
    left, right = call(functools.partial(factor_kernel, top), [square] * 2, got, got_other, left, right, target, scratch=[square])
    spread = order // LANES
    rows = order // members
    blocks = call(
        functools.partial(gradient_kernel, top), [(rows * spread, LANES)] * members,
        far, swap(far, 0), left, right, weights.reshape(1, 1), scratch=[square] * 2)
    arrived = [blocks[0]] + [
        lax.ppermute(blocks[s], "ens", [(i, (i + s) % members) for i in range(members)]) for s in range(1, members)]
    total = call(sum_kernel, [(rows * spread, LANES)], *arrived)[0]
    return total.reshape(rows, 1, order)


def solution(mesh):
    levels = mesh.shape["tm"].bit_length() - 1
    assert mesh.shape["tm"] == 1 << levels and levels >= 3
    placed = (P("ens", "tm", None, None), P("ens"), P())
    return jax.shard_map(
        functools.partial(shards, levels, mesh.shape["ens"]),
        mesh=mesh, in_specs=placed, out_specs=P("ens", "tm", None), check_vma=False)
```

time: 146 us -> 68 us (0.47)
  the two profiles are of different devices: /device:TPU:0 before, /device:TPU:9 now
where the time goes in v1:
time: 68 us; the launch traced here: 67.8 us
  waiting for transfers between devices  45.9 us (68%)
  starting transfers between devices  10.9 us (16%)
  Pallas kernels  9 us (13%)
  local copies, waits for them, and re-layouts  1.22 us (2%)
  between operations  0.71 us (1%)
    ppermute x5, waiting for transfers between devices, swap(): return lax.ppermute(x, 'tm', [(i, i ^ 1 << level) for i in range(slices)])  23.7 us
    ppermute x3, waiting for transfers between devices, shards(): lax.ppermute(blocks[s], 'ens', [(i, (i + s) % members) for i in range(mem...  22.2 us
    pallas_call x5, Pallas kernels, call(): pl.pallas_call(kernel, out_shape=[jax.ShapeDtypeStruct(s, f32) for s in o...  9 us
    ppermute x5, starting transfers between devices, swap(): return lax.ppermute(x, 'tm', [(i, i ^ 1 << level) for i in range(slices)])  7.1 us
    ppermute x3, starting transfers between devices, shards(): lax.ppermute(blocks[s], 'ens', [(i, (i + s) % members) for i in range(mem...  3.84 us
  transfers between devices with their start and end apart: 8, of which 6 were waited for; matrix products, arithmetic and copies ran while one was open for 0% of the time, Pallas kernels for 5%

profile of v1, /device:TPU:9, one launch (start us, length us, event | category | flops | bytes accessed | tf_op | source)
XLA Modules:
  0.0 67.8 jit_solution(15118373255005503301)
XLA Ops:
  0.0 0.7 collective-permute-start
  0.7 2.5 %collective-permute-done.other = f32[512,512]{1,0:T(8,128)S(1)} collective-permute-done((f32[512,512]{1,0:T(8,128)}, f32[512,512]{1,0:T(8,128)S(1)}, u32[]{:S(2)}, u32[]{:S(2)}) %collective-permute-start) | collective-permute-done | bytes 1048608 | tf_op jit(solution)/shard_map/ppermute | solution.py:182
  3.2 0.0 copy-start
  3.2 1.2 %copy-done = f32[1,1,512,512]{3,2,1,0:T(8,128)S(1)} copy-done((f32[1,1,512,512]{3,2,1,0:T(8,128)S(1)}, f32[1,1,512,512]{3,2,1,0:T(8,128)}, u32[]{:S(2)}) %copy-start) | copy-done | bytes 1048600
  4.4 1.7 %shard_map.37 = (f32[512,512]{1,0:T(8,128)S(1)}, f32[256,512]{1,0:T(8,128)S(1)}, f32[512,512]{1,0:T(8,128)S(1)}, f32[512,512]{1,0:T(8,128)S(1)}) custom-call(f32[512,512]{1,0:T(8,128)S(1)} %bitcast.5, f32[512,512]{1,0:T(8,128)S(1)} %collective-permute-done.other), custom_call_target="tpu_custom_call" | custom-call | tf_op jit(solution)/shard_map/pallas_call | solution.py:30
  6.1 1.5 %collective-permute-start.1 = (f32[256,512]{1,0:T(8,128)S(1)}, f32[256,512]{1,0:T(8,128)S(1)}, u32[]{:S(2)}, u32[]{:S(2)}) collective-permute-start(f32[256,512]{1,0:T(8,128)S(1)} %get-tuple-element.15), channel_id=1, source_target_pairs={{0,8},{4,12},{8,0},{12,4},{16,24},{20,28},{24,16},{28,20},{1,9},{5... | collective-permute-start | bytes 1572872 | tf_op jit(solution)/shard_map/ppermute | solution.py:182
  7.6 11.7 %collective-permute-done.1.got = f32[256,512]{1,0:T(8,128)S(1)} collective-permute-done((f32[256,512]{1,0:T(8,128)S(1)}, f32[256,512]{1,0:T(8,128)S(1)}, u32[]{:S(2)}, u32[]{:S(2)}) %collective-permute-start.1) | collective-permute-done | bytes 524320 | tf_op jit(solution)/shard_map/ppermute | solution.py:182
  19.3 0.6 shard_map.38
  19.9 1.3 %collective-permute-start.2 = (f32[256,512]{1,0:T(8,128)S(1)}, f32[256,512]{1,0:T(8,128)S(1)}, u32[]{:S(2)}, u32[]{:S(2)}) collective-permute-start(f32[256,512]{1,0:T(8,128)S(1)} %shard_map.38), channel_id=1, source_target_pairs={{0,16},{4,20},{8,24},{12,28},{16,0},{20,4},{24,8},{28,12},{1,17},{... | collective-permute-start | bytes 1572872 | tf_op jit(solution)/shard_map/ppermute | solution.py:182
  21.2 1.5 %collective-permute-start.4 = (f32[256,512]{1,0:T(8,128)S(1)}, f32[256,512]{1,0:T(8,128)S(1)}, u32[]{:S(2)}, u32[]{:S(2)}) collective-permute-start(f32[256,512]{1,0:T(8,128)S(1)} %collective-permute-done.1.got), channel_id=1, source_target_pairs={{0,4},{4,0},{8,12},{12,8},{16,20},{20,16},{24,28},{28,24},{1,5},{5... | collective-permute-start | bytes 1572872 | tf_op jit(solution)/shard_map/ppermute | solution.py:182
  22.7 9.5 %collective-permute-done.2.mine = f32[256,512]{1,0:T(8,128)S(1)} collective-permute-done((f32[256,512]{1,0:T(8,128)S(1)}, f32[256,512]{1,0:T(8,128)S(1)}, u32[]{:S(2)}, u32[]{:S(2)}) %collective-permute-start.2) | collective-permute-done | bytes 524320 | tf_op jit(solution)/shard_map/ppermute | solution.py:182
  32.2 2.1 %collective-permute-start.3 = (f32[256,512]{1,0:T(8,128)S(1)}, f32[256,512]{1,0:T(8,128)S(1)}, u32[]{:S(2)}, u32[]{:S(2)}) collective-permute-start(f32[256,512]{1,0:T(8,128)S(1)} %collective-permute-done.2.mine), channel_id=1, source_target_pairs={{0,4},{4,0},{8,12},{12,8},{16,20},{20,16},{24,28},{28,24},{1,5},{5... | collective-permute-start | bytes 1572872 | tf_op jit(solution)/shard_map/ppermute | solution.py:182
  35.0 0.0 collective-permute-done.4.got_other
  35.0 3.5 %shard_map.39 = (f32[512,512]{1,0:T(8,128)S(1)}, f32[512,512]{1,0:T(8,128)S(1)}) custom-call(f32[256,512]{1,0:T(8,128)S(1)} %collective-permute-done.1.got, f32[256,512]{1,0:T(8,128)S(1)} %collective-permute-done.4.got_other, f32[512,512]{1,0:T(8,128)S(1)} %get-tuple-element.17.left, f32[512,512]{1,0:T(8,128)S(1)} %get-tuple-element.18.right, f32[512,512]{1,0:T(8,128)} %target.1), custom_call_target="tpu_custom_call" | custom-call | tf_op jit(solution)/shard_map/pallas_call | solution.py:30
  38.5 0.0 collective-permute-done.3.other
  38.5 2.4 %shard_map.40 = (f32[512,128]{1,0:T(8,128)S(1)}, f32[512,128]{1,0:T(8,128)S(1)}, f32[512,128]{1,0:T(8,128)S(1)}, f32[512,128]{1,0:T(8,128)S(1)}) custom-call(f32[256,512]{1,0:T(8,128)S(1)} %collective-permute-done.2.mine, f32[256,512]{1,0:T(8,128)S(1)} %collective-permute-done.3.other, f32[512,512]{1,0:T(8,128)S(1)} %get-tuple-element.19.left, ...), custom_call_target="tpu_custom_call" | custom-call | tf_op jit(solution)/shard_map/pallas_call | solution.py:30
  41.0 1.4 %collective-permute-start.5 = (f32[512,128]{1,0:T(8,128)S(1)}, f32[512,128]{1,0:T(8,128)S(1)}, u32[]{:S(2)}, u32[]{:S(2)}) collective-permute-start(f32[512,128]{1,0:T(8,128)S(1)} %get-tuple-element.22), channel_id=1, source_target_pairs={{0,1},{1,2},{2,3},{3,0},{4,5},{5,6},{6,7},{7,4},{8,9},{9,10},{10,1... | collective-permute-start | bytes 786440 | tf_op jit(solution)/shard_map/ppermute | solution.py:204
  42.3 1.1 %collective-permute-start.6 = (f32[512,128]{1,0:T(8,128)S(1)}, f32[512,128]{1,0:T(8,128)S(1)}, u32[]{:S(2)}, u32[]{:S(2)}) collective-permute-start(f32[512,128]{1,0:T(8,128)S(1)} %get-tuple-element.23), channel_id=1, source_target_pairs={{0,2},{1,3},{2,0},{3,1},{4,6},{5,7},{6,4},{7,5},{8,10},{9,11},{10,... | collective-permute-start | bytes 786440 | tf_op jit(solution)/shard_map/ppermute | solution.py:204
  43.4 1.4 %collective-permute-start.7 = (f32[512,128]{1,0:T(8,128)S(1)}, f32[512,128]{1,0:T(8,128)S(1)}, u32[]{:S(2)}, u32[]{:S(2)}) collective-permute-start(f32[512,128]{1,0:T(8,128)S(1)} %get-tuple-element.24), channel_id=1, source_target_pairs={{0,3},{1,0},{2,1},{3,2},{4,7},{5,4},{6,5},{7,6},{8,11},{9,8},{10,9... | collective-permute-start | bytes 786440 | tf_op jit(solution)/shard_map/ppermute | solution.py:204
  44.8 4.1 %collective-permute-done.5.refs_1_ = f32[512,128]{1,0:T(8,128)S(1)} collective-permute-done((f32[512,128]{1,0:T(8,128)S(1)}, f32[512,128]{1,0:T(8,128)S(1)}, u32[]{:S(2)}, u32[]{:S(2)}) %collective-permute-start.5) | collective-permute-done | bytes 262176 | tf_op jit(solution)/shard_map/ppermute | solution.py:204
  48.9 16.0 %collective-permute-done.6.refs_2_ = f32[512,128]{1,0:T(8,128)S(1)} collective-permute-done((f32[512,128]{1,0:T(8,128)S(1)}, f32[512,128]{1,0:T(8,128)S(1)}, u32[]{:S(2)}, u32[]{:S(2)}) %collective-permute-start.6) | collective-permute-done | bytes 262176 | tf_op jit(solution)/shard_map/ppermute | solution.py:204
  64.9 2.1 %collective-permute-done.7.refs_3_ = f32[512,128]{1,0:T(8,128)S(1)} collective-permute-done((f32[512,128]{1,0:T(8,128)S(1)}, f32[512,128]{1,0:T(8,128)S(1)}, u32[]{:S(2)}, u32[]{:S(2)}) %collective-permute-start.7) | collective-permute-done | bytes 262176 | tf_op jit(solution)/shard_map/ppermute | solution.py:204
  67.0 0.8 %shard_map.41 = f32[512,128]{1,0:T(8,128)} custom-call(f32[512,128]{1,0:T(8,128)S(1)} %get-tuple-element.21.refs_0_, f32[512,128]{1,0:T(8,128)S(1)} %collective-permute-done.5.refs_1_, f32[512,128]{1,0:T(8,128)S(1)} %collective-permute-done.6.refs_2_, f32[512,128]{1,0:T(8,128)S(1)} %collective-permute-done.7.refs_3_), custom_call_target="tpu_custom_call" | custom-call | tf_op jit(solution)/shard_map/pallas_call | solution.py:30
Async XLA Ops:
  0.0 3.2 %collective-permute-start = (f32[512,512]{1,0:T(8,128)}, f32[512,512]{1,0:T(8,128)S(1)}, u32[]{:S(2)}, u32[]{:S(2)}) collective-permute-start(f32[512,512]{1,0:T(8,128)} %bitcast.4), channel_id=1, source_target_pairs={{0,4},{4,0},{8,12},{12,8},{16,20},{20,16},{24,28},{28,24},{1,5},{5... | collective-permute-start | bytes 3145736 | tf_op jit(solution)/shard_map/ppermute | solution.py:182
  3.2 1.2 %copy-start = (f32[1,1,512,512]{3,2,1,0:T(8,128)S(1)}, f32[1,1,512,512]{3,2,1,0:T(8,128)}, u32[]{:S(2)}) copy-start(f32[1,1,512,512]{3,2,1,0:T(8,128)} %param.3) | copy-start | bytes 3145732
  6.1 13.2 %collective-permute-start.1 = (f32[256,512]{1,0:T(8,128)S(1)}, f32[256,512]{1,0:T(8,128)S(1)}, u32[]{:S(2)}, u32[]{:S(2)}) collective-permute-start(f32[256,512]{1,0:T(8,128)S(1)} %get-tuple-element.15), channel_id=1, source_target_pairs={{0,8},{4,12},{8,0},{12,4},{16,24},{20,28},{24,16},{28,20},{1,9},{5... | collective-permute-start | bytes 1572872 | tf_op jit(solution)/shard_map/ppermute | solution.py:182
  19.9 12.3 %collective-permute-start.2 = (f32[256,512]{1,0:T(8,128)S(1)}, f32[256,512]{1,0:T(8,128)S(1)}, u32[]{:S(2)}, u32[]{:S(2)}) collective-permute-start(f32[256,512]{1,0:T(8,128)S(1)} %shard_map.38), channel_id=1, source_target_pairs={{0,16},{4,20},{8,24},{12,28},{16,0},{20,4},{24,8},{28,12},{1,17},{... | collective-permute-start | bytes 1572872 | tf_op jit(solution)/shard_map/ppermute | solution.py:182
  21.2 13.8 %collective-permute-start.4 = (f32[256,512]{1,0:T(8,128)S(1)}, f32[256,512]{1,0:T(8,128)S(1)}, u32[]{:S(2)}, u32[]{:S(2)}) collective-permute-start(f32[256,512]{1,0:T(8,128)S(1)} %collective-permute-done.1.got), channel_id=1, source_target_pairs={{0,4},{4,0},{8,12},{12,8},{16,20},{20,16},{24,28},{28,24},{1,5},{5... | collective-permute-start | bytes 1572872 | tf_op jit(solution)/shard_map/ppermute | solution.py:182
  32.2 6.3 %collective-permute-start.3 = (f32[256,512]{1,0:T(8,128)S(1)}, f32[256,512]{1,0:T(8,128)S(1)}, u32[]{:S(2)}, u32[]{:S(2)}) collective-permute-start(f32[256,512]{1,0:T(8,128)S(1)} %collective-permute-done.2.mine), channel_id=1, source_target_pairs={{0,4},{4,0},{8,12},{12,8},{16,20},{20,16},{24,28},{28,24},{1,5},{5... | collective-permute-start | bytes 1572872 | tf_op jit(solution)/shard_map/ppermute | solution.py:182
  41.0 8.0 %collective-permute-start.5 = (f32[512,128]{1,0:T(8,128)S(1)}, f32[512,128]{1,0:T(8,128)S(1)}, u32[]{:S(2)}, u32[]{:S(2)}) collective-permute-start(f32[512,128]{1,0:T(8,128)S(1)} %get-tuple-element.22), channel_id=1, source_target_pairs={{0,1},{1,2},{2,3},{3,0},{4,5},{5,6},{6,7},{7,4},{8,9},{9,10},{10,1... | collective-permute-start | bytes 786440 | tf_op jit(solution)/shard_map/ppermute | solution.py:204
  42.3 22.6 %collective-permute-start.6 = (f32[512,128]{1,0:T(8,128)S(1)}, f32[512,128]{1,0:T(8,128)S(1)}, u32[]{:S(2)}, u32[]{:S(2)}) collective-permute-start(f32[512,128]{1,0:T(8,128)S(1)} %get-tuple-element.23), channel_id=1, source_target_pairs={{0,2},{1,3},{2,0},{3,1},{4,6},{5,7},{6,4},{7,5},{8,10},{9,11},{10,... | collective-permute-start | bytes 786440 | tf_op jit(solution)/shard_map/ppermute | solution.py:204
  43.4 23.6 %collective-permute-start.7 = (f32[512,128]{1,0:T(8,128)S(1)}, f32[512,128]{1,0:T(8,128)S(1)}, u32[]{:S(2)}, u32[]{:S(2)}) collective-permute-start(f32[512,128]{1,0:T(8,128)S(1)} %get-tuple-element.24), channel_id=1, source_target_pairs={{0,3},{1,0},{2,1},{3,2},{4,7},{5,4},{6,5},{7,6},{8,11},{9,8},{10,9... | collective-permute-start | bytes 786440 | tf_op jit(solution)/shard_map/ppermute | solution.py:204

commit v2 on v1

v2 whole, which is shorter than its diff:
```python
import functools

import jax
import jax.numpy as jnp
from jax import lax
from jax.experimental import pallas as pl
from jax.experimental.pallas import tpu as pltpu
from jax.sharding import PartitionSpec as P

LANES = 128
PIECES = (1, 1, 1, 1)
f32, bf16 = jnp.float32, jnp.bfloat16


def split(x):
    high = x.astype(bf16)
    return high, (x - high.astype(f32)).astype(bf16)


def product(a, b, b_turned=False):
    (ah, al), (bh, bl) = split(a), split(b)
    dims = (((1,), (1 if b_turned else 0,)), ((), ()))
    dot = functools.partial(lax.dot_general, dimension_numbers=dims, preferred_element_type=f32)
    return dot(ah, bh) + (dot(al, bh) + dot(ah, bl))


def bit(level):
    return lax.rem(lax.div(lax.axis_index("tm"), 1 << level), 2)


def call(kernel, outs, *operands, scratch=()):
    return pl.pallas_call(
        kernel,
        out_shape=[jax.ShapeDtypeStruct(s, f32) for s in outs],
        in_specs=[pl.BlockSpec(memory_space=pltpu.VMEM)] * len(operands),
        out_specs=[pl.BlockSpec(memory_space=pltpu.VMEM)] * len(outs),
        scratch_shapes=[pltpu.VMEM(s, f32) for s in scratch],
        compiler_params=pltpu.CompilerParams(vmem_limit_bytes=48 << 20),
    )(*operands)


def place(full, mine, other):
    half = full.shape[0] // 2
    core = bit(0)
    for pieces, base in ((mine, core * half), (other, (1 - core) * half)):
        at = 0
        for piece in pieces:
            rows = piece.shape[0]
            full[pl.ds(pl.multiple_of(base + at, 8), rows), :] = piece[...]
            at += rows


def cut(rows, pieces):
    at = 0
    for piece in pieces:
        piece[...] = rows[at:at + piece.shape[0], :]
        at += piece.shape[0]


def early_kernel(slice_here, target, mine):
    first = lax.axis_index("tm") == 0

    @pl.when(first)
    def _():
        mine[...] = product(slice_here[...], target[...], b_turned=True)

    @pl.when(jnp.logical_not(first))
    def _():
        mine[...] = slice_here[...]


def send_kernel(mine, other, target, *rest):
    sends, columns = rest[:-1], rest[-1]
    core, turned = bit(0), bit(1)
    half = mine.shape[0] // 2

    @pl.when((turned == 0) & (core == 0))
    def _():
        cut(product(other[...], mine[:, :half]).T, sends)

    @pl.when((turned == 0) & (core == 1))
    def _():
        columns[...] = other[:, half:]

        @pl.when(lax.axis_index("tm") == 1)
        def _():
            columns[...] = product(other[...], target[half:, :], b_turned=True)

        cut(product(mine[...], columns[...]).T, sends)

    @pl.when((turned == 1) & (core == 0))
    def _():
        cut(product(other[:half, :], mine[...]), sends)

    @pl.when((turned == 1) & (core == 1))
    def _():
        cut(product(mine[half:, :], other[...]), sends)


def own_kernel(mine, other, target, own, left, right, lo, hi):
    core, turned = bit(0), bit(1)
    order = mine.shape[0]

    @pl.when(core == 0)
    def _():
        lo[...] = mine[...]
        hi[...] = other[...]

    @pl.when(core == 1)
    def _():
        lo[...] = other[...]
        hi[...] = mine[...]

        @pl.when(lax.axis_index("tm") == 1)
        def _():
            lo[...] = product(other[...], target[...], b_turned=True)

    both = product(hi[...], lo[...])
    identity = (lax.broadcasted_iota(jnp.int32, (order, order), 0) == lax.broadcasted_iota(jnp.int32, (order, order), 1)).astype(f32)

    @pl.when(turned == 0)
    def _():
        own[...] = both

        @pl.when(core == 0)
        def _():
            left[...] = lo[...]
            right[...] = hi[...]

        @pl.when(core == 1)
        def _():
            left[...] = both
            right[...] = identity

    @pl.when(turned == 1)
    def _():
        over = both.T
        own[...] = over

        @pl.when(core == 0)
        def _():
            left[...] = hi[...].T
            right[...] = lo[...].T

        @pl.when(core == 1)
        def _():
            left[...] = identity
            right[...] = over


def turn_kernel(level, count, *refs):
    mine, other, got, got_other = (refs[i * count:(i + 1) * count] for i in range(4))
    left, right, own, left_out, right_out = refs[4 * count:4 * count + 5]
    sends, full = refs[4 * count + 5:-1], refs[-1]
    half = full.shape[0] // 2
    flip = bit(level) != bit(level + 1)
    place(full, got, got_other)
    new_right = product(full[...], right[...])
    place(full, mine, other)

    @pl.when(flip)
    def _():
        own[...] = full[...].T
        left_out[...] = new_right.T
        right_out[...] = left[...].T

    @pl.when(jnp.logical_not(flip))
    def _():
        own[...] = full[...]
        full[...] = full[...].T
        left_out[...] = left[...]
        right_out[...] = new_right

    cut(full[pl.ds(pl.multiple_of(bit(0) * half, 8), half), :], sends)


def half_kernel(got, own, out):
    out[...] = product(got[...], own[...])


def factor_kernel(count, *refs):
    right, out, full = refs[2 * count:]
    place(full, refs[:count], refs[count:2 * count])
    out[...] = product(full[...], right[...])


def gradient_kernel(turned_level, count, order_of, *refs):
    left, right, weight = refs[2 * count:2 * count + 3]
    blocks, (full, terms) = refs[2 * count + 3:-2], refs[-2:]
    place(full, refs[:count], refs[count:2 * count])
    scale = weight[...] * (0.5 - bit(turned_level).astype(f32))
    cyclic = product(left[...], product(full[...], right[...]))
    terms[...] = scale * (cyclic - cyclic.T)
    rows = terms.shape[0] // len(blocks)
    spread = terms.shape[1] // LANES
    here = lax.axis_index("ens")
    for step, block in enumerate(blocks):
        part = terms[pl.ds(pl.multiple_of(order_of(here, step) * rows, 8), rows), :]
        for j in range(spread):
            block[pl.ds(j, rows, stride=spread), :] = part[:, j * LANES:(j + 1) * LANES]


def sum_kernel(*refs):
    terms, out = refs[:-1], refs[-1]
    here = lax.axis_index("ens")
    total = terms[0][...]
    for term in terms[1:-1]:
        total = total + term[...]
    out[...] = total

    @pl.when((here == 0) | (here == 3))
    def _():
        out[...] = total + terms[-1][...]


def plain_sum_kernel(*refs):
    total = refs[0][...]
    for ref in refs[1:-1]:
        total = total + ref[...]
    refs[-1][...] = total


def reduce_rows(blocks, shape):
    members = len(blocks)

    def move(x, pairs):
        return lax.ppermute(x, "ens", pairs)

    if members == 4:
        over_two = move(blocks[2], [(0, 1), (1, 3), (3, 2), (2, 0)])
        across = move(blocks[3], [(0, 3), (3, 0)])
        beside = move(blocks[1], [(0, 1), (1, 0), (2, 3), (3, 2)])
        joined = move(blocks[3] + over_two, [(1, 2), (2, 1)])
        return call(sum_kernel, [shape], blocks[0], beside, across, joined, over_two)[0]
    arrived = [move(blocks[s], [(i, (i + s) % members) for i in range(members)]) for s in range(1, members)]
    return call(plain_sum_kernel, [shape], blocks[0], *arrived)[0]


def shards(levels, members, propagators, weights, target):
    order = target.shape[0]
    square = (order, order)
    slices = 1 << levels
    count = len(PIECES)
    pieces = [(order // 2 * p // sum(PIECES), order) for p in PIECES]

    def swap(x, level):
        return lax.ppermute(x, "tm", [(i, i ^ (1 << level)) for i in range(slices)])

    slice_here = propagators[0, 0]
    other = swap(slice_here, 0)
    mine = call(early_kernel, [square], slice_here, target)[0]
    sends = call(send_kernel, pieces, mine, other, target, scratch=[(order, order // 2)])
    own, left, right = call(own_kernel, [square] * 3, mine, other, target, scratch=[square] * 2)
    top = levels - 1
    for level in range(1, top):
        got = [swap(s, level) for s in sends]
        products = [call(half_kernel, [g.shape], g, own)[0] for g in got]
        got_other = [swap(g, 0) for g in got]
        if level + 1 < top:
            outs = call(
                functools.partial(turn_kernel, level, count), [square] * 3 + pieces,
                *products, *[swap(p, 0) for p in products], *got, *got_other, left, right, scratch=[square])
            (own, left, right), sends = outs[:3], outs[3:]
    far = [swap(p, top) for p in products]
    right = call(functools.partial(factor_kernel, count), [square], *got, *got_other, right, scratch=[square])[0]
    far_other = [swap(f, 0) for f in far]
    rows, spread = order // members, order // LANES
    block = (rows * spread, LANES)
    order_of = (lambda here, step: here ^ step) if members == 4 else (lambda here, step: lax.rem(here + step, members))
    blocks = call(
        functools.partial(gradient_kernel, top - 1, count, order_of), [block] * members,
        *far, *far_other, left, right, weights.reshape(1, 1), scratch=[square] * 2)
    return reduce_rows(blocks, block).reshape(rows, 1, order)


def solution(mesh):
    levels = mesh.shape["tm"].bit_length() - 1
    assert mesh.shape["tm"] == 1 << levels and levels >= 3
    placed = (P("ens", "tm", None, None), P("ens"), P())
    return jax.shard_map(
        functools.partial(shards, levels, mesh.shape["ens"]),
        mesh=mesh, in_specs=placed, out_specs=P("ens", "tm", None), check_vma=False)
```

time: 68 us -> 56 us (0.82)
  the two profiles are of different devices: /device:TPU:9 before, /device:TPU:0 now
where the time goes in v2:
time: 56 us; the launch traced here: 55.4 us
  starting transfers between devices  22.3 us (40%)
  waiting for transfers between devices  19.5 us (35%)
  Pallas kernels  10.1 us (18%)
  local copies, waits for them, and re-layouts  2.64 us (5%)
  between operations  0.81 us (1%)
    ppermute x4, waiting for transfers between devices, move(): return lax.ppermute(x, 'ens', pairs)  14.9 us
    ppermute x17, starting transfers between devices, swap(): return lax.ppermute(x, 'tm', [(i, i ^ 1 << level) for i in range(slices)])  14.8 us
    pallas_call x10, Pallas kernels, call(): pl.pallas_call(kernel, out_shape=[jax.ShapeDtypeStruct(s, f32) for s in o...  10.1 us
    ppermute x4, starting transfers between devices, move(): return lax.ppermute(x, 'ens', pairs)  7.51 us
    ppermute x17, waiting for transfers between devices, swap(): return lax.ppermute(x, 'tm', [(i, i ^ 1 << level) for i in range(slices)])  4.57 us
    unnamed x6, local copies, waits for them, and re-layouts  2.64 us
  transfers between devices with their start and end apart: 21, of which 7 were waited for; matrix products, arithmetic and copies ran while one was open for 0% of the time, Pallas kernels for 11%

profile of v2, /device:TPU:0, one launch (start us, length us, event | category | flops | bytes accessed | tf_op | source)
XLA Modules:
  0.0 55.4 jit_solution(11948798414886481533)
XLA Ops:
  0.0 0.5 collective-permute-start
  0.5 0.0 copy-start
  0.5 1.2 %copy-done = f32[512,512]{1,0:T(8,128)S(1)} copy-done((f32[512,512]{1,0:T(8,128)S(1)}, f32[512,512]{1,0:T(8,128)}, u32[]{:S(2)}) %copy-start) | copy-done | bytes 1048600
  1.7 0.0 copy-start.2
  1.7 1.2 %copy-done.2 = f32[1,1,512,512]{3,2,1,0:T(8,128)S(1)} copy-done((f32[1,1,512,512]{3,2,1,0:T(8,128)S(1)}, f32[1,1,512,512]{3,2,1,0:T(8,128)}, u32[]{:S(2)}) %copy-start.2) | copy-done | bytes 1048600
  2.9 0.0 copy-start.1
  2.9 1.0 %shard_map.37.mine = f32[512,512]{1,0:T(8,128)S(1)} custom-call(f32[512,512]{1,0:T(8,128)S(1)} %bitcast.5, f32[512,512]{1,0:T(8,128)S(1)} %copy-done), custom_call_target="tpu_custom_call" | custom-call | tf_op jit(solution)/shard_map/pallas_call | solution.py:32
  3.9 0.0 collective-permute-done.other
  3.9 0.2 copy-done.1
  4.1 0.7 %shard_map.38 = (f32[64,512]{1,0:T(8,128)S(1)}, f32[64,512]{1,0:T(8,128)S(1)}, f32[64,512]{1,0:T(8,128)S(1)}, f32[64,512]{1,0:T(8,128)S(1)}) custom-call(f32[512,512]{1,0:T(8,128)S(1)} %shard_map.37.mine, f32[512,512]{1,0:T(8,128)S(1)} %collective-permute-done.other, f32[512,512]{1,0:T(8,128)S(1)} %copy-done.1), custom_call_target="tpu_custom_call" | custom-call | tf_op jit(solution)/shard_map/pallas_call | solution.py:32
  4.8 2.5 %collective-permute-start.1 = (f32[64,512]{1,0:T(8,128)S(1)}, f32[64,512]{1,0:T(8,128)S(1)}, u32[]{:S(2)}, u32[]{:S(2)}) collective-permute-start(f32[64,512]{1,0:T(8,128)S(1)} %get-tuple-element.16), channel_id=1, source_target_pairs={{0,8},{4,12},{8,0},{12,4},{16,24},{20,28},{24,16},{28,20},{1,9},{5... | collective-permute-start | bytes 393224 | tf_op jit(solution)/shard_map/ppermute | solution.py:247
  7.3 0.1 collective-permute-start.3
  7.4 1.9 %collective-permute-start.5 = (f32[64,512]{1,0:T(8,128)S(1)}, f32[64,512]{1,0:T(8,128)S(1)}, u32[]{:S(2)}, u32[]{:S(2)}) collective-permute-start(f32[64,512]{1,0:T(8,128)S(1)} %get-tuple-element.19), channel_id=1, source_target_pairs={{0,8},{4,12},{8,0},{12,4},{16,24},{20,28},{24,16},{28,20},{1,9},{5... | collective-permute-start | bytes 393224 | tf_op jit(solution)/shard_map/ppermute | solution.py:247
  9.3 0.1 collective-permute-start.7
  9.4 2.6 %shard_map.39 = (f32[512,512]{1,0:T(8,128)S(1)}, f32[512,512]{1,0:T(8,128)S(1)}, f32[512,512]{1,0:T(8,128)S(1)}) custom-call(f32[512,512]{1,0:T(8,128)S(1)} %shard_map.37.mine, f32[512,512]{1,0:T(8,128)S(1)} %collective-permute-done.other, f32[512,512]{1,0:T(8,128)} %target.5), custom_call_target="tpu_custom_call" | custom-call | tf_op jit(solution)/shard_map/pallas_call | solution.py:32
  12.0 0.0 collective-permute-done.1.got.refs_0_
  12.0 0.4 shard_map.40
  12.4 2.1 %collective-permute-start.2 = (f32[64,512]{1,0:T(8,128)S(1)}, f32[64,512]{1,0:T(8,128)S(1)}, u32[]{:S(2)}, u32[]{:S(2)}) collective-permute-start(f32[64,512]{1,0:T(8,128)S(1)} %shard_map.40), channel_id=1, source_target_pairs={{0,16},{4,20},{8,24},{12,28},{16,0},{20,4},{24,8},{28,12},{1,17},{... | collective-permute-start | bytes 393224 | tf_op jit(solution)/shard_map/ppermute | solution.py:247
  14.5 0.0 collective-permute-done.3.got.refs_1_
  14.5 0.4 shard_map.41
  14.9 2.0 %collective-permute-start.4 = (f32[64,512]{1,0:T(8,128)S(1)}, f32[64,512]{1,0:T(8,128)S(1)}, u32[]{:S(2)}, u32[]{:S(2)}) collective-permute-start(f32[64,512]{1,0:T(8,128)S(1)} %shard_map.41), channel_id=1, source_target_pairs={{0,16},{4,20},{8,24},{12,28},{16,0},{20,4},{24,8},{28,12},{1,17},{... | collective-permute-start | bytes 393224 | tf_op jit(solution)/shard_map/ppermute | solution.py:247
  17.0 0.3 collective-permute-done.5.got.refs_2_
  17.3 0.4 shard_map.42
  17.7 2.1 %collective-permute-start.6 = (f32[64,512]{1,0:T(8,128)S(1)}, f32[64,512]{1,0:T(8,128)S(1)}, u32[]{:S(2)}, u32[]{:S(2)}) collective-permute-start(f32[64,512]{1,0:T(8,128)S(1)} %shard_map.42), channel_id=1, source_target_pairs={{0,16},{4,20},{8,24},{12,28},{16,0},{20,4},{24,8},{28,12},{1,17},{... | collective-permute-start | bytes 393224 | tf_op jit(solution)/shard_map/ppermute | solution.py:247
  19.8 0.1 collective-permute-done.7.got.refs_3_
  19.9 0.4 shard_map.43
  20.3 1.9 %collective-permute-start.8 = (f32[64,512]{1,0:T(8,128)S(1)}, f32[64,512]{1,0:T(8,128)S(1)}, u32[]{:S(2)}, u32[]{:S(2)}) collective-permute-start(f32[64,512]{1,0:T(8,128)S(1)} %shard_map.43), channel_id=1, source_target_pairs={{0,16},{4,20},{8,24},{12,28},{16,0},{20,4},{24,8},{28,12},{1,17},{... | collective-permute-start | bytes 393224 | tf_op jit(solution)/shard_map/ppermute | solution.py:247
  22.2 0.0 collective-permute-start.13
  22.2 0.0 collective-permute-done.2.refs_0_
  22.2 0.5 collective-permute-start.14
  22.8 0.0 collective-permute-done.4.refs_1_
  22.8 0.1 collective-permute-start.15
  22.8 1.6 %collective-permute-done.6.refs_2_ = f32[64,512]{1,0:T(8,128)S(1)} collective-permute-done((f32[64,512]{1,0:T(8,128)S(1)}, f32[64,512]{1,0:T(8,128)S(1)}, u32[]{:S(2)}, u32[]{:S(2)}) %collective-permute-start.6) | collective-permute-done | bytes 131104 | tf_op jit(solution)/shard_map/ppermute | solution.py:247
  24.5 0.0 collective-permute-start.16
  24.5 2.5 %collective-permute-done.8.refs_3_ = f32[64,512]{1,0:T(8,128)S(1)} collective-permute-done((f32[64,512]{1,0:T(8,128)S(1)}, f32[64,512]{1,0:T(8,128)S(1)}, u32[]{:S(2)}, u32[]{:S(2)}) %collective-permute-start.8) | collective-permute-done | bytes 131104 | tf_op jit(solution)/shard_map/ppermute | solution.py:247
  27.0 0.0 collective-permute-start.9
  27.0 0.0 collective-permute-done.13.refs_4_
  27.0 0.5 collective-permute-start.10
  27.5 0.0 collective-permute-done.14.refs_5_
  27.5 0.1 collective-permute-start.11
  27.6 0.0 collective-permute-done.15.refs_6_
  27.6 0.4 collective-permute-start.12
  28.7 0.0 collective-permute-done.16.refs_7_
  28.7 1.0 %shard_map.44.refs_9_ = f32[512,512]{1,0:T(8,128)S(1)} custom-call(f32[64,512]{1,0:T(8,128)S(1)} %collective-permute-done.1.got.refs_0_, f32[64,512]{1,0:T(8,128)S(1)} %collective-permute-done.3.got.refs_1_, f32[64,512]{1,0:T(8,128)S(1)} %collective-permute-done.5.got.refs_2_, f32[64,512]{1,0:T(8,128)S(1)} %collective-permute-done.7.got.refs_3_, ...), custom_call_target="tpu_custom_call" | custom-call | tf_op jit(solution)/shard_map/pallas_call | solution.py:32
  29.7 0.0 collective-permute-done.9.refs_4_
  29.7 0.0 collective-permute-done.10.refs_5_
  29.8 0.0 collective-permute-done.11.refs_6_
  29.8 0.0 collective-permute-done.12.refs_7_
  29.8 2.4 %shard_map.45 = (f32[512,128]{1,0:T(8,128)S(1)}, f32[512,128]{1,0:T(8,128)S(1)}, f32[512,128]{1,0:T(8,128)S(1)}, f32[512,128]{1,0:T(8,128)S(1)}) custom-call(f32[64,512]{1,0:T(8,128)S(1)} %collective-permute-done.2.refs_0_, f32[64,512]{1,0:T(8,128)S(1)} %collective-permute-done.4.refs_1_, f32[64,512]{1,0:T(8,128)S(1)} %collective-permute-done.6.refs_2_, ...), custom_call_target="tpu_custom_call" | custom-call | tf_op jit(solution)/shard_map/pallas_call | solution.py:32
  32.1 2.3 %collective-permute-start.19 = (f32[512,128]{1,0:T(8,128)S(1)}, f32[512,128]{1,0:T(8,128)S(1)}, u32[]{:S(2)}, u32[]{:S(2)}) collective-permute-start(f32[512,128]{1,0:T(8,128)S(1)} %get-tuple-element.26), channel_id=1, source_target_pairs={{0,1},{1,3},{3,2},{2,0},{4,5},{5,7},{7,6},{6,4},{8,9},{9,11},{11,1... | collective-permute-start | bytes 786440 | tf_op jit(solution)/shard_map/ppermute | solution.py:227
  34.5 2.6 %collective-permute-start.17 = (f32[512,128]{1,0:T(8,128)S(1)}, f32[512,128]{1,0:T(8,128)S(1)}, u32[]{:S(2)}, u32[]{:S(2)}) collective-permute-start(f32[512,128]{1,0:T(8,128)S(1)} %get-tuple-element.24), channel_id=1, source_target_pairs={{0,1},{1,0},{2,3},{3,2},{4,5},{5,4},{6,7},{7,6},{8,9},{9,8},{10,11... | collective-permute-start | bytes 786440 | tf_op jit(solution)/shard_map/ppermute | solution.py:227
  37.1 1.9 %collective-permute-start.18 = (f32[512,128]{1,0:T(8,128)S(1)}, f32[512,128]{1,0:T(8,128)S(1)}, u32[]{:S(2)}, u32[]{:S(2)}) collective-permute-start(f32[512,128]{1,0:T(8,128)S(1)} %get-tuple-element.25), channel_id=1, source_target_pairs={{0,3},{3,0},{4,7},{7,4},{8,11},{11,8},{12,15},{15,12},{16,19},{19,... | collective-permute-start | bytes 786440 | tf_op jit(solution)/shard_map/ppermute | solution.py:227
  39.0 3.2 %collective-permute-done.19.refs_4_ = f32[512,128]{1,0:T(8,128)S(1)} collective-permute-done((f32[512,128]{1,0:T(8,128)S(1)}, f32[512,128]{1,0:T(8,128)S(1)}, u32[]{:S(2)}, u32[]{:S(2)}) %collective-permute-start.19) | collective-permute-done | bytes 262176 | tf_op jit(solution)/shard_map/ppermute | solution.py:227
  42.2 0.7 %collective-permute-start.20 = (f32[512,128]{1,0:T(8,128)S(1)}, f32[512,128]{1,0:T(8,128)S(1)}, u32[]{:S(2)}, u32[]{:S(2)}) collective-permute-start(f32[512,128]{1,0:T(8,128)S(1)} %add.3), channel_id=1, source_target_pairs={{1,2},{2,1},{5,6},{6,5},{9,10},{10,9},{13,14},{14,13},{17,18},{18,... | collective-permute-start | bytes 786440 | tf_op jit(solution)/shard_map/ppermute | solution.py:227
  42.9 4.8 %collective-permute-done.17.refs_1_ = f32[512,128]{1,0:T(8,128)S(1)} collective-permute-done((f32[512,128]{1,0:T(8,128)S(1)}, f32[512,128]{1,0:T(8,128)S(1)}, u32[]{:S(2)}, u32[]{:S(2)}) %collective-permute-start.17) | collective-permute-done | bytes 262176 | tf_op jit(solution)/shard_map/ppermute | solution.py:227
  47.7 6.9 %collective-permute-done.18.refs_2_ = f32[512,128]{1,0:T(8,128)S(1)} collective-permute-done((f32[512,128]{1,0:T(8,128)S(1)}, f32[512,128]{1,0:T(8,128)S(1)}, u32[]{:S(2)}, u32[]{:S(2)}) %collective-permute-start.18) | collective-permute-done | bytes 262176 | tf_op jit(solution)/shard_map/ppermute | solution.py:227
  54.6 0.0 collective-permute-done.20.refs_3_
  54.6 0.8 %shard_map.46 = f32[512,128]{1,0:T(8,128)} custom-call(f32[512,128]{1,0:T(8,128)S(1)} %get-tuple-element.23.refs_0_, f32[512,128]{1,0:T(8,128)S(1)} %collective-permute-done.17.refs_1_, f32[512,128]{1,0:T(8,128)S(1)} %collective-permute-done.18.refs_2_, f32[512,128]{1,0:T(8,128)S(1)} %collective-permute-done.20.refs_3_, ...), custom_call_target="tpu_custom_call" | custom-call | tf_op jit(solution)/shard_map/pallas_call | solution.py:32
  (1 shorter events, 0.0 us)
Async XLA Ops:
  0.0 3.9 %collective-permute-start = (f32[512,512]{1,0:T(8,128)}, f32[512,512]{1,0:T(8,128)S(1)}, u32[]{:S(2)}, u32[]{:S(2)}) collective-permute-start(f32[512,512]{1,0:T(8,128)} %bitcast.4), channel_id=1, source_target_pairs={{0,4},{4,0},{8,12},{12,8},{16,20},{20,16},{24,28},{28,24},{1,5},{5... | collective-permute-start | bytes 3145736 | tf_op jit(solution)/shard_map/ppermute | solution.py:247
  0.5 1.2 %copy-start = (f32[512,512]{1,0:T(8,128)S(1)}, f32[512,512]{1,0:T(8,128)}, u32[]{:S(2)}) copy-start(f32[512,512]{1,0:T(8,128)} %target.5) | copy-start | bytes 3145732
  1.7 1.2 %copy-start.2 = (f32[1,1,512,512]{3,2,1,0:T(8,128)S(1)}, f32[1,1,512,512]{3,2,1,0:T(8,128)}, u32[]{:S(2)}) copy-start(f32[1,1,512,512]{3,2,1,0:T(8,128)} %param.3) | copy-start | bytes 3145732
  2.9 1.2 %copy-start.1 = (f32[512,512]{1,0:T(8,128)S(1)}, f32[512,512]{1,0:T(8,128)}, u32[]{:S(2)}) copy-start(f32[512,512]{1,0:T(8,128)} %target.5) | copy-start | bytes 3145732
  4.8 7.2 %collective-permute-start.1 = (f32[64,512]{1,0:T(8,128)S(1)}, f32[64,512]{1,0:T(8,128)S(1)}, u32[]{:S(2)}, u32[]{:S(2)}) collective-permute-start(f32[64,512]{1,0:T(8,128)S(1)} %get-tuple-element.16), channel_id=1, source_target_pairs={{0,8},{4,12},{8,0},{12,4},{16,24},{20,28},{24,16},{28,20},{1,9},{5... | collective-permute-start | bytes 393224 | tf_op jit(solution)/shard_map/ppermute | solution.py:247
  7.3 7.2 %collective-permute-start.3 = (f32[64,512]{1,0:T(8,128)S(1)}, f32[64,512]{1,0:T(8,128)S(1)}, u32[]{:S(2)}, u32[]{:S(2)}) collective-permute-start(f32[64,512]{1,0:T(8,128)S(1)} %get-tuple-element.18), channel_id=1, source_target_pairs={{0,8},{4,12},{8,0},{12,4},{16,24},{20,28},{24,16},{28,20},{1,9},{5... | collective-permute-start | bytes 393224 | tf_op jit(solution)/shard_map/ppermute | solution.py:247
  7.4 9.9 %collective-permute-start.5 = (f32[64,512]{1,0:T(8,128)S(1)}, f32[64,512]{1,0:T(8,128)S(1)}, u32[]{:S(2)}, u32[]{:S(2)}) collective-permute-start(f32[64,512]{1,0:T(8,128)S(1)} %get-tuple-element.19), channel_id=1, source_target_pairs={{0,8},{4,12},{8,0},{12,4},{16,24},{20,28},{24,16},{28,20},{1,9},{5... | collective-permute-start | bytes 393224 | tf_op jit(solution)/shard_map/ppermute | solution.py:247
  9.3 10.6 %collective-permute-start.7 = (f32[64,512]{1,0:T(8,128)S(1)}, f32[64,512]{1,0:T(8,128)S(1)}, u32[]{:S(2)}, u32[]{:S(2)}) collective-permute-start(f32[64,512]{1,0:T(8,128)S(1)} %get-tuple-element.20), channel_id=1, source_target_pairs={{0,8},{4,12},{8,0},{12,4},{16,24},{20,28},{24,16},{28,20},{1,9},{5... | collective-permute-start | bytes 393224 | tf_op jit(solution)/shard_map/ppermute | solution.py:247
  12.4 9.8 %collective-permute-start.2 = (f32[64,512]{1,0:T(8,128)S(1)}, f32[64,512]{1,0:T(8,128)S(1)}, u32[]{:S(2)}, u32[]{:S(2)}) collective-permute-start(f32[64,512]{1,0:T(8,128)S(1)} %shard_map.40), channel_id=1, source_target_pairs={{0,16},{4,20},{8,24},{12,28},{16,0},{20,4},{24,8},{28,12},{1,17},{... | collective-permute-start | bytes 393224 | tf_op jit(solution)/shard_map/ppermute | solution.py:247
  14.9 7.8 %collective-permute-start.4 = (f32[64,512]{1,0:T(8,128)S(1)}, f32[64,512]{1,0:T(8,128)S(1)}, u32[]{:S(2)}, u32[]{:S(2)}) collective-permute-start(f32[64,512]{1,0:T(8,128)S(1)} %shard_map.41), channel_id=1, source_target_pairs={{0,16},{4,20},{8,24},{12,28},{16,0},{20,4},{24,8},{28,12},{1,17},{... | collective-permute-start | bytes 393224 | tf_op jit(solution)/shard_map/ppermute | solution.py:247
  17.7 6.8 %collective-permute-start.6 = (f32[64,512]{1,0:T(8,128)S(1)}, f32[64,512]{1,0:T(8,128)S(1)}, u32[]{:S(2)}, u32[]{:S(2)}) collective-permute-start(f32[64,512]{1,0:T(8,128)S(1)} %shard_map.42), channel_id=1, source_target_pairs={{0,16},{4,20},{8,24},{12,28},{16,0},{20,4},{24,8},{28,12},{1,17},{... | collective-permute-start | bytes 393224 | tf_op jit(solution)/shard_map/ppermute | solution.py:247
  20.3 6.7 %collective-permute-start.8 = (f32[64,512]{1,0:T(8,128)S(1)}, f32[64,512]{1,0:T(8,128)S(1)}, u32[]{:S(2)}, u32[]{:S(2)}) collective-permute-start(f32[64,512]{1,0:T(8,128)S(1)} %shard_map.43), channel_id=1, source_target_pairs={{0,16},{4,20},{8,24},{12,28},{16,0},{20,4},{24,8},{28,12},{1,17},{... | collective-permute-start | bytes 393224 | tf_op jit(solution)/shard_map/ppermute | solution.py:247
  22.2 4.8 %collective-permute-start.13 = (f32[64,512]{1,0:T(8,128)S(1)}, f32[64,512]{1,0:T(8,128)S(1)}, u32[]{:S(2)}, u32[]{:S(2)}) collective-permute-start(f32[64,512]{1,0:T(8,128)S(1)} %collective-permute-done.1.got.refs_0_), channel_id=1, source_target_pairs={{0,4},{4,0},{8,12},{12,8},{16,20},{20,16},{24,28},{28,24},{1,5},{5... | collective-permute-start | bytes 393224 | tf_op jit(solution)/shard_map/ppermute | solution.py:247
  22.2 5.3 %collective-permute-start.14 = (f32[64,512]{1,0:T(8,128)S(1)}, f32[64,512]{1,0:T(8,128)S(1)}, u32[]{:S(2)}, u32[]{:S(2)}) collective-permute-start(f32[64,512]{1,0:T(8,128)S(1)} %collective-permute-done.3.got.refs_1_), channel_id=1, source_target_pairs={{0,4},{4,0},{8,12},{12,8},{16,20},{20,16},{24,28},{28,24},{1,5},{5... | collective-permute-start | bytes 393224 | tf_op jit(solution)/shard_map/ppermute | solution.py:247
  22.8 4.8 %collective-permute-start.15 = (f32[64,512]{1,0:T(8,128)S(1)}, f32[64,512]{1,0:T(8,128)S(1)}, u32[]{:S(2)}, u32[]{:S(2)}) collective-permute-start(f32[64,512]{1,0:T(8,128)S(1)} %collective-permute-done.5.got.refs_2_), channel_id=1, source_target_pairs={{0,4},{4,0},{8,12},{12,8},{16,20},{20,16},{24,28},{28,24},{1,5},{5... | collective-permute-start | bytes 393224 | tf_op jit(solution)/shard_map/ppermute | solution.py:247
  24.5 4.2 %collective-permute-start.16 = (f32[64,512]{1,0:T(8,128)S(1)}, f32[64,512]{1,0:T(8,128)S(1)}, u32[]{:S(2)}, u32[]{:S(2)}) collective-permute-start(f32[64,512]{1,0:T(8,128)S(1)} %collective-permute-done.7.got.refs_3_), channel_id=1, source_target_pairs={{0,4},{4,0},{8,12},{12,8},{16,20},{20,16},{24,28},{28,24},{1,5},{5... | collective-permute-start | bytes 393224 | tf_op jit(solution)/shard_map/ppermute | solution.py:247
  27.0 2.7 %collective-permute-start.9 = (f32[64,512]{1,0:T(8,128)S(1)}, f32[64,512]{1,0:T(8,128)S(1)}, u32[]{:S(2)}, u32[]{:S(2)}) collective-permute-start(f32[64,512]{1,0:T(8,128)S(1)} %collective-permute-done.2.refs_0_), channel_id=1, source_target_pairs={{0,4},{4,0},{8,12},{12,8},{16,20},{20,16},{24,28},{28,24},{1,5},{5... | collective-permute-start | bytes 393224 | tf_op jit(solution)/shard_map/ppermute | solution.py:247
  27.0 2.8 %collective-permute-start.10 = (f32[64,512]{1,0:T(8,128)S(1)}, f32[64,512]{1,0:T(8,128)S(1)}, u32[]{:S(2)}, u32[]{:S(2)}) collective-permute-start(f32[64,512]{1,0:T(8,128)S(1)} %collective-permute-done.4.refs_1_), channel_id=1, source_target_pairs={{0,4},{4,0},{8,12},{12,8},{16,20},{20,16},{24,28},{28,24},{1,5},{5... | collective-permute-start | bytes 393224 | tf_op jit(solution)/shard_map/ppermute | solution.py:247
  27.5 2.3 %collective-permute-start.11 = (f32[64,512]{1,0:T(8,128)S(1)}, f32[64,512]{1,0:T(8,128)S(1)}, u32[]{:S(2)}, u32[]{:S(2)}) collective-permute-start(f32[64,512]{1,0:T(8,128)S(1)} %collective-permute-done.6.refs_2_), channel_id=1, source_target_pairs={{0,4},{4,0},{8,12},{12,8},{16,20},{20,16},{24,28},{28,24},{1,5},{5... | collective-permute-start | bytes 393224 | tf_op jit(solution)/shard_map/ppermute | solution.py:247
  27.6 2.2 %collective-permute-start.12 = (f32[64,512]{1,0:T(8,128)S(1)}, f32[64,512]{1,0:T(8,128)S(1)}, u32[]{:S(2)}, u32[]{:S(2)}) collective-permute-start(f32[64,512]{1,0:T(8,128)S(1)} %collective-permute-done.8.refs_3_), channel_id=1, source_target_pairs={{0,4},{4,0},{8,12},{12,8},{16,20},{20,16},{24,28},{28,24},{1,5},{5... | collective-permute-start | bytes 393224 | tf_op jit(solution)/shard_map/ppermute | solution.py:247
  32.1 10.0 %collective-permute-start.19 = (f32[512,128]{1,0:T(8,128)S(1)}, f32[512,128]{1,0:T(8,128)S(1)}, u32[]{:S(2)}, u32[]{:S(2)}) collective-permute-start(f32[512,128]{1,0:T(8,128)S(1)} %get-tuple-element.26), channel_id=1, source_target_pairs={{0,1},{1,3},{3,2},{2,0},{4,5},{5,7},{7,6},{6,4},{8,9},{9,11},{11,1... | collective-permute-start | bytes 786440 | tf_op jit(solution)/shard_map/ppermute | solution.py:227
  34.5 13.2 %collective-permute-start.17 = (f32[512,128]{1,0:T(8,128)S(1)}, f32[512,128]{1,0:T(8,128)S(1)}, u32[]{:S(2)}, u32[]{:S(2)}) collective-permute-start(f32[512,128]{1,0:T(8,128)S(1)} %get-tuple-element.24), channel_id=1, source_target_pairs={{0,1},{1,0},{2,3},{3,2},{4,5},{5,4},{6,7},{7,6},{8,9},{9,8},{10,11... | collective-permute-start | bytes 786440 | tf_op jit(solution)/shard_map/ppermute | solution.py:227
  37.1 17.5 %collective-permute-start.18 = (f32[512,128]{1,0:T(8,128)S(1)}, f32[512,128]{1,0:T(8,128)S(1)}, u32[]{:S(2)}, u32[]{:S(2)}) collective-permute-start(f32[512,128]{1,0:T(8,128)S(1)} %get-tuple-element.25), channel_id=1, source_target_pairs={{0,3},{3,0},{4,7},{7,4},{8,11},{11,8},{12,15},{15,12},{16,19},{19,... | collective-permute-start | bytes 786440 | tf_op jit(solution)/shard_map/ppermute | solution.py:227
  42.2 12.4 %collective-permute-start.20 = (f32[512,128]{1,0:T(8,128)S(1)}, f32[512,128]{1,0:T(8,128)S(1)}, u32[]{:S(2)}, u32[]{:S(2)}) collective-permute-start(f32[512,128]{1,0:T(8,128)S(1)} %add.3), channel_id=1, source_target_pairs={{1,2},{2,1},{5,6},{6,5},{9,10},{10,9},{13,14},{14,13},{17,18},{18,... | collective-permute-start | bytes 786440 | tf_op jit(solution)/shard_map/ppermute | solution.py:227

commit v3 on v2

--- a/solution.py
+++ b/solution.py
@@ -57,16 +57,17 @@
         at += piece.shape[0]
 
 
-def early_kernel(slice_here, target, mine):
-    first = lax.axis_index("tm") == 0
-
-    @pl.when(first)
-    def _():
-        mine[...] = product(slice_here[...], target[...], b_turned=True)
-
-    @pl.when(jnp.logical_not(first))
-    def _():
-        mine[...] = slice_here[...]
+def early_kernel(slice_here, target, mine, target_here, arrivals):
+    copies = [
+        pltpu.make_async_copy(slice_here, mine, arrivals.at[0]), pltpu.make_async_copy(target, target_here, arrivals.at[1])]
+    for copy in copies:
+        copy.start()
+    for copy in copies:
+        copy.wait()
+
+    @pl.when(lax.axis_index("tm") == 0)
+    def _():
+        mine[...] = product(mine[...], target_here[...], b_turned=True)
 
 
 def send_kernel(mine, other, target, *rest):
@@ -184,7 +185,29 @@
     out[...] = product(full[...], right[...])
 
 
-def gradient_kernel(turned_level, count, order_of, *refs):
+def corner(rows):
+    return [lax.broadcasted_iota(jnp.int32, (rows // 2, rows), d) for d in (0, 1)]
+
+
+def pack(square):
+    rows = square.shape[0]
+    half = rows // 2
+    row, column = corner(rows)
+    top, low = square[:half, :], pltpu.roll(square[half:, :], half, 1)
+    return jnp.where((column >= half) | (column > row), top, jnp.where(column < row, low, 0.0))
+
+
+def unpack(packed):
+    half, rows = packed.shape
+    row, column = corner(rows)
+    over = jnp.concatenate([packed, jnp.zeros_like(packed)], 0).T
+    top = jnp.where((column >= half) | (column > row), packed, jnp.where(column < row, -over[:half, :], 0.0))
+    moved, over_moved = pltpu.roll(packed, half, 1), pltpu.roll(over[:half, :], half, 1)
+    low = jnp.where(column - half < row, moved, jnp.where(column - half > row, -over_moved, 0.0))
+    return jnp.concatenate([top, jnp.where(column < half, -over[half:, :], low)], 0)
+
+
+def gradient_kernel(turned_level, count, order_of, packed, *refs):
     left, right, weight = refs[2 * count:2 * count + 3]
     blocks, (full, terms) = refs[2 * count + 3:-2], refs[-2:]
     place(full, refs[:count], refs[count:2 * count])
@@ -192,48 +215,50 @@
     cyclic = product(left[...], product(full[...], right[...]))
     terms[...] = scale * (cyclic - cyclic.T)
     rows = terms.shape[0] // len(blocks)
-    spread = terms.shape[1] // LANES
     here = lax.axis_index("ens")
     for step, block in enumerate(blocks):
-        part = terms[pl.ds(pl.multiple_of(order_of(here, step) * rows, 8), rows), :]
-        for j in range(spread):
-            block[pl.ds(j, rows, stride=spread), :] = part[:, j * LANES:(j + 1) * LANES]
-
-
-def sum_kernel(*refs):
-    terms, out = refs[:-1], refs[-1]
+        which = order_of(here, step)
+        at = pl.ds(pl.multiple_of(which * rows, 8), rows)
+        if packed:
+            for j in range(len(blocks) - 1):
+                column = jnp.where(j < which, j, j + 1)
+                block[j * rows:(j + 1) * rows, :] = terms[at, pl.ds(pl.multiple_of(column * rows, LANES), rows)]
+            block[(len(blocks) - 1) * rows:, :] = pack(terms[at, pl.ds(pl.multiple_of(which * rows, LANES), rows)])
+        else:
+            for j in range(terms.shape[1] // LANES):
+                block[j * rows:(j + 1) * rows, :] = terms[at, j * LANES:(j + 1) * LANES]
+
+
+def sum_kernel(rows, packed, *refs):
+    terms, (out, total) = refs[:-2], refs[-2:]
+    spread = out.shape[0] // rows
     here = lax.axis_index("ens")
-    total = terms[0][...]
+    added = terms[0][...]
     for term in terms[1:-1]:
-        total = total + term[...]
-    out[...] = total
-
-    @pl.when((here == 0) | (here == 3))
-    def _():
-        out[...] = total + terms[-1][...]
-
-
-def plain_sum_kernel(*refs):
-    total = refs[0][...]
-    for ref in refs[1:-1]:
-        total = total + ref[...]
-    refs[-1][...] = total
-
-
-def reduce_rows(blocks, shape):
+        added = added + term[...]
+    added = added + jnp.where((lax.axis_size("ens") != 4) | (here == 0) | (here == 3), terms[-1][...], 0.0)
+    if packed:
+        total[:(spread - 1) * rows, :] = added[:(spread - 1) * rows, :]
+        total[(spread - 1) * rows:, :] = unpack(added[(spread - 1) * rows:, :])
+    else:
+        total[...] = added
+    for j in range(spread):
+        at = jnp.where(j < here, j, jnp.where(j == here, spread - 1, j - 1)) if packed else j
+        out[pl.ds(j, rows, stride=spread), :] = total[pl.ds(pl.multiple_of(at * rows, 8), rows), :]
+
+
+def send_rows(blocks):
     members = len(blocks)
 
     def move(x, pairs):
         return lax.ppermute(x, "ens", pairs)
 
-    if members == 4:
-        over_two = move(blocks[2], [(0, 1), (1, 3), (3, 2), (2, 0)])
-        across = move(blocks[3], [(0, 3), (3, 0)])
-        beside = move(blocks[1], [(0, 1), (1, 0), (2, 3), (3, 2)])
-        joined = move(blocks[3] + over_two, [(1, 2), (2, 1)])
-        return call(sum_kernel, [shape], blocks[0], beside, across, joined, over_two)[0]
-    arrived = [move(blocks[s], [(i, (i + s) % members) for i in range(members)]) for s in range(1, members)]
-    return call(plain_sum_kernel, [shape], blocks[0], *arrived)[0]
+    if members != 4:
+        return [move(blocks[s], [(i, (i + s) % members) for i in range(members)]) for s in range(1, members)]
+    _, beside, over_two, across = blocks
+    over = move(over_two, [(0, 1), (1, 3), (3, 2), (2, 0)])
+    arrived = [move(across, [(0, 3), (3, 0)]), move(beside, [(0, 1), (1, 0), (2, 3), (3, 2)])]
+    return [*arrived, move(across + over, [(1, 2), (2, 1)]), over]
 
 
 def shards(levels, members, propagators, weights, target):
@@ -248,7 +273,14 @@
 
     slice_here = propagators[0, 0]
     other = swap(slice_here, 0)
-    mine = call(early_kernel, [square], slice_here, target)[0]
+    mine, target = pl.pallas_call(
+        early_kernel,
+        out_shape=[jax.ShapeDtypeStruct(square, f32)] * 2,
+        in_specs=[pl.BlockSpec(memory_space=pltpu.HBM)] * 2,
+        out_specs=[pl.BlockSpec(memory_space=pltpu.VMEM)] * 2,
+        scratch_shapes=[pltpu.SemaphoreType.DMA((2,))],
+        compiler_params=pltpu.CompilerParams(vmem_limit_bytes=48 << 20),
+    )(slice_here, target)
     sends = call(send_kernel, pieces, mine, other, target, scratch=[(order, order // 2)])
     own, left, right = call(own_kernel, [square] * 3, mine, other, target, scratch=[square] * 2)
     top = levels - 1
@@ -265,12 +297,17 @@
     right = call(functools.partial(factor_kernel, count), [square], *got, *got_other, right, scratch=[square])[0]
     far_other = [swap(f, 0) for f in far]
     rows, spread = order // members, order // LANES
-    block = (rows * spread, LANES)
+    packed = rows == LANES
+    block = (rows * spread - packed * rows // 2, LANES)
     order_of = (lambda here, step: here ^ step) if members == 4 else (lambda here, step: lax.rem(here + step, members))
     blocks = call(
-        functools.partial(gradient_kernel, top - 1, count, order_of), [block] * members,
-        *far, *far_other, left, right, weights.reshape(1, 1), scratch=[square] * 2)
-    return reduce_rows(blocks, block).reshape(rows, 1, order)
+        functools.partial(gradient_kernel, top - 1, count, order_of, packed),
+        [block] * members, *far, *far_other, left, right, weights.reshape(1, 1), scratch=[square] * 2)
+    arrived = send_rows(blocks)
+    total = call(
+        functools.partial(sum_kernel, rows, packed), [(rows * spread, LANES)], blocks[0], *arrived,
+        scratch=[(rows * spread, LANES)])[0]
+    return total.reshape(rows, 1, order)
 
 
 def solution(mesh):

time: 56 us -> 53.2 us (0.950)
  the two profiles are of different devices: /device:TPU:0 before, /device:TPU:8 now
where the time goes in v3:
time: 53.2 us; the launch traced here: 53 us
  waiting for transfers between devices  22.3 us (42%)
  starting transfers between devices  16.7 us (31%)
  Pallas kernels  10.4 us (20%)
  local copies, waits for them, and re-layouts  2.75 us (5%)
  between operations  0.81 us (2%)
    ppermute x4, waiting for transfers between devices, move(): return lax.ppermute(x, 'ens', pairs)  13 us
    ppermute x17, waiting for transfers between devices, swap(): return lax.ppermute(x, 'tm', [(i, i ^ 1 << level) for i in range(slices)])  9.24 us
    pallas_call x9, Pallas kernels, call(): pl.pallas_call(kernel, out_shape=[jax.ShapeDtypeStruct(s, f32) for s in o...  9.19 us
    ppermute x4, starting transfers between devices, move(): return lax.ppermute(x, 'ens', pairs)  8.43 us
    ppermute x17, starting transfers between devices, swap(): return lax.ppermute(x, 'tm', [(i, i ^ 1 << level) for i in range(slices)])  8.29 us
    unnamed x6, local copies, waits for them, and re-layouts  2.75 us
    pallas_call x1, Pallas kernels, shards(): pl.pallas_call(early_kernel, out_shape=[jax.ShapeDtypeStruct(square, f32)...  1.19 us
  transfers between devices with their start and end apart: 21, of which 9 were waited for; matrix products, arithmetic and copies ran while one was open for 0% of the time, Pallas kernels for 12%

profile of v3, /device:TPU:8, one launch (start us, length us, event | category | flops | bytes accessed | tf_op | source)
XLA Modules:
  0.0 53.0 jit_solution(9507325594841347834)
XLA Ops:
  0.0 0.0 collective-permute-start
  0.0 0.0 copy-start.1
  0.0 1.2 %copy-done.1 = f32[512,512]{1,0:T(8,128)S(1)} copy-done((f32[512,512]{1,0:T(8,128)S(1)}, f32[512,512]{1,0:T(8,128)}, u32[]{:S(2)}) %copy-start.1) | copy-done | bytes 1048600
  1.2 0.0 copy-start.2
  1.2 1.2 %copy-done.2 = f32[1,1,512,512]{3,2,1,0:T(8,128)S(1)} copy-done((f32[1,1,512,512]{3,2,1,0:T(8,128)S(1)}, f32[1,1,512,512]{3,2,1,0:T(8,128)}, u32[]{:S(2)}) %copy-start.2) | copy-done | bytes 1048600
  2.5 1.2 %shard_map.37 = (f32[512,512]{1,0:T(8,128)S(1)}, f32[512,512]{1,0:T(8,128)S(1)}) custom-call(f32[512,512]{1,0:T(8,128)S(1)} %bitcast.5, f32[512,512]{1,0:T(8,128)S(1)} %copy-done.1), custom_call_target="tpu_custom_call" | custom-call | tf_op jit(solution)/shard_map/pallas_call | solution.py:276
  3.6 0.0 copy-start
  3.7 0.0 collective-permute-done.other
  3.7 0.7 %shard_map.38 = (f32[64,512]{1,0:T(8,128)S(1)}, f32[64,512]{1,0:T(8,128)S(1)}, f32[64,512]{1,0:T(8,128)S(1)}, f32[64,512]{1,0:T(8,128)S(1)}) custom-call(f32[512,512]{1,0:T(8,128)S(1)} %get-tuple-element.18.mine, f32[512,512]{1,0:T(8,128)S(1)} %collective-permute-done.other, f32[512,512]{1,0:T(8,128)S(1)} %get-tuple-element.19.target), custom_call_target="tpu_custom_call" | custom-call | tf_op jit(solution)/shard_map/pallas_call | solution.py:32
  4.4 0.3 copy-done
  4.7 0.5 collective-permute-start.1
  5.1 1.6 %collective-permute-start.3 = (f32[64,512]{1,0:T(8,128)S(1)}, f32[64,512]{1,0:T(8,128)S(1)}, u32[]{:S(2)}, u32[]{:S(2)}) collective-permute-start(f32[64,512]{1,0:T(8,128)S(1)} %get-tuple-element.22), channel_id=1, source_target_pairs={{0,8},{4,12},{8,0},{12,4},{16,24},{20,28},{24,16},{28,20},{1,9},{5... | collective-permute-start | bytes 393224 | tf_op jit(solution)/shard_map/ppermute | solution.py:272
  6.7 0.5 collective-permute-start.5
  7.2 1.6 %collective-permute-start.7 = (f32[64,512]{1,0:T(8,128)S(1)}, f32[64,512]{1,0:T(8,128)S(1)}, u32[]{:S(2)}, u32[]{:S(2)}) collective-permute-start(f32[64,512]{1,0:T(8,128)S(1)} %get-tuple-element.24), channel_id=1, source_target_pairs={{0,8},{4,12},{8,0},{12,4},{16,24},{20,28},{24,16},{28,20},{1,9},{5... | collective-permute-start | bytes 393224 | tf_op jit(solution)/shard_map/ppermute | solution.py:272
  8.7 2.6 %shard_map.39 = (f32[512,512]{1,0:T(8,128)S(1)}, f32[512,512]{1,0:T(8,128)S(1)}, f32[512,512]{1,0:T(8,128)S(1)}) custom-call(f32[512,512]{1,0:T(8,128)S(1)} %get-tuple-element.18.mine, f32[512,512]{1,0:T(8,128)S(1)} %collective-permute-done.other, f32[512,512]{1,0:T(8,128)} %copy-done), custom_call_target="tpu_custom_call" | custom-call | tf_op jit(solution)/shard_map/pallas_call | solution.py:32
  11.3 0.0 collective-permute-done.1.got.refs_0_
  11.3 0.4 shard_map.40
  11.7 0.6 %collective-permute-start.2 = (f32[64,512]{1,0:T(8,128)S(1)}, f32[64,512]{1,0:T(8,128)S(1)}, u32[]{:S(2)}, u32[]{:S(2)}) collective-permute-start(f32[64,512]{1,0:T(8,128)S(1)} %shard_map.40), channel_id=1, source_target_pairs={{0,16},{4,20},{8,24},{12,28},{16,0},{20,4},{24,8},{28,12},{1,17},{... | collective-permute-start | bytes 393224 | tf_op jit(solution)/shard_map/ppermute | solution.py:272
  12.3 1.6 %collective-permute-done.3.got.refs_1_ = f32[64,512]{1,0:T(8,128)S(1)} collective-permute-done((f32[64,512]{1,0:T(8,128)S(1)}, f32[64,512]{1,0:T(8,128)S(1)}, u32[]{:S(2)}, u32[]{:S(2)}) %collective-permute-start.3) | collective-permute-done | bytes 131104 | tf_op jit(solution)/shard_map/ppermute | solution.py:272
  13.8 0.4 shard_map.41
  14.3 0.5 collective-permute-start.4
  14.8 1.9 %collective-permute-done.5.got.refs_2_ = f32[64,512]{1,0:T(8,128)S(1)} collective-permute-done((f32[64,512]{1,0:T(8,128)S(1)}, f32[64,512]{1,0:T(8,128)S(1)}, u32[]{:S(2)}, u32[]{:S(2)}) %collective-permute-start.5) | collective-permute-done | bytes 131104 | tf_op jit(solution)/shard_map/ppermute | solution.py:272
  16.7 0.4 shard_map.42
  17.1 0.5 collective-permute-start.6
  17.6 0.8 %collective-permute-done.7.got.refs_3_ = f32[64,512]{1,0:T(8,128)S(1)} collective-permute-done((f32[64,512]{1,0:T(8,128)S(1)}, f32[64,512]{1,0:T(8,128)S(1)}, u32[]{:S(2)}, u32[]{:S(2)}) %collective-permute-start.7) | collective-permute-done | bytes 131104 | tf_op jit(solution)/shard_map/ppermute | solution.py:272
  18.4 0.4 shard_map.43
  18.8 1.2 %collective-permute-start.8 = (f32[64,512]{1,0:T(8,128)S(1)}, f32[64,512]{1,0:T(8,128)S(1)}, u32[]{:S(2)}, u32[]{:S(2)}) collective-permute-start(f32[64,512]{1,0:T(8,128)S(1)} %shard_map.43), channel_id=1, source_target_pairs={{0,16},{4,20},{8,24},{12,28},{16,0},{20,4},{24,8},{28,12},{1,17},{... | collective-permute-start | bytes 393224 | tf_op jit(solution)/shard_map/ppermute | solution.py:272
  20.0 0.0 collective-permute-start.13
  20.0 0.0 collective-permute-done.2.refs_0_
  20.0 0.5 collective-permute-start.14
  20.5 0.5 collective-permute-done.4.refs_1_
  21.0 0.0 collective-permute-start.15
  21.0 2.8 %collective-permute-done.6.refs_2_ = f32[64,512]{1,0:T(8,128)S(1)} collective-permute-done((f32[64,512]{1,0:T(8,128)S(1)}, f32[64,512]{1,0:T(8,128)S(1)}, u32[]{:S(2)}, u32[]{:S(2)}) %collective-permute-start.6) | collective-permute-done | bytes 131104 | tf_op jit(solution)/shard_map/ppermute | solution.py:272
  23.8 0.0 collective-permute-start.16
  23.8 1.6 %collective-permute-done.8.refs_3_ = f32[64,512]{1,0:T(8,128)S(1)} collective-permute-done((f32[64,512]{1,0:T(8,128)S(1)}, f32[64,512]{1,0:T(8,128)S(1)}, u32[]{:S(2)}, u32[]{:S(2)}) %collective-permute-start.8) | collective-permute-done | bytes 131104 | tf_op jit(solution)/shard_map/ppermute | solution.py:272
  25.4 0.0 collective-permute-start.9
  25.4 0.0 collective-permute-done.13.refs_4_
  25.4 0.5 collective-permute-start.10
  26.0 0.0 collective-permute-done.14.refs_5_
  26.0 0.1 collective-permute-start.11
  26.0 0.0 collective-permute-done.15.refs_6_
  26.0 0.4 collective-permute-start.12
  27.1 0.0 collective-permute-done.16.refs_7_
  27.1 1.0 %shard_map.44.refs_9_ = f32[512,512]{1,0:T(8,128)S(1)} custom-call(f32[64,512]{1,0:T(8,128)S(1)} %collective-permute-done.1.got.refs_0_, f32[64,512]{1,0:T(8,128)S(1)} %collective-permute-done.3.got.refs_1_, f32[64,512]{1,0:T(8,128)S(1)} %collective-permute-done.5.got.refs_2_, f32[64,512]{1,0:T(8,128)S(1)} %collective-permute-done.7.got.refs_3_, ...), custom_call_target="tpu_custom_call" | custom-call | tf_op jit(solution)/shard_map/pallas_call | solution.py:32
  28.2 0.0 collective-permute-done.9.refs_4_
  28.2 0.0 collective-permute-done.10.refs_5_
  28.2 0.0 collective-permute-done.11.refs_6_
  28.2 0.0 collective-permute-done.12.refs_7_
  28.2 2.3 %shard_map.45 = (f32[448,128]{1,0:T(8,128)S(1)}, f32[448,128]{1,0:T(8,128)S(1)}, f32[448,128]{1,0:T(8,128)S(1)}, f32[448,128]{1,0:T(8,128)S(1)}) custom-call(f32[64,512]{1,0:T(8,128)S(1)} %collective-permute-done.2.refs_0_, f32[64,512]{1,0:T(8,128)S(1)} %collective-permute-done.4.refs_1_, f32[64,512]{1,0:T(8,128)S(1)} %collective-permute-done.6.refs_2_, ...), custom_call_target="tpu_custom_call" | custom-call | tf_op jit(solution)/shard_map/pallas_call | solution.py:32
  30.6 2.6 %collective-permute-start.19 = (f32[448,128]{1,0:T(8,128)S(1)}, f32[448,128]{1,0:T(8,128)S(1)}, u32[]{:S(2)}, u32[]{:S(2)}) collective-permute-start(f32[448,128]{1,0:T(8,128)S(1)} %get-tuple-element.30), channel_id=1, source_target_pairs={{0,1},{1,3},{3,2},{2,0},{4,5},{5,7},{7,6},{6,4},{8,9},{9,11},{11,1... | collective-permute-start | bytes 688136 | tf_op jit(solution)/shard_map/ppermute | solution.py:254
  33.2 0.7 %collective-permute-start.17 = (f32[448,128]{1,0:T(8,128)S(1)}, f32[448,128]{1,0:T(8,128)S(1)}, u32[]{:S(2)}, u32[]{:S(2)}) collective-permute-start(f32[448,128]{1,0:T(8,128)S(1)} %get-tuple-element.28), channel_id=1, source_target_pairs={{0,3},{3,0},{4,7},{7,4},{8,11},{11,8},{12,15},{15,12},{16,19},{19,... | collective-permute-start | bytes 688136 | tf_op jit(solution)/shard_map/ppermute | solution.py:254
  33.9 3.2 %collective-permute-start.18 = (f32[448,128]{1,0:T(8,128)S(1)}, f32[448,128]{1,0:T(8,128)S(1)}, u32[]{:S(2)}, u32[]{:S(2)}) collective-permute-start(f32[448,128]{1,0:T(8,128)S(1)} %get-tuple-element.29), channel_id=1, source_target_pairs={{0,1},{1,0},{2,3},{3,2},{4,5},{5,4},{6,7},{7,6},{8,9},{9,8},{10,11... | collective-permute-start | bytes 688136 | tf_op jit(solution)/shard_map/ppermute | solution.py:254
  37.1 7.1 %collective-permute-done.19.refs_4_ = f32[448,128]{1,0:T(8,128)S(1)} collective-permute-done((f32[448,128]{1,0:T(8,128)S(1)}, f32[448,128]{1,0:T(8,128)S(1)}, u32[]{:S(2)}, u32[]{:S(2)}) %collective-permute-start.19) | collective-permute-done | bytes 229408 | tf_op jit(solution)/shard_map/ppermute | solution.py:254
  44.2 1.9 %collective-permute-start.20 = (f32[448,128]{1,0:T(8,128)S(1)}, f32[448,128]{1,0:T(8,128)S(1)}, u32[]{:S(2)}, u32[]{:S(2)}) collective-permute-start(f32[448,128]{1,0:T(8,128)S(1)} %add.3), channel_id=1, source_target_pairs={{1,2},{2,1},{5,6},{6,5},{9,10},{10,9},{13,14},{14,13},{17,18},{18,... | collective-permute-start | bytes 688136 | tf_op jit(solution)/shard_map/ppermute | solution.py:254
  46.1 0.0 collective-permute-done.17.refs_1_
  46.1 1.9 %collective-permute-done.18.refs_2_ = f32[448,128]{1,0:T(8,128)S(1)} collective-permute-done((f32[448,128]{1,0:T(8,128)S(1)}, f32[448,128]{1,0:T(8,128)S(1)}, u32[]{:S(2)}, u32[]{:S(2)}) %collective-permute-start.18) | collective-permute-done | bytes 229408 | tf_op jit(solution)/shard_map/ppermute | solution.py:254
  48.0 4.1 %collective-permute-done.20.refs_3_ = f32[448,128]{1,0:T(8,128)S(1)} collective-permute-done((f32[448,128]{1,0:T(8,128)S(1)}, f32[448,128]{1,0:T(8,128)S(1)}, u32[]{:S(2)}, u32[]{:S(2)}) %collective-permute-start.20) | collective-permute-done | bytes 229408 | tf_op jit(solution)/shard_map/ppermute | solution.py:254
  52.1 0.9 %shard_map.46 = f32[512,128]{1,0:T(8,128)} custom-call(f32[448,128]{1,0:T(8,128)S(1)} %get-tuple-element.27.refs_0_, f32[448,128]{1,0:T(8,128)S(1)} %collective-permute-done.17.refs_1_, f32[448,128]{1,0:T(8,128)S(1)} %collective-permute-done.18.refs_2_, f32[448,128]{1,0:T(8,128)S(1)} %collective-permute-done.20.refs_3_, ...), custom_call_target="tpu_custom_call" | custom-call | tf_op jit(solution)/shard_map/pallas_call | solution.py:32
  (1 shorter events, 0.0 us)
Async XLA Ops:
  0.0 3.7 %collective-permute-start = (f32[512,512]{1,0:T(8,128)}, f32[512,512]{1,0:T(8,128)S(1)}, u32[]{:S(2)}, u32[]{:S(2)}) collective-permute-start(f32[512,512]{1,0:T(8,128)} %bitcast.4), channel_id=1, source_target_pairs={{0,4},{4,0},{8,12},{12,8},{16,20},{20,16},{24,28},{28,24},{1,5},{5... | collective-permute-start | bytes 3145736 | tf_op jit(solution)/shard_map/ppermute | solution.py:272
  0.0 1.2 %copy-start.1 = (f32[512,512]{1,0:T(8,128)S(1)}, f32[512,512]{1,0:T(8,128)}, u32[]{:S(2)}) copy-start(f32[512,512]{1,0:T(8,128)} %target.1) | copy-start | bytes 3145732
  1.2 1.2 %copy-start.2 = (f32[1,1,512,512]{3,2,1,0:T(8,128)S(1)}, f32[1,1,512,512]{3,2,1,0:T(8,128)}, u32[]{:S(2)}) copy-start(f32[1,1,512,512]{3,2,1,0:T(8,128)} %param.3) | copy-start | bytes 3145732
  3.6 1.0 %copy-start = (f32[512,512]{1,0:T(8,128)}, f32[512,512]{1,0:T(8,128)S(1)}, u32[]{:S(2)}) copy-start(f32[512,512]{1,0:T(8,128)S(1)} %get-tuple-element.19.target) | copy-start | bytes 3145732
  4.7 6.6 %collective-permute-start.1 = (f32[64,512]{1,0:T(8,128)S(1)}, f32[64,512]{1,0:T(8,128)S(1)}, u32[]{:S(2)}, u32[]{:S(2)}) collective-permute-start(f32[64,512]{1,0:T(8,128)S(1)} %get-tuple-element.20), channel_id=1, source_target_pairs={{0,8},{4,12},{8,0},{12,4},{16,24},{20,28},{24,16},{28,20},{1,9},{5... | collective-permute-start | bytes 393224 | tf_op jit(solution)/shard_map/ppermute | solution.py:272
  5.1 8.7 %collective-permute-start.3 = (f32[64,512]{1,0:T(8,128)S(1)}, f32[64,512]{1,0:T(8,128)S(1)}, u32[]{:S(2)}, u32[]{:S(2)}) collective-permute-start(f32[64,512]{1,0:T(8,128)S(1)} %get-tuple-element.22), channel_id=1, source_target_pairs={{0,8},{4,12},{8,0},{12,4},{16,24},{20,28},{24,16},{28,20},{1,9},{5... | collective-permute-start | bytes 393224 | tf_op jit(solution)/shard_map/ppermute | solution.py:272
  6.7 10.0 %collective-permute-start.5 = (f32[64,512]{1,0:T(8,128)S(1)}, f32[64,512]{1,0:T(8,128)S(1)}, u32[]{:S(2)}, u32[]{:S(2)}) collective-permute-start(f32[64,512]{1,0:T(8,128)S(1)} %get-tuple-element.23), channel_id=1, source_target_pairs={{0,8},{4,12},{8,0},{12,4},{16,24},{20,28},{24,16},{28,20},{1,9},{5... | collective-permute-start | bytes 393224 | tf_op jit(solution)/shard_map/ppermute | solution.py:272
  7.2 11.2 %collective-permute-start.7 = (f32[64,512]{1,0:T(8,128)S(1)}, f32[64,512]{1,0:T(8,128)S(1)}, u32[]{:S(2)}, u32[]{:S(2)}) collective-permute-start(f32[64,512]{1,0:T(8,128)S(1)} %get-tuple-element.24), channel_id=1, source_target_pairs={{0,8},{4,12},{8,0},{12,4},{16,24},{20,28},{24,16},{28,20},{1,9},{5... | collective-permute-start | bytes 393224 | tf_op jit(solution)/shard_map/ppermute | solution.py:272
  11.7 8.3 %collective-permute-start.2 = (f32[64,512]{1,0:T(8,128)S(1)}, f32[64,512]{1,0:T(8,128)S(1)}, u32[]{:S(2)}, u32[]{:S(2)}) collective-permute-start(f32[64,512]{1,0:T(8,128)S(1)} %shard_map.40), channel_id=1, source_target_pairs={{0,16},{4,20},{8,24},{12,28},{16,0},{20,4},{24,8},{28,12},{1,17},{... | collective-permute-start | bytes 393224 | tf_op jit(solution)/shard_map/ppermute | solution.py:272
  14.3 6.7 %collective-permute-start.4 = (f32[64,512]{1,0:T(8,128)S(1)}, f32[64,512]{1,0:T(8,128)S(1)}, u32[]{:S(2)}, u32[]{:S(2)}) collective-permute-start(f32[64,512]{1,0:T(8,128)S(1)} %shard_map.41), channel_id=1, source_target_pairs={{0,16},{4,20},{8,24},{12,28},{16,0},{20,4},{24,8},{28,12},{1,17},{... | collective-permute-start | bytes 393224 | tf_op jit(solution)/shard_map/ppermute | solution.py:272
  17.1 6.7 %collective-permute-start.6 = (f32[64,512]{1,0:T(8,128)S(1)}, f32[64,512]{1,0:T(8,128)S(1)}, u32[]{:S(2)}, u32[]{:S(2)}) collective-permute-start(f32[64,512]{1,0:T(8,128)S(1)} %shard_map.42), channel_id=1, source_target_pairs={{0,16},{4,20},{8,24},{12,28},{16,0},{20,4},{24,8},{28,12},{1,17},{... | collective-permute-start | bytes 393224 | tf_op jit(solution)/shard_map/ppermute | solution.py:272
  18.8 6.6 %collective-permute-start.8 = (f32[64,512]{1,0:T(8,128)S(1)}, f32[64,512]{1,0:T(8,128)S(1)}, u32[]{:S(2)}, u32[]{:S(2)}) collective-permute-start(f32[64,512]{1,0:T(8,128)S(1)} %shard_map.43), channel_id=1, source_target_pairs={{0,16},{4,20},{8,24},{12,28},{16,0},{20,4},{24,8},{28,12},{1,17},{... | collective-permute-start | bytes 393224 | tf_op jit(solution)/shard_map/ppermute | solution.py:272
  20.0 5.5 %collective-permute-start.13 = (f32[64,512]{1,0:T(8,128)S(1)}, f32[64,512]{1,0:T(8,128)S(1)}, u32[]{:S(2)}, u32[]{:S(2)}) collective-permute-start(f32[64,512]{1,0:T(8,128)S(1)} %collective-permute-done.1.got.refs_0_), channel_id=1, source_target_pairs={{0,4},{4,0},{8,12},{12,8},{16,20},{20,16},{24,28},{28,24},{1,5},{5... | collective-permute-start | bytes 393224 | tf_op jit(solution)/shard_map/ppermute | solution.py:272
  20.0 6.0 %collective-permute-start.14 = (f32[64,512]{1,0:T(8,128)S(1)}, f32[64,512]{1,0:T(8,128)S(1)}, u32[]{:S(2)}, u32[]{:S(2)}) collective-permute-start(f32[64,512]{1,0:T(8,128)S(1)} %collective-permute-done.3.got.refs_1_), channel_id=1, source_target_pairs={{0,4},{4,0},{8,12},{12,8},{16,20},{20,16},{24,28},{28,24},{1,5},{5... | collective-permute-start | bytes 393224 | tf_op jit(solution)/shard_map/ppermute | solution.py:272
  21.0 5.1 %collective-permute-start.15 = (f32[64,512]{1,0:T(8,128)S(1)}, f32[64,512]{1,0:T(8,128)S(1)}, u32[]{:S(2)}, u32[]{:S(2)}) collective-permute-start(f32[64,512]{1,0:T(8,128)S(1)} %collective-permute-done.5.got.refs_2_), channel_id=1, source_target_pairs={{0,4},{4,0},{8,12},{12,8},{16,20},{20,16},{24,28},{28,24},{1,5},{5... | collective-permute-start | bytes 393224 | tf_op jit(solution)/shard_map/ppermute | solution.py:272
  23.8 3.3 %collective-permute-start.16 = (f32[64,512]{1,0:T(8,128)S(1)}, f32[64,512]{1,0:T(8,128)S(1)}, u32[]{:S(2)}, u32[]{:S(2)}) collective-permute-start(f32[64,512]{1,0:T(8,128)S(1)} %collective-permute-done.7.got.refs_3_), channel_id=1, source_target_pairs={{0,4},{4,0},{8,12},{12,8},{16,20},{20,16},{24,28},{28,24},{1,5},{5... | collective-permute-start | bytes 393224 | tf_op jit(solution)/shard_map/ppermute | solution.py:272
  25.4 2.7 %collective-permute-start.9 = (f32[64,512]{1,0:T(8,128)S(1)}, f32[64,512]{1,0:T(8,128)S(1)}, u32[]{:S(2)}, u32[]{:S(2)}) collective-permute-start(f32[64,512]{1,0:T(8,128)S(1)} %collective-permute-done.2.refs_0_), channel_id=1, source_target_pairs={{0,4},{4,0},{8,12},{12,8},{16,20},{20,16},{24,28},{28,24},{1,5},{5... | collective-permute-start | bytes 393224 | tf_op jit(solution)/shard_map/ppermute | solution.py:272
  25.4 2.8 %collective-permute-start.10 = (f32[64,512]{1,0:T(8,128)S(1)}, f32[64,512]{1,0:T(8,128)S(1)}, u32[]{:S(2)}, u32[]{:S(2)}) collective-permute-start(f32[64,512]{1,0:T(8,128)S(1)} %collective-permute-done.4.refs_1_), channel_id=1, source_target_pairs={{0,4},{4,0},{8,12},{12,8},{16,20},{20,16},{24,28},{28,24},{1,5},{5... | collective-permute-start | bytes 393224 | tf_op jit(solution)/shard_map/ppermute | solution.py:272
  26.0 2.3 %collective-permute-start.11 = (f32[64,512]{1,0:T(8,128)S(1)}, f32[64,512]{1,0:T(8,128)S(1)}, u32[]{:S(2)}, u32[]{:S(2)}) collective-permute-start(f32[64,512]{1,0:T(8,128)S(1)} %collective-permute-done.6.refs_2_), channel_id=1, source_target_pairs={{0,4},{4,0},{8,12},{12,8},{16,20},{20,16},{24,28},{28,24},{1,5},{5... | collective-permute-start | bytes 393224 | tf_op jit(solution)/shard_map/ppermute | solution.py:272
  26.0 2.2 %collective-permute-start.12 = (f32[64,512]{1,0:T(8,128)S(1)}, f32[64,512]{1,0:T(8,128)S(1)}, u32[]{:S(2)}, u32[]{:S(2)}) collective-permute-start(f32[64,512]{1,0:T(8,128)S(1)} %collective-permute-done.8.refs_3_), channel_id=1, source_target_pairs={{0,4},{4,0},{8,12},{12,8},{16,20},{20,16},{24,28},{28,24},{1,5},{5... | collective-permute-start | bytes 393224 | tf_op jit(solution)/shard_map/ppermute | solution.py:272
  30.6 13.6 %collective-permute-start.19 = (f32[448,128]{1,0:T(8,128)S(1)}, f32[448,128]{1,0:T(8,128)S(1)}, u32[]{:S(2)}, u32[]{:S(2)}) collective-permute-start(f32[448,128]{1,0:T(8,128)S(1)} %get-tuple-element.30), channel_id=1, source_target_pairs={{0,1},{1,3},{3,2},{2,0},{4,5},{5,7},{7,6},{6,4},{8,9},{9,11},{11,1... | collective-permute-start | bytes 688136 | tf_op jit(solution)/shard_map/ppermute | solution.py:254
  33.2 12.9 %collective-permute-start.17 = (f32[448,128]{1,0:T(8,128)S(1)}, f32[448,128]{1,0:T(8,128)S(1)}, u32[]{:S(2)}, u32[]{:S(2)}) collective-permute-start(f32[448,128]{1,0:T(8,128)S(1)} %get-tuple-element.28), channel_id=1, source_target_pairs={{0,3},{3,0},{4,7},{7,4},{8,11},{11,8},{12,15},{15,12},{16,19},{19,... | collective-permute-start | bytes 688136 | tf_op jit(solution)/shard_map/ppermute | solution.py:254
  33.9 14.1 %collective-permute-start.18 = (f32[448,128]{1,0:T(8,128)S(1)}, f32[448,128]{1,0:T(8,128)S(1)}, u32[]{:S(2)}, u32[]{:S(2)}) collective-permute-start(f32[448,128]{1,0:T(8,128)S(1)} %get-tuple-element.29), channel_id=1, source_target_pairs={{0,1},{1,0},{2,3},{3,2},{4,5},{5,4},{6,7},{7,6},{8,9},{9,8},{10,11... | collective-permute-start | bytes 688136 | tf_op jit(solution)/shard_map/ppermute | solution.py:254
  44.2 7.9 %collective-permute-start.20 = (f32[448,128]{1,0:T(8,128)S(1)}, f32[448,128]{1,0:T(8,128)S(1)}, u32[]{:S(2)}, u32[]{:S(2)}) collective-permute-start(f32[448,128]{1,0:T(8,128)S(1)} %add.3), channel_id=1, source_target_pairs={{1,2},{2,1},{5,6},{6,5},{9,10},{10,9},{13,14},{14,13},{17,18},{18,... | collective-permute-start | bytes 688136 | tf_op jit(solution)/shard_map/ppermute | solution.py:254

commit v4 on v3

--- a/solution.py
+++ b/solution.py
@@ -35,7 +35,7 @@
         in_specs=[pl.BlockSpec(memory_space=pltpu.VMEM)] * len(operands),
         out_specs=[pl.BlockSpec(memory_space=pltpu.VMEM)] * len(outs),
         scratch_shapes=[pltpu.VMEM(s, f32) for s in scratch],
-        compiler_params=pltpu.CompilerParams(vmem_limit_bytes=48 << 20),
+        compiler_params=pltpu.CompilerParams(vmem_limit_bytes=16 << 20),
     )(*operands)
 
 
@@ -57,21 +57,11 @@
         at += piece.shape[0]
 
 
-def early_kernel(slice_here, target, mine, target_here, arrivals):
-    copies = [
-        pltpu.make_async_copy(slice_here, mine, arrivals.at[0]), pltpu.make_async_copy(target, target_here, arrivals.at[1])]
-    for copy in copies:
-        copy.start()
-    for copy in copies:
-        copy.wait()
-
-    @pl.when(lax.axis_index("tm") == 0)
-    def _():
-        mine[...] = product(mine[...], target_here[...], b_turned=True)
-
-
-def send_kernel(mine, other, target, *rest):
-    sends, columns = rest[:-1], rest[-1]
+def early_kernel(slice_here, mine):
+    mine[...] = slice_here[...]
+
+
+def send_kernel(mine, other, *sends):
     core, turned = bit(0), bit(1)
     half = mine.shape[0] // 2
 
@@ -81,78 +71,74 @@
 
     @pl.when((turned == 0) & (core == 1))
     def _():
-        columns[...] = other[:, half:]
-
-        @pl.when(lax.axis_index("tm") == 1)
+        cut(product(mine[...], other[:, half:]).T, sends)
+
+    @pl.when((turned == 1) & (core == 0))
+    def _():
+        cut(product(other[:half, :], mine[...]), sends)
+
+    @pl.when((turned == 1) & (core == 1))
+    def _():
+        cut(product(mine[half:, :], other[...]), sends)
+
+
+def own_kernel(short, mine, other, target, own, left, right):
+    core, turned = bit(0), bit(1)
+    takes = (bit(2) == turned) if short else (core < 0)
+
+    def identity(out):
+        row, column = (lax.broadcasted_iota(jnp.int32, out.shape, d) for d in (0, 1))
+        out[...] = (row == column).astype(f32)
+
+    @pl.when((core == 0) & (turned == 0))
+    def _():
+        left[...] = mine[...]
+        right[...] = other[...]
+
+        @pl.when(takes)
         def _():
-            columns[...] = product(other[...], target[half:, :], b_turned=True)
-
-        cut(product(mine[...], columns[...]).T, sends)
-
-    @pl.when((turned == 1) & (core == 0))
-    def _():
-        cut(product(other[:half, :], mine[...]), sends)
-
-    @pl.when((turned == 1) & (core == 1))
-    def _():
-        cut(product(mine[half:, :], other[...]), sends)
-
-
-def own_kernel(mine, other, target, own, left, right, lo, hi):
-    core, turned = bit(0), bit(1)
-    order = mine.shape[0]
-
-    @pl.when(core == 0)
-    def _():
-        lo[...] = mine[...]
-        hi[...] = other[...]
-
-    @pl.when(core == 1)
-    def _():
-        lo[...] = other[...]
-        hi[...] = mine[...]
-
-        @pl.when(lax.axis_index("tm") == 1)
+            left[...] = product(left[...], target[...], b_turned=True)
+
+        own[...] = product(other[...], left[...])
+
+    @pl.when((core == 0) & (turned == 1))
+    def _():
+        left[...] = other[...].T
+        right[...] = mine[...].T
+
+        @pl.when(takes)
         def _():
-            lo[...] = product(other[...], target[...], b_turned=True)
-
-    both = product(hi[...], lo[...])
-    identity = (lax.broadcasted_iota(jnp.int32, (order, order), 0) == lax.broadcasted_iota(jnp.int32, (order, order), 1)).astype(f32)
-
-    @pl.when(turned == 0)
-    def _():
-        own[...] = both
-
-        @pl.when(core == 0)
+            left[...] = product(left[...], target[...])
+
+        own[...] = product(right[...], left[...])
+
+    @pl.when((core == 1) & (turned == 0))
+    def _():
+        own[...] = product(mine[...], other[...])
+        identity(right)
+
+        @pl.when(takes)
         def _():
-            left[...] = lo[...]
-            right[...] = hi[...]
-
-        @pl.when(core == 1)
+            own[...] = product(own[...], target[...], b_turned=True)
+
+        left[...] = own[...]
+
+    @pl.when((core == 1) & (turned == 1))
+    def _():
+        right[...] = product(mine[...], other[...]).T
+        own[...] = right[...]
+        identity(left)
+
+        @pl.when(takes)
         def _():
-            left[...] = both
-            right[...] = identity
-
-    @pl.when(turned == 1)
-    def _():
-        over = both.T
-        own[...] = over
-
-        @pl.when(core == 0)
-        def _():
-            left[...] = hi[...].T
-            right[...] = lo[...].T
-
-        @pl.when(core == 1)
-        def _():
-            left[...] = identity
-            right[...] = over
-
-
-def turn_kernel(level, count, *refs):
+            left[...] = target[...]
+            own[...] = product(right[...], target[...])
+
+
+def turn_kernel(top, level, count, *refs):
     mine, other, got, got_other = (refs[i * count:(i + 1) * count] for i in range(4))
-    left, right, own, left_out, right_out = refs[4 * count:4 * count + 5]
-    sends, full = refs[4 * count + 5:-1], refs[-1]
+    left, right, target, own, left_out, right_out = refs[4 * count:4 * count + 6]
+    sends, full = refs[4 * count + 6:-1], refs[-1]
     half = full.shape[0] // 2
     flip = bit(level) != bit(level + 1)
     place(full, got, got_other)
@@ -173,15 +159,30 @@
         right_out[...] = new_right
 
     cut(full[pl.ds(pl.multiple_of(bit(0) * half, 8), half), :], sends)
+    if level + 2 == top:
+        for out in own, left_out:
+            @pl.when((bit(top) == bit(level + 1)) & (bit(top) == 0))
+            def _(out=out):
+                out[...] = product(out[...], target[...], b_turned=True)
+
+            @pl.when((bit(top) == bit(level + 1)) & (bit(top) == 1))
+            def _(out=out):
+                out[...] = product(out[...], target[...])
 
 
 def half_kernel(got, own, out):
     out[...] = product(got[...], own[...])
 
 
-def factor_kernel(count, *refs):
-    right, out, full = refs[2 * count:]
-    place(full, refs[:count], refs[count:2 * count])
+def join_kernel(*refs):
+    at = 0
+    for piece in refs[:-1]:
+        refs[-1][at:at + piece.shape[0], :] = piece[...]
+        at += piece.shape[0]
+
+
+def factor_kernel(near, near_other, right, out, full):
+    place(full, [near], [near_other])
     out[...] = product(full[...], right[...])
 
 
@@ -207,10 +208,9 @@
     return jnp.concatenate([top, jnp.where(column < half, -over[half:, :], low)], 0)
 
 
-def gradient_kernel(turned_level, count, order_of, packed, *refs):
-    left, right, weight = refs[2 * count:2 * count + 3]
-    blocks, (full, terms) = refs[2 * count + 3:-2], refs[-2:]
-    place(full, refs[:count], refs[count:2 * count])
+def gradient_kernel(turned_level, order_of, packed, far, far_other, left, right, weight, *refs):
+    blocks, (full, terms) = refs[:-2], refs[-2:]
+    place(full, [far], [far_other])
     scale = weight[...] * (0.5 - bit(turned_level).astype(f32))
     cyclic = product(left[...], product(full[...], right[...]))
     terms[...] = scale * (cyclic - cyclic.T)
@@ -273,36 +273,29 @@
 
     slice_here = propagators[0, 0]
     other = swap(slice_here, 0)
-    mine, target = pl.pallas_call(
-        early_kernel,
-        out_shape=[jax.ShapeDtypeStruct(square, f32)] * 2,
-        in_specs=[pl.BlockSpec(memory_space=pltpu.HBM)] * 2,
-        out_specs=[pl.BlockSpec(memory_space=pltpu.VMEM)] * 2,
-        scratch_shapes=[pltpu.SemaphoreType.DMA((2,))],
-        compiler_params=pltpu.CompilerParams(vmem_limit_bytes=48 << 20),
-    )(slice_here, target)
-    sends = call(send_kernel, pieces, mine, other, target, scratch=[(order, order // 2)])
-    own, left, right = call(own_kernel, [square] * 3, mine, other, target, scratch=[square] * 2)
+    mine = call(early_kernel, [square], slice_here)[0]
+    sends = call(send_kernel, pieces, mine, other)
+    own, left, right = call(functools.partial(own_kernel, levels == 3), [square] * 3, mine, other, target)
     top = levels - 1
     for level in range(1, top):
         got = [swap(s, level) for s in sends]
         products = [call(half_kernel, [g.shape], g, own)[0] for g in got]
-        got_other = [swap(g, 0) for g in got]
         if level + 1 < top:
             outs = call(
-                functools.partial(turn_kernel, level, count), [square] * 3 + pieces,
-                *products, *[swap(p, 0) for p in products], *got, *got_other, left, right, scratch=[square])
+                functools.partial(turn_kernel, top, level, count), [square] * 3 + pieces, *products,
+                *[swap(p, 0) for p in products], *got, *[swap(g, 0) for g in got], left, right, target, scratch=[square])
             (own, left, right), sends = outs[:3], outs[3:]
     far = [swap(p, top) for p in products]
-    right = call(functools.partial(factor_kernel, count), [square], *got, *got_other, right, scratch=[square])[0]
-    far_other = [swap(f, 0) for f in far]
+    near = call(join_kernel, [(order // 2, order)], *got)[0]
+    right = call(factor_kernel, [square], near, swap(near, 0), right, scratch=[square])[0]
+    far = call(join_kernel, [(order // 2, order)], *far)[0]
     rows, spread = order // members, order // LANES
     packed = rows == LANES
     block = (rows * spread - packed * rows // 2, LANES)
     order_of = (lambda here, step: here ^ step) if members == 4 else (lambda here, step: lax.rem(here + step, members))
     blocks = call(
-        functools.partial(gradient_kernel, top - 1, count, order_of, packed),
-        [block] * members, *far, *far_other, left, right, weights.reshape(1, 1), scratch=[square] * 2)
+        functools.partial(gradient_kernel, top - 1, order_of, packed),
+        [block] * members, far, swap(far, 0), left, right, weights.reshape(1, 1), scratch=[square] * 2)
     arrived = send_rows(blocks)
     total = call(
         functools.partial(sum_kernel, rows, packed), [(rows * spread, LANES)], blocks[0], *arrived,

time: 53.2 us -> 51 us (0.959)
  the two profiles are of different devices: /device:TPU:8 before, /device:TPU:14 now
where the time goes in v4:
time: 51 us; the launch traced here: 50.8 us
  waiting for transfers between devices  24.8 us (49%)
  starting transfers between devices  14.5 us (28%)
  Pallas kernels  9.45 us (19%)
  local copies, waits for them, and re-layouts  1.23 us (2%)
  between operations  0.79 us (2%)
    ppermute x4, waiting for transfers between devices, move(): return lax.ppermute(x, 'ens', pairs)  13 us
    ppermute x11, waiting for transfers between devices, swap(): return lax.ppermute(x, 'tm', [(i, i ^ 1 << level) for i in range(slices)])  11.8 us
    pallas_call x12, Pallas kernels, call(): pl.pallas_call(kernel, out_shape=[jax.ShapeDtypeStruct(s, f32) for s in o...  9.45 us
    ppermute x4, starting transfers between devices, move(): return lax.ppermute(x, 'ens', pairs)  8.43 us
    ppermute x11, starting transfers between devices, swap(): return lax.ppermute(x, 'tm', [(i, i ^ 1 << level) for i in range(slices)])  6.07 us
    unnamed x4, local copies, waits for them, and re-layouts  1.23 us
  transfers between devices with their start and end apart: 15, of which 11 were waited for; matrix products, arithmetic and copies ran while one was open for 0% of the time, Pallas kernels for 11%

profile of v4, /device:TPU:14, one launch (start us, length us, event | category | flops | bytes accessed | tf_op | source)
XLA Modules:
  0.0 50.8 jit_solution(14070204674777575699)
XLA Ops:
  0.0 0.0 collective-permute-start
  0.0 0.0 copy-start.1
  0.0 1.2 %copy-done.1 = f32[1,1,512,512]{3,2,1,0:T(8,128)S(1)} copy-done((f32[1,1,512,512]{3,2,1,0:T(8,128)S(1)}, f32[1,1,512,512]{3,2,1,0:T(8,128)}, u32[]{:S(2)}) %copy-start.1) | copy-done | bytes 1048600
  1.2 0.1 shard_map.37.mine
  1.3 0.0 copy-start
  1.3 1.6 %collective-permute-done.other = f32[512,512]{1,0:T(8,128)S(1)} collective-permute-done((f32[512,512]{1,0:T(8,128)}, f32[512,512]{1,0:T(8,128)S(1)}, u32[]{:S(2)}, u32[]{:S(2)}) %collective-permute-start) | collective-permute-done | bytes 1048608 | tf_op jit(solution)/shard_map/ppermute | solution.py:272
  2.9 0.6 %shard_map.38 = (f32[64,512]{1,0:T(8,128)S(1)}, f32[64,512]{1,0:T(8,128)S(1)}, f32[64,512]{1,0:T(8,128)S(1)}, f32[64,512]{1,0:T(8,128)S(1)}) custom-call(f32[512,512]{1,0:T(8,128)S(1)} %shard_map.37.mine, f32[512,512]{1,0:T(8,128)S(1)} %collective-permute-done.other), custom_call_target="tpu_custom_call" | custom-call | tf_op jit(solution)/shard_map/pallas_call | solution.py:32
  3.5 0.7 %collective-permute-start.1 = (f32[64,512]{1,0:T(8,128)S(1)}, f32[64,512]{1,0:T(8,128)S(1)}, u32[]{:S(2)}, u32[]{:S(2)}) collective-permute-start(f32[64,512]{1,0:T(8,128)S(1)} %get-tuple-element.16), channel_id=1, source_target_pairs={{0,8},{4,12},{8,0},{12,4},{16,24},{20,28},{24,16},{28,20},{1,9},{5... | collective-permute-start | bytes 393224 | tf_op jit(solution)/shard_map/ppermute | solution.py:272
  4.2 1.4 %collective-permute-start.3 = (f32[64,512]{1,0:T(8,128)S(1)}, f32[64,512]{1,0:T(8,128)S(1)}, u32[]{:S(2)}, u32[]{:S(2)}) collective-permute-start(f32[64,512]{1,0:T(8,128)S(1)} %get-tuple-element.18), channel_id=1, source_target_pairs={{0,8},{4,12},{8,0},{12,4},{16,24},{20,28},{24,16},{28,20},{1,9},{5... | collective-permute-start | bytes 393224 | tf_op jit(solution)/shard_map/ppermute | solution.py:272
  5.6 0.6 %collective-permute-start.5 = (f32[64,512]{1,0:T(8,128)S(1)}, f32[64,512]{1,0:T(8,128)S(1)}, u32[]{:S(2)}, u32[]{:S(2)}) collective-permute-start(f32[64,512]{1,0:T(8,128)S(1)} %get-tuple-element.19), channel_id=1, source_target_pairs={{0,8},{4,12},{8,0},{12,4},{16,24},{20,28},{24,16},{28,20},{1,9},{5... | collective-permute-start | bytes 393224 | tf_op jit(solution)/shard_map/ppermute | solution.py:272
  6.2 1.4 %collective-permute-start.7 = (f32[64,512]{1,0:T(8,128)S(1)}, f32[64,512]{1,0:T(8,128)S(1)}, u32[]{:S(2)}, u32[]{:S(2)}) collective-permute-start(f32[64,512]{1,0:T(8,128)S(1)} %get-tuple-element.20), channel_id=1, source_target_pairs={{0,8},{4,12},{8,0},{12,4},{16,24},{20,28},{24,16},{28,20},{1,9},{5... | collective-permute-start | bytes 393224 | tf_op jit(solution)/shard_map/ppermute | solution.py:272
  7.6 0.0 copy-done
  7.6 2.8 %shard_map.39 = (f32[512,512]{1,0:T(8,128)S(1)}, f32[512,512]{1,0:T(8,128)S(1)}, f32[512,512]{1,0:T(8,128)S(1)}) custom-call(f32[512,512]{1,0:T(8,128)S(1)} %shard_map.37.mine, f32[512,512]{1,0:T(8,128)S(1)} %collective-permute-done.other, f32[512,512]{1,0:T(8,128)S(1)} %copy-done), custom_call_target="tpu_custom_call" | custom-call | tf_op jit(solution)/shard_map/pallas_call | solution.py:32
  10.4 0.0 collective-permute-done.1.got.refs_0_
  10.4 0.4 shard_map.40
  10.8 0.1 collective-permute-start.2
  10.9 1.8 %collective-permute-done.3.got.refs_1_ = f32[64,512]{1,0:T(8,128)S(1)} collective-permute-done((f32[64,512]{1,0:T(8,128)S(1)}, f32[64,512]{1,0:T(8,128)S(1)}, u32[]{:S(2)}, u32[]{:S(2)}) %collective-permute-start.3) | collective-permute-done | bytes 131104 | tf_op jit(solution)/shard_map/ppermute | solution.py:272
  12.7 0.4 shard_map.41
  13.1 0.6 %collective-permute-start.4 = (f32[64,512]{1,0:T(8,128)S(1)}, f32[64,512]{1,0:T(8,128)S(1)}, u32[]{:S(2)}, u32[]{:S(2)}) collective-permute-start(f32[64,512]{1,0:T(8,128)S(1)} %shard_map.41), channel_id=1, source_target_pairs={{0,16},{4,20},{8,24},{12,28},{16,0},{20,4},{24,8},{28,12},{1,17},{... | collective-permute-start | bytes 393224 | tf_op jit(solution)/shard_map/ppermute | solution.py:272
  13.7 1.8 %collective-permute-done.5.got.refs_2_ = f32[64,512]{1,0:T(8,128)S(1)} collective-permute-done((f32[64,512]{1,0:T(8,128)S(1)}, f32[64,512]{1,0:T(8,128)S(1)}, u32[]{:S(2)}, u32[]{:S(2)}) %collective-permute-start.5) | collective-permute-done | bytes 131104 | tf_op jit(solution)/shard_map/ppermute | solution.py:272
  15.5 0.4 shard_map.42
  15.9 0.6 %collective-permute-start.6 = (f32[64,512]{1,0:T(8,128)S(1)}, f32[64,512]{1,0:T(8,128)S(1)}, u32[]{:S(2)}, u32[]{:S(2)}) collective-permute-start(f32[64,512]{1,0:T(8,128)S(1)} %shard_map.42), channel_id=1, source_target_pairs={{0,16},{4,20},{8,24},{12,28},{16,0},{20,4},{24,8},{28,12},{1,17},{... | collective-permute-start | bytes 393224 | tf_op jit(solution)/shard_map/ppermute | solution.py:272
  16.5 1.0 %collective-permute-done.7.got.refs_3_ = f32[64,512]{1,0:T(8,128)S(1)} collective-permute-done((f32[64,512]{1,0:T(8,128)S(1)}, f32[64,512]{1,0:T(8,128)S(1)}, u32[]{:S(2)}, u32[]{:S(2)}) %collective-permute-start.7) | collective-permute-done | bytes 131104 | tf_op jit(solution)/shard_map/ppermute | solution.py:272
  17.5 0.4 shard_map.43
  17.9 0.6 %collective-permute-start.8 = (f32[64,512]{1,0:T(8,128)S(1)}, f32[64,512]{1,0:T(8,128)S(1)}, u32[]{:S(2)}, u32[]{:S(2)}) collective-permute-start(f32[64,512]{1,0:T(8,128)S(1)} %shard_map.43), channel_id=1, source_target_pairs={{0,16},{4,20},{8,24},{12,28},{16,0},{20,4},{24,8},{28,12},{1,17},{... | collective-permute-start | bytes 393224 | tf_op jit(solution)/shard_map/ppermute | solution.py:272
  18.6 0.1 collective-permute-start.10
  18.6 0.0 collective-permute-done.2.refs_0_
  18.6 1.2 %collective-permute-done.4.refs_1_ = f32[64,512]{1,0:T(8,128)S(1)} collective-permute-done((f32[64,512]{1,0:T(8,128)S(1)}, f32[64,512]{1,0:T(8,128)S(1)}, u32[]{:S(2)}, u32[]{:S(2)}) %collective-permute-start.4) | collective-permute-done | bytes 131104 | tf_op jit(solution)/shard_map/ppermute | solution.py:272
  19.8 2.8 %collective-permute-done.6.refs_2_ = f32[64,512]{1,0:T(8,128)S(1)} collective-permute-done((f32[64,512]{1,0:T(8,128)S(1)}, f32[64,512]{1,0:T(8,128)S(1)}, u32[]{:S(2)}, u32[]{:S(2)}) %collective-permute-start.6) | collective-permute-done | bytes 131104 | tf_op jit(solution)/shard_map/ppermute | solution.py:272
  22.6 1.5 %collective-permute-done.8.refs_3_ = f32[64,512]{1,0:T(8,128)S(1)} collective-permute-done((f32[64,512]{1,0:T(8,128)S(1)}, f32[64,512]{1,0:T(8,128)S(1)}, u32[]{:S(2)}, u32[]{:S(2)}) %collective-permute-start.8) | collective-permute-done | bytes 131104 | tf_op jit(solution)/shard_map/ppermute | solution.py:272
  24.1 0.1 collective-permute-start.9
  24.9 0.0 collective-permute-done.10.near_other
  24.9 1.0 %shard_map.46.right = f32[512,512]{1,0:T(8,128)S(1)} custom-call(f32[256,512]{1,0:T(8,128)S(1)} %shard_map.45.near, f32[256,512]{1,0:T(8,128)S(1)} %collective-permute-done.10.near_other, f32[512,512]{1,0:T(8,128)S(1)} %get-tuple-element.22.right), custom_call_target="tpu_custom_call" | custom-call | tf_op jit(solution)/shard_map/pallas_call | solution.py:32
  25.9 0.2 collective-permute-done.9.far_other
  26.1 2.3 %shard_map.47 = (f32[448,128]{1,0:T(8,128)S(1)}, f32[448,128]{1,0:T(8,128)S(1)}, f32[448,128]{1,0:T(8,128)S(1)}, f32[448,128]{1,0:T(8,128)S(1)}) custom-call(f32[256,512]{1,0:T(8,128)S(1)} %shard_map.44.far, f32[256,512]{1,0:T(8,128)S(1)} %collective-permute-done.9.far_other, f32[512,512]{1,0:T(8,128)S(1)} %get-tuple-element.21.left, ...), custom_call_target="tpu_custom_call" | custom-call | tf_op jit(solution)/shard_map/pallas_call | solution.py:32
  28.4 2.6 %collective-permute-start.13 = (f32[448,128]{1,0:T(8,128)S(1)}, f32[448,128]{1,0:T(8,128)S(1)}, u32[]{:S(2)}, u32[]{:S(2)}) collective-permute-start(f32[448,128]{1,0:T(8,128)S(1)} %get-tuple-element.26), channel_id=1, source_target_pairs={{0,1},{1,3},{3,2},{2,0},{4,5},{5,7},{7,6},{6,4},{8,9},{9,11},{11,1... | collective-permute-start | bytes 688136 | tf_op jit(solution)/shard_map/ppermute | solution.py:254
  31.1 0.7 %collective-permute-start.11 = (f32[448,128]{1,0:T(8,128)S(1)}, f32[448,128]{1,0:T(8,128)S(1)}, u32[]{:S(2)}, u32[]{:S(2)}) collective-permute-start(f32[448,128]{1,0:T(8,128)S(1)} %get-tuple-element.24), channel_id=1, source_target_pairs={{0,3},{3,0},{4,7},{7,4},{8,11},{11,8},{12,15},{15,12},{16,19},{19,... | collective-permute-start | bytes 688136 | tf_op jit(solution)/shard_map/ppermute | solution.py:254
  31.7 3.2 %collective-permute-start.12 = (f32[448,128]{1,0:T(8,128)S(1)}, f32[448,128]{1,0:T(8,128)S(1)}, u32[]{:S(2)}, u32[]{:S(2)}) collective-permute-start(f32[448,128]{1,0:T(8,128)S(1)} %get-tuple-element.25), channel_id=1, source_target_pairs={{0,1},{1,0},{2,3},{3,2},{4,5},{5,4},{6,7},{7,6},{8,9},{9,8},{10,11... | collective-permute-start | bytes 688136 | tf_op jit(solution)/shard_map/ppermute | solution.py:254
  34.9 6.5 %collective-permute-done.13.refs_4_ = f32[448,128]{1,0:T(8,128)S(1)} collective-permute-done((f32[448,128]{1,0:T(8,128)S(1)}, f32[448,128]{1,0:T(8,128)S(1)}, u32[]{:S(2)}, u32[]{:S(2)}) %collective-permute-start.13) | collective-permute-done | bytes 229408 | tf_op jit(solution)/shard_map/ppermute | solution.py:254
  41.4 1.9 %collective-permute-start.14 = (f32[448,128]{1,0:T(8,128)S(1)}, f32[448,128]{1,0:T(8,128)S(1)}, u32[]{:S(2)}, u32[]{:S(2)}) collective-permute-start(f32[448,128]{1,0:T(8,128)S(1)} %add.3), channel_id=1, source_target_pairs={{1,2},{2,1},{5,6},{6,5},{9,10},{10,9},{13,14},{14,13},{17,18},{18,... | collective-permute-start | bytes 688136 | tf_op jit(solution)/shard_map/ppermute | solution.py:254
  43.4 0.0 collective-permute-done.11.refs_1_
  43.4 2.7 %collective-permute-done.12.refs_2_ = f32[448,128]{1,0:T(8,128)S(1)} collective-permute-done((f32[448,128]{1,0:T(8,128)S(1)}, f32[448,128]{1,0:T(8,128)S(1)}, u32[]{:S(2)}, u32[]{:S(2)}) %collective-permute-start.12) | collective-permute-done | bytes 229408 | tf_op jit(solution)/shard_map/ppermute | solution.py:254
  46.1 3.8 %collective-permute-done.14.refs_3_ = f32[448,128]{1,0:T(8,128)S(1)} collective-permute-done((f32[448,128]{1,0:T(8,128)S(1)}, f32[448,128]{1,0:T(8,128)S(1)}, u32[]{:S(2)}, u32[]{:S(2)}) %collective-permute-start.14) | collective-permute-done | bytes 229408 | tf_op jit(solution)/shard_map/ppermute | solution.py:254
  49.9 0.9 %shard_map.48 = f32[512,128]{1,0:T(8,128)} custom-call(f32[448,128]{1,0:T(8,128)S(1)} %get-tuple-element.23.refs_0_, f32[448,128]{1,0:T(8,128)S(1)} %collective-permute-done.11.refs_1_, f32[448,128]{1,0:T(8,128)S(1)} %collective-permute-done.12.refs_2_, f32[448,128]{1,0:T(8,128)S(1)} %collective-permute-done.14.refs_3_, ...), custom_call_target="tpu_custom_call" | custom-call | tf_op jit(solution)/shard_map/pallas_call | solution.py:32
  (3 shorter events, 0.1 us)
Async XLA Ops:
  0.0 2.9 %collective-permute-start = (f32[512,512]{1,0:T(8,128)}, f32[512,512]{1,0:T(8,128)S(1)}, u32[]{:S(2)}, u32[]{:S(2)}) collective-permute-start(f32[512,512]{1,0:T(8,128)} %bitcast.4), channel_id=1, source_target_pairs={{0,4},{4,0},{8,12},{12,8},{16,20},{20,16},{24,28},{28,24},{1,5},{5... | collective-permute-start | bytes 3145736 | tf_op jit(solution)/shard_map/ppermute | solution.py:272
  0.0 1.2 %copy-start.1 = (f32[1,1,512,512]{3,2,1,0:T(8,128)S(1)}, f32[1,1,512,512]{3,2,1,0:T(8,128)}, u32[]{:S(2)}) copy-start(f32[1,1,512,512]{3,2,1,0:T(8,128)} %param.3) | copy-start | bytes 3145732
  1.3 6.3 %copy-start = (f32[512,512]{1,0:T(8,128)S(1)}, f32[512,512]{1,0:T(8,128)}, u32[]{:S(2)}) copy-start(f32[512,512]{1,0:T(8,128)} %target.1) | copy-start | bytes 3145732
  3.5 6.9 %collective-permute-start.1 = (f32[64,512]{1,0:T(8,128)S(1)}, f32[64,512]{1,0:T(8,128)S(1)}, u32[]{:S(2)}, u32[]{:S(2)}) collective-permute-start(f32[64,512]{1,0:T(8,128)S(1)} %get-tuple-element.16), channel_id=1, source_target_pairs={{0,8},{4,12},{8,0},{12,4},{16,24},{20,28},{24,16},{28,20},{1,9},{5... | collective-permute-start | bytes 393224 | tf_op jit(solution)/shard_map/ppermute | solution.py:272
  4.2 8.6 %collective-permute-start.3 = (f32[64,512]{1,0:T(8,128)S(1)}, f32[64,512]{1,0:T(8,128)S(1)}, u32[]{:S(2)}, u32[]{:S(2)}) collective-permute-start(f32[64,512]{1,0:T(8,128)S(1)} %get-tuple-element.18), channel_id=1, source_target_pairs={{0,8},{4,12},{8,0},{12,4},{16,24},{20,28},{24,16},{28,20},{1,9},{5... | collective-permute-start | bytes 393224 | tf_op jit(solution)/shard_map/ppermute | solution.py:272
  5.6 9.9 %collective-permute-start.5 = (f32[64,512]{1,0:T(8,128)S(1)}, f32[64,512]{1,0:T(8,128)S(1)}, u32[]{:S(2)}, u32[]{:S(2)}) collective-permute-start(f32[64,512]{1,0:T(8,128)S(1)} %get-tuple-element.19), channel_id=1, source_target_pairs={{0,8},{4,12},{8,0},{12,4},{16,24},{20,28},{24,16},{28,20},{1,9},{5... | collective-permute-start | bytes 393224 | tf_op jit(solution)/shard_map/ppermute | solution.py:272
  6.2 11.3 %collective-permute-start.7 = (f32[64,512]{1,0:T(8,128)S(1)}, f32[64,512]{1,0:T(8,128)S(1)}, u32[]{:S(2)}, u32[]{:S(2)}) collective-permute-start(f32[64,512]{1,0:T(8,128)S(1)} %get-tuple-element.20), channel_id=1, source_target_pairs={{0,8},{4,12},{8,0},{12,4},{16,24},{20,28},{24,16},{28,20},{1,9},{5... | collective-permute-start | bytes 393224 | tf_op jit(solution)/shard_map/ppermute | solution.py:272
  10.8 7.8 %collective-permute-start.2 = (f32[64,512]{1,0:T(8,128)S(1)}, f32[64,512]{1,0:T(8,128)S(1)}, u32[]{:S(2)}, u32[]{:S(2)}) collective-permute-start(f32[64,512]{1,0:T(8,128)S(1)} %shard_map.40), channel_id=1, source_target_pairs={{0,16},{4,20},{8,24},{12,28},{16,0},{20,4},{24,8},{28,12},{1,17},{... | collective-permute-start | bytes 393224 | tf_op jit(solution)/shard_map/ppermute | solution.py:272
  13.1 6.7 %collective-permute-start.4 = (f32[64,512]{1,0:T(8,128)S(1)}, f32[64,512]{1,0:T(8,128)S(1)}, u32[]{:S(2)}, u32[]{:S(2)}) collective-permute-start(f32[64,512]{1,0:T(8,128)S(1)} %shard_map.41), channel_id=1, source_target_pairs={{0,16},{4,20},{8,24},{12,28},{16,0},{20,4},{24,8},{28,12},{1,17},{... | collective-permute-start | bytes 393224 | tf_op jit(solution)/shard_map/ppermute | solution.py:272
  15.9 6.7 %collective-permute-start.6 = (f32[64,512]{1,0:T(8,128)S(1)}, f32[64,512]{1,0:T(8,128)S(1)}, u32[]{:S(2)}, u32[]{:S(2)}) collective-permute-start(f32[64,512]{1,0:T(8,128)S(1)} %shard_map.42), channel_id=1, source_target_pairs={{0,16},{4,20},{8,24},{12,28},{16,0},{20,4},{24,8},{28,12},{1,17},{... | collective-permute-start | bytes 393224 | tf_op jit(solution)/shard_map/ppermute | solution.py:272
  17.9 6.2 %collective-permute-start.8 = (f32[64,512]{1,0:T(8,128)S(1)}, f32[64,512]{1,0:T(8,128)S(1)}, u32[]{:S(2)}, u32[]{:S(2)}) collective-permute-start(f32[64,512]{1,0:T(8,128)S(1)} %shard_map.43), channel_id=1, source_target_pairs={{0,16},{4,20},{8,24},{12,28},{16,0},{20,4},{24,8},{28,12},{1,17},{... | collective-permute-start | bytes 393224 | tf_op jit(solution)/shard_map/ppermute | solution.py:272
  18.6 6.3 %collective-permute-start.10 = (f32[256,512]{1,0:T(8,128)S(1)}, f32[256,512]{1,0:T(8,128)S(1)}, u32[]{:S(2)}, u32[]{:S(2)}) collective-permute-start(f32[256,512]{1,0:T(8,128)S(1)} %shard_map.45.near), channel_id=1, source_target_pairs={{0,4},{4,0},{8,12},{12,8},{16,20},{20,16},{24,28},{28,24},{1,5},{5... | collective-permute-start | bytes 1572872 | tf_op jit(solution)/shard_map/ppermute | solution.py:272
  24.1 2.0 %collective-permute-start.9 = (f32[256,512]{1,0:T(8,128)S(1)}, f32[256,512]{1,0:T(8,128)S(1)}, u32[]{:S(2)}, u32[]{:S(2)}) collective-permute-start(f32[256,512]{1,0:T(8,128)S(1)} %shard_map.44.far), channel_id=1, source_target_pairs={{0,4},{4,0},{8,12},{12,8},{16,20},{20,16},{24,28},{28,24},{1,5},{5... | collective-permute-start | bytes 1572872 | tf_op jit(solution)/shard_map/ppermute | solution.py:272
  28.4 13.0 %collective-permute-start.13 = (f32[448,128]{1,0:T(8,128)S(1)}, f32[448,128]{1,0:T(8,128)S(1)}, u32[]{:S(2)}, u32[]{:S(2)}) collective-permute-start(f32[448,128]{1,0:T(8,128)S(1)} %get-tuple-element.26), channel_id=1, source_target_pairs={{0,1},{1,3},{3,2},{2,0},{4,5},{5,7},{7,6},{6,4},{8,9},{9,11},{11,1... | collective-permute-start | bytes 688136 | tf_op jit(solution)/shard_map/ppermute | solution.py:254
  31.1 12.3 %collective-permute-start.11 = (f32[448,128]{1,0:T(8,128)S(1)}, f32[448,128]{1,0:T(8,128)S(1)}, u32[]{:S(2)}, u32[]{:S(2)}) collective-permute-start(f32[448,128]{1,0:T(8,128)S(1)} %get-tuple-element.24), channel_id=1, source_target_pairs={{0,3},{3,0},{4,7},{7,4},{8,11},{11,8},{12,15},{15,12},{16,19},{19,... | collective-permute-start | bytes 688136 | tf_op jit(solution)/shard_map/ppermute | solution.py:254
  31.7 14.4 %collective-permute-start.12 = (f32[448,128]{1,0:T(8,128)S(1)}, f32[448,128]{1,0:T(8,128)S(1)}, u32[]{:S(2)}, u32[]{:S(2)}) collective-permute-start(f32[448,128]{1,0:T(8,128)S(1)} %get-tuple-element.25), channel_id=1, source_target_pairs={{0,1},{1,0},{2,3},{3,2},{4,5},{5,4},{6,7},{7,6},{8,9},{9,8},{10,11... | collective-permute-start | bytes 688136 | tf_op jit(solution)/shard_map/ppermute | solution.py:254
  41.4 8.4 %collective-permute-start.14 = (f32[448,128]{1,0:T(8,128)S(1)}, f32[448,128]{1,0:T(8,128)S(1)}, u32[]{:S(2)}, u32[]{:S(2)}) collective-permute-start(f32[448,128]{1,0:T(8,128)S(1)} %add.3), channel_id=1, source_target_pairs={{1,2},{2,1},{5,6},{6,5},{9,10},{10,9},{13,14},{14,13},{17,18},{18,... | collective-permute-start | bytes 688136 | tf_op jit(solution)/shard_map/ppermute | solution.py:254

commit v5 on v4

--- a/solution.py
+++ b/solution.py
@@ -208,25 +208,45 @@
     return jnp.concatenate([top, jnp.where(column < half, -over[half:, :], low)], 0)
 
 
-def gradient_kernel(turned_level, order_of, packed, far, far_other, left, right, weight, *refs):
-    blocks, (full, terms) = refs[:-2], refs[-2:]
+def lay_out(block, part, which, packed):
+    rows, columns = part.shape
+    if not packed:
+        for j in range(columns // LANES):
+            block[j * rows:(j + 1) * rows, :] = part[:, j * LANES:(j + 1) * LANES]
+        return
+    count = columns // rows
+    for j in range(count - 1):
+        at = jnp.where(j < which, j, j + 1)
+        block[j * rows:(j + 1) * rows, :] = part[:, pl.ds(pl.multiple_of(at * rows, LANES), rows)]
+    block[(count - 1) * rows:, :] = pack(part[:, pl.ds(pl.multiple_of(which * rows, LANES), rows)])
+
+
+def sign(turned_level, weight):
+    return weight[...] * (0.5 - bit(turned_level).astype(f32))
+
+
+def first_block_kernel(turned_level, which_of, far, far_other, left, right, weight, cyclic, block, full, part):
     place(full, [far], [far_other])
-    scale = weight[...] * (0.5 - bit(turned_level).astype(f32))
-    cyclic = product(left[...], product(full[...], right[...]))
-    terms[...] = scale * (cyclic - cyclic.T)
-    rows = terms.shape[0] // len(blocks)
+    cyclic[...] = product(left[...], product(full[...], right[...]))
+    rows = part.shape[0]
+    which = which_of(lax.axis_index("ens"))
+    at = pl.ds(pl.multiple_of(which * rows, LANES), rows)
+    part[...] = sign(turned_level, weight) * (cyclic[at, :] - cyclic[:, at].T)
+    lay_out(block, part, which, True)
+
+
+def blocks_kernel(turned_level, which_of, packed, cyclic, weight, *refs):
+    blocks, terms = refs[:-1], refs[-1]
+    terms[...] = sign(turned_level, weight) * (cyclic[...] - cyclic[...].T)
+    rows = terms.shape[0] // lax.axis_size("ens")
     here = lax.axis_index("ens")
-    for step, block in enumerate(blocks):
-        which = order_of(here, step)
-        at = pl.ds(pl.multiple_of(which * rows, 8), rows)
-        if packed:
-            for j in range(len(blocks) - 1):
-                column = jnp.where(j < which, j, j + 1)
-                block[j * rows:(j + 1) * rows, :] = terms[at, pl.ds(pl.multiple_of(column * rows, LANES), rows)]
-            block[(len(blocks) - 1) * rows:, :] = pack(terms[at, pl.ds(pl.multiple_of(which * rows, LANES), rows)])
-        else:
-            for j in range(terms.shape[1] // LANES):
-                block[j * rows:(j + 1) * rows, :] = terms[at, j * LANES:(j + 1) * LANES]
+    for which, block in zip(which_of(here), blocks):
+        lay_out(block, terms.at[pl.ds(pl.multiple_of(which * rows, 8), rows), :], which, packed)
+
+
+def cyclic_kernel(far, far_other, left, right, cyclic, full):
+    place(full, [far], [far_other])
+    cyclic[...] = product(left[...], product(full[...], right[...]))
 
 
 def sum_kernel(rows, packed, *refs):
@@ -292,10 +312,22 @@
     rows, spread = order // members, order // LANES
     packed = rows == LANES
     block = (rows * spread - packed * rows // 2, LANES)
-    order_of = (lambda here, step: here ^ step) if members == 4 else (lambda here, step: lax.rem(here + step, members))
-    blocks = call(
-        functools.partial(gradient_kernel, top - 1, order_of, packed),
-        [block] * members, far, swap(far, 0), left, right, weights.reshape(1, 1), scratch=[square] * 2)
+    factors = (far, swap(far, 0), left, right, weights.reshape(1, 1))
+    if members == 4 and packed:
+        cyclic, over_two = call(
+            functools.partial(first_block_kernel, top - 1, lambda here: here ^ 2), [square, block], *factors,
+            scratch=[square, (rows, order)])
+        blocks = call(
+            functools.partial(blocks_kernel, top - 1, lambda here: (here, here ^ 1, here ^ 3), packed), [block] * 3,
+            cyclic, factors[-1], scratch=[square])
+        blocks = [blocks[0], blocks[1], over_two, blocks[2]]
+    else:
+        order_of = (lambda here: [here ^ s for s in range(members)]) if members == 4 else (
+            lambda here: [lax.rem(here + s, members) for s in range(members)])
+        cyclic = call(cyclic_kernel, [square], *factors[:4], scratch=[square])[0]
+        blocks = call(
+            functools.partial(blocks_kernel, top - 1, order_of, packed), [block] * members, cyclic, factors[-1],
+            scratch=[square])
     arrived = send_rows(blocks)
     total = call(
         functools.partial(sum_kernel, rows, packed), [(rows * spread, LANES)], blocks[0], *arrived,

time: 51 us -> 50.6 us (level)
  waiting for transfers between devices: 24.8 us -> 23.8 us
  Pallas kernels: 9.45 us -> 10 us
    ppermute x4, waiting for transfers between devices: 13 us -> 12.1 us  [move(): return lax.ppermute(x, 'ens', pairs)]
    pallas_call x12 -> x13, Pallas kernels: 9.45 us -> 10 us  [call(): pl.pallas_call(kernel, out_shape=[jax.ShapeDtypeStruct(s, f32) for s in o...]
  transfers between devices with their start and end apart: 15 -> 15, of which waited for: 11 -> 11; matrix products, arithmetic and copies ran while one was open for 0% -> 0% of each run, Pallas kernels for 11% -> 12%
where the time goes in v5:
time: 50.6 us; the launch traced here: 50.4 us
  waiting for transfers between devices  23.8 us (47%)
  starting transfers between devices  14.5 us (29%)
  Pallas kernels  10 us (20%)
  local copies, waits for them, and re-layouts  1.23 us (2%)
  between operations  0.81 us (2%)
    ppermute x4, waiting for transfers between devices, move(): return lax.ppermute(x, 'ens', pairs)  12.1 us
    ppermute x11, waiting for transfers between devices, swap(): return lax.ppermute(x, 'tm', [(i, i ^ 1 << level) for i in range(slices)])  11.8 us
    pallas_call x13, Pallas kernels, call(): pl.pallas_call(kernel, out_shape=[jax.ShapeDtypeStruct(s, f32) for s in o...  10 us
    ppermute x4, starting transfers between devices, move(): return lax.ppermute(x, 'ens', pairs)  8.45 us
    ppermute x11, starting transfers between devices, swap(): return lax.ppermute(x, 'tm', [(i, i ^ 1 << level) for i in range(slices)])  6.07 us
    unnamed x4, local copies, waits for them, and re-layouts  1.23 us
  transfers between devices with their start and end apart: 15, of which 11 were waited for; matrix products, arithmetic and copies ran while one was open for 0% of the time, Pallas kernels for 12%

profile of v5, /device:TPU:14, one launch (start us, length us, event | category | flops | bytes accessed | tf_op | source)
XLA Modules:
  0.0 50.4 jit_solution(13135561403546260131)
XLA Ops:
  0.0 0.0 collective-permute-start
  0.0 0.0 copy-start.1
  0.0 1.2 %copy-done.1 = f32[1,1,512,512]{3,2,1,0:T(8,128)S(1)} copy-done((f32[1,1,512,512]{3,2,1,0:T(8,128)S(1)}, f32[1,1,512,512]{3,2,1,0:T(8,128)}, u32[]{:S(2)}) %copy-start.1) | copy-done | bytes 1048600
  1.2 0.1 shard_map.37.mine
  1.3 0.0 copy-start
  1.3 1.6 %collective-permute-done.other = f32[512,512]{1,0:T(8,128)S(1)} collective-permute-done((f32[512,512]{1,0:T(8,128)}, f32[512,512]{1,0:T(8,128)S(1)}, u32[]{:S(2)}, u32[]{:S(2)}) %collective-permute-start) | collective-permute-done | bytes 1048608 | tf_op jit(solution)/shard_map/ppermute | solution.py:292
  2.9 0.6 %shard_map.38 = (f32[64,512]{1,0:T(8,128)S(1)}, f32[64,512]{1,0:T(8,128)S(1)}, f32[64,512]{1,0:T(8,128)S(1)}, f32[64,512]{1,0:T(8,128)S(1)}) custom-call(f32[512,512]{1,0:T(8,128)S(1)} %shard_map.37.mine, f32[512,512]{1,0:T(8,128)S(1)} %collective-permute-done.other), custom_call_target="tpu_custom_call" | custom-call | tf_op jit(solution)/shard_map/pallas_call | solution.py:32
  3.5 0.7 %collective-permute-start.1 = (f32[64,512]{1,0:T(8,128)S(1)}, f32[64,512]{1,0:T(8,128)S(1)}, u32[]{:S(2)}, u32[]{:S(2)}) collective-permute-start(f32[64,512]{1,0:T(8,128)S(1)} %get-tuple-element.17), channel_id=1, source_target_pairs={{0,8},{4,12},{8,0},{12,4},{16,24},{20,28},{24,16},{28,20},{1,9},{5... | collective-permute-start | bytes 393224 | tf_op jit(solution)/shard_map/ppermute | solution.py:292
  4.2 1.4 %collective-permute-start.3 = (f32[64,512]{1,0:T(8,128)S(1)}, f32[64,512]{1,0:T(8,128)S(1)}, u32[]{:S(2)}, u32[]{:S(2)}) collective-permute-start(f32[64,512]{1,0:T(8,128)S(1)} %get-tuple-element.19), channel_id=1, source_target_pairs={{0,8},{4,12},{8,0},{12,4},{16,24},{20,28},{24,16},{28,20},{1,9},{5... | collective-permute-start | bytes 393224 | tf_op jit(solution)/shard_map/ppermute | solution.py:292
  5.6 0.6 %collective-permute-start.5 = (f32[64,512]{1,0:T(8,128)S(1)}, f32[64,512]{1,0:T(8,128)S(1)}, u32[]{:S(2)}, u32[]{:S(2)}) collective-permute-start(f32[64,512]{1,0:T(8,128)S(1)} %get-tuple-element.20), channel_id=1, source_target_pairs={{0,8},{4,12},{8,0},{12,4},{16,24},{20,28},{24,16},{28,20},{1,9},{5... | collective-permute-start | bytes 393224 | tf_op jit(solution)/shard_map/ppermute | solution.py:292
  6.2 1.4 %collective-permute-start.7 = (f32[64,512]{1,0:T(8,128)S(1)}, f32[64,512]{1,0:T(8,128)S(1)}, u32[]{:S(2)}, u32[]{:S(2)}) collective-permute-start(f32[64,512]{1,0:T(8,128)S(1)} %get-tuple-element.21), channel_id=1, source_target_pairs={{0,8},{4,12},{8,0},{12,4},{16,24},{20,28},{24,16},{28,20},{1,9},{5... | collective-permute-start | bytes 393224 | tf_op jit(solution)/shard_map/ppermute | solution.py:292
  7.6 0.0 copy-done
  7.6 2.8 %shard_map.39 = (f32[512,512]{1,0:T(8,128)S(1)}, f32[512,512]{1,0:T(8,128)S(1)}, f32[512,512]{1,0:T(8,128)S(1)}) custom-call(f32[512,512]{1,0:T(8,128)S(1)} %shard_map.37.mine, f32[512,512]{1,0:T(8,128)S(1)} %collective-permute-done.other, f32[512,512]{1,0:T(8,128)S(1)} %copy-done), custom_call_target="tpu_custom_call" | custom-call | tf_op jit(solution)/shard_map/pallas_call | solution.py:32
  10.4 0.0 collective-permute-done.1.got.refs_0_
  10.4 0.4 shard_map.40
  10.8 0.1 collective-permute-start.2
  10.9 1.8 %collective-permute-done.3.got.refs_1_ = f32[64,512]{1,0:T(8,128)S(1)} collective-permute-done((f32[64,512]{1,0:T(8,128)S(1)}, f32[64,512]{1,0:T(8,128)S(1)}, u32[]{:S(2)}, u32[]{:S(2)}) %collective-permute-start.3) | collective-permute-done | bytes 131104 | tf_op jit(solution)/shard_map/ppermute | solution.py:292
  12.7 0.4 shard_map.41
  13.1 0.6 %collective-permute-start.4 = (f32[64,512]{1,0:T(8,128)S(1)}, f32[64,512]{1,0:T(8,128)S(1)}, u32[]{:S(2)}, u32[]{:S(2)}) collective-permute-start(f32[64,512]{1,0:T(8,128)S(1)} %shard_map.41), channel_id=1, source_target_pairs={{0,16},{4,20},{8,24},{12,28},{16,0},{20,4},{24,8},{28,12},{1,17},{... | collective-permute-start | bytes 393224 | tf_op jit(solution)/shard_map/ppermute | solution.py:292
  13.7 1.8 %collective-permute-done.5.got.refs_2_ = f32[64,512]{1,0:T(8,128)S(1)} collective-permute-done((f32[64,512]{1,0:T(8,128)S(1)}, f32[64,512]{1,0:T(8,128)S(1)}, u32[]{:S(2)}, u32[]{:S(2)}) %collective-permute-start.5) | collective-permute-done | bytes 131104 | tf_op jit(solution)/shard_map/ppermute | solution.py:292
  15.5 0.4 shard_map.42
  15.9 0.6 %collective-permute-start.6 = (f32[64,512]{1,0:T(8,128)S(1)}, f32[64,512]{1,0:T(8,128)S(1)}, u32[]{:S(2)}, u32[]{:S(2)}) collective-permute-start(f32[64,512]{1,0:T(8,128)S(1)} %shard_map.42), channel_id=1, source_target_pairs={{0,16},{4,20},{8,24},{12,28},{16,0},{20,4},{24,8},{28,12},{1,17},{... | collective-permute-start | bytes 393224 | tf_op jit(solution)/shard_map/ppermute | solution.py:292
  16.5 1.0 %collective-permute-done.7.got.refs_3_ = f32[64,512]{1,0:T(8,128)S(1)} collective-permute-done((f32[64,512]{1,0:T(8,128)S(1)}, f32[64,512]{1,0:T(8,128)S(1)}, u32[]{:S(2)}, u32[]{:S(2)}) %collective-permute-start.7) | collective-permute-done | bytes 131104 | tf_op jit(solution)/shard_map/ppermute | solution.py:292
  17.5 0.4 shard_map.43
  17.9 0.6 %collective-permute-start.8 = (f32[64,512]{1,0:T(8,128)S(1)}, f32[64,512]{1,0:T(8,128)S(1)}, u32[]{:S(2)}, u32[]{:S(2)}) collective-permute-start(f32[64,512]{1,0:T(8,128)S(1)} %shard_map.43), channel_id=1, source_target_pairs={{0,16},{4,20},{8,24},{12,28},{16,0},{20,4},{24,8},{28,12},{1,17},{... | collective-permute-start | bytes 393224 | tf_op jit(solution)/shard_map/ppermute | solution.py:292
  18.6 0.1 collective-permute-start.10
  18.6 0.0 collective-permute-done.2.refs_0_
  18.6 1.2 %collective-permute-done.4.refs_1_ = f32[64,512]{1,0:T(8,128)S(1)} collective-permute-done((f32[64,512]{1,0:T(8,128)S(1)}, f32[64,512]{1,0:T(8,128)S(1)}, u32[]{:S(2)}, u32[]{:S(2)}) %collective-permute-start.4) | collective-permute-done | bytes 131104 | tf_op jit(solution)/shard_map/ppermute | solution.py:292
  19.8 2.8 %collective-permute-done.6.refs_2_ = f32[64,512]{1,0:T(8,128)S(1)} collective-permute-done((f32[64,512]{1,0:T(8,128)S(1)}, f32[64,512]{1,0:T(8,128)S(1)}, u32[]{:S(2)}, u32[]{:S(2)}) %collective-permute-start.6) | collective-permute-done | bytes 131104 | tf_op jit(solution)/shard_map/ppermute | solution.py:292
  22.6 1.5 %collective-permute-done.8.refs_3_ = f32[64,512]{1,0:T(8,128)S(1)} collective-permute-done((f32[64,512]{1,0:T(8,128)S(1)}, f32[64,512]{1,0:T(8,128)S(1)}, u32[]{:S(2)}, u32[]{:S(2)}) %collective-permute-start.8) | collective-permute-done | bytes 131104 | tf_op jit(solution)/shard_map/ppermute | solution.py:292
  24.1 0.1 collective-permute-start.9
  24.9 0.0 collective-permute-done.10.near_other
  24.9 1.0 %shard_map.46.right = f32[512,512]{1,0:T(8,128)S(1)} custom-call(f32[256,512]{1,0:T(8,128)S(1)} %shard_map.45.near, f32[256,512]{1,0:T(8,128)S(1)} %collective-permute-done.10.near_other, f32[512,512]{1,0:T(8,128)S(1)} %get-tuple-element.23.right), custom_call_target="tpu_custom_call" | custom-call | tf_op jit(solution)/shard_map/pallas_call | solution.py:32
  25.9 0.2 collective-permute-done.9.far_other
  26.1 2.2 %shard_map.47 = (f32[512,512]{1,0:T(8,128)S(1)}, f32[448,128]{1,0:T(8,128)S(1)}) custom-call(f32[256,512]{1,0:T(8,128)S(1)} %shard_map.44.far, f32[256,512]{1,0:T(8,128)S(1)} %collective-permute-done.9.far_other, f32[512,512]{1,0:T(8,128)S(1)} %get-tuple-element.22.left, f32[512,512]{1,0:T(8,128)S(1)} %shard_map.46.right, f32[1,1]{1,0:T(1,128)} %bitcast.3.weight), custom_call_target="tpu_custom_call" | custom-call | tf_op jit(solution)/shard_map/pallas_call | solution.py:32
  28.3 2.7 %collective-permute-start.13 = (f32[448,128]{1,0:T(8,128)S(1)}, f32[448,128]{1,0:T(8,128)S(1)}, u32[]{:S(2)}, u32[]{:S(2)}) collective-permute-start(f32[448,128]{1,0:T(8,128)S(1)} %get-tuple-element.28), channel_id=1, source_target_pairs={{0,1},{1,3},{3,2},{2,0},{4,5},{5,7},{7,6},{6,4},{8,9},{9,11},{11,1... | collective-permute-start | bytes 688136 | tf_op jit(solution)/shard_map/ppermute | solution.py:274
  31.0 0.6 %shard_map.48 = (f32[448,128]{1,0:T(8,128)S(1)}, f32[448,128]{1,0:T(8,128)S(1)}, f32[448,128]{1,0:T(8,128)S(1)}) custom-call(f32[512,512]{1,0:T(8,128)S(1)} %get-tuple-element.24.cyclic, f32[1,1]{1,0:T(1,128)} %bitcast.4.weight), custom_call_target="tpu_custom_call" | custom-call | tf_op jit(solution)/shard_map/pallas_call | solution.py:32
  31.6 0.7 %collective-permute-start.11 = (f32[448,128]{1,0:T(8,128)S(1)}, f32[448,128]{1,0:T(8,128)S(1)}, u32[]{:S(2)}, u32[]{:S(2)}) collective-permute-start(f32[448,128]{1,0:T(8,128)S(1)} %get-tuple-element.26), channel_id=1, source_target_pairs={{0,3},{3,0},{4,7},{7,4},{8,11},{11,8},{12,15},{15,12},{16,19},{19,... | collective-permute-start | bytes 688136 | tf_op jit(solution)/shard_map/ppermute | solution.py:274
  32.3 3.2 %collective-permute-start.12 = (f32[448,128]{1,0:T(8,128)S(1)}, f32[448,128]{1,0:T(8,128)S(1)}, u32[]{:S(2)}, u32[]{:S(2)}) collective-permute-start(f32[448,128]{1,0:T(8,128)S(1)} %get-tuple-element.27), channel_id=1, source_target_pairs={{0,1},{1,0},{2,3},{3,2},{4,5},{5,4},{6,7},{7,6},{8,9},{9,8},{10,11... | collective-permute-start | bytes 688136 | tf_op jit(solution)/shard_map/ppermute | solution.py:274
  35.5 5.8 %collective-permute-done.13.refs_4_ = f32[448,128]{1,0:T(8,128)S(1)} collective-permute-done((f32[448,128]{1,0:T(8,128)S(1)}, f32[448,128]{1,0:T(8,128)S(1)}, u32[]{:S(2)}, u32[]{:S(2)}) %collective-permute-start.13) | collective-permute-done | bytes 229408 | tf_op jit(solution)/shard_map/ppermute | solution.py:274
  41.4 1.9 %collective-permute-start.14 = (f32[448,128]{1,0:T(8,128)S(1)}, f32[448,128]{1,0:T(8,128)S(1)}, u32[]{:S(2)}, u32[]{:S(2)}) collective-permute-start(f32[448,128]{1,0:T(8,128)S(1)} %add.3), channel_id=1, source_target_pairs={{1,2},{2,1},{5,6},{6,5},{9,10},{10,9},{13,14},{14,13},{17,18},{18,... | collective-permute-start | bytes 688136 | tf_op jit(solution)/shard_map/ppermute | solution.py:274
  43.3 0.0 collective-permute-done.11.refs_1_
  43.3 2.8 %collective-permute-done.12.refs_2_ = f32[448,128]{1,0:T(8,128)S(1)} collective-permute-done((f32[448,128]{1,0:T(8,128)S(1)}, f32[448,128]{1,0:T(8,128)S(1)}, u32[]{:S(2)}, u32[]{:S(2)}) %collective-permute-start.12) | collective-permute-done | bytes 229408 | tf_op jit(solution)/shard_map/ppermute | solution.py:274
  46.1 3.4 %collective-permute-done.14.refs_3_ = f32[448,128]{1,0:T(8,128)S(1)} collective-permute-done((f32[448,128]{1,0:T(8,128)S(1)}, f32[448,128]{1,0:T(8,128)S(1)}, u32[]{:S(2)}, u32[]{:S(2)}) %collective-permute-start.14) | collective-permute-done | bytes 229408 | tf_op jit(solution)/shard_map/ppermute | solution.py:274
  49.5 0.9 %shard_map.49 = f32[512,128]{1,0:T(8,128)} custom-call(f32[448,128]{1,0:T(8,128)S(1)} %get-tuple-element.25.refs_0_, f32[448,128]{1,0:T(8,128)S(1)} %collective-permute-done.11.refs_1_, f32[448,128]{1,0:T(8,128)S(1)} %collective-permute-done.12.refs_2_, f32[448,128]{1,0:T(8,128)S(1)} %collective-permute-done.14.refs_3_, ...), custom_call_target="tpu_custom_call" | custom-call | tf_op jit(solution)/shard_map/pallas_call | solution.py:32
  (3 shorter events, 0.1 us)
Async XLA Ops:
  0.0 2.9 %collective-permute-start = (f32[512,512]{1,0:T(8,128)}, f32[512,512]{1,0:T(8,128)S(1)}, u32[]{:S(2)}, u32[]{:S(2)}) collective-permute-start(f32[512,512]{1,0:T(8,128)} %bitcast.5), channel_id=1, source_target_pairs={{0,4},{4,0},{8,12},{12,8},{16,20},{20,16},{24,28},{28,24},{1,5},{5... | collective-permute-start | bytes 3145736 | tf_op jit(solution)/shard_map/ppermute | solution.py:292
  0.0 1.2 %copy-start.1 = (f32[1,1,512,512]{3,2,1,0:T(8,128)S(1)}, f32[1,1,512,512]{3,2,1,0:T(8,128)}, u32[]{:S(2)}) copy-start(f32[1,1,512,512]{3,2,1,0:T(8,128)} %param.3) | copy-start | bytes 3145732
  1.3 6.3 %copy-start = (f32[512,512]{1,0:T(8,128)S(1)}, f32[512,512]{1,0:T(8,128)}, u32[]{:S(2)}) copy-start(f32[512,512]{1,0:T(8,128)} %target.1) | copy-start | bytes 3145732
  3.5 6.9 %collective-permute-start.1 = (f32[64,512]{1,0:T(8,128)S(1)}, f32[64,512]{1,0:T(8,128)S(1)}, u32[]{:S(2)}, u32[]{:S(2)}) collective-permute-start(f32[64,512]{1,0:T(8,128)S(1)} %get-tuple-element.17), channel_id=1, source_target_pairs={{0,8},{4,12},{8,0},{12,4},{16,24},{20,28},{24,16},{28,20},{1,9},{5... | collective-permute-start | bytes 393224 | tf_op jit(solution)/shard_map/ppermute | solution.py:292
  4.2 8.6 %collective-permute-start.3 = (f32[64,512]{1,0:T(8,128)S(1)}, f32[64,512]{1,0:T(8,128)S(1)}, u32[]{:S(2)}, u32[]{:S(2)}) collective-permute-start(f32[64,512]{1,0:T(8,128)S(1)} %get-tuple-element.19), channel_id=1, source_target_pairs={{0,8},{4,12},{8,0},{12,4},{16,24},{20,28},{24,16},{28,20},{1,9},{5... | collective-permute-start | bytes 393224 | tf_op jit(solution)/shard_map/ppermute | solution.py:292
  5.6 9.9 %collective-permute-start.5 = (f32[64,512]{1,0:T(8,128)S(1)}, f32[64,512]{1,0:T(8,128)S(1)}, u32[]{:S(2)}, u32[]{:S(2)}) collective-permute-start(f32[64,512]{1,0:T(8,128)S(1)} %get-tuple-element.20), channel_id=1, source_target_pairs={{0,8},{4,12},{8,0},{12,4},{16,24},{20,28},{24,16},{28,20},{1,9},{5... | collective-permute-start | bytes 393224 | tf_op jit(solution)/shard_map/ppermute | solution.py:292
  6.2 11.3 %collective-permute-start.7 = (f32[64,512]{1,0:T(8,128)S(1)}, f32[64,512]{1,0:T(8,128)S(1)}, u32[]{:S(2)}, u32[]{:S(2)}) collective-permute-start(f32[64,512]{1,0:T(8,128)S(1)} %get-tuple-element.21), channel_id=1, source_target_pairs={{0,8},{4,12},{8,0},{12,4},{16,24},{20,28},{24,16},{28,20},{1,9},{5... | collective-permute-start | bytes 393224 | tf_op jit(solution)/shard_map/ppermute | solution.py:292
  10.8 7.8 %collective-permute-start.2 = (f32[64,512]{1,0:T(8,128)S(1)}, f32[64,512]{1,0:T(8,128)S(1)}, u32[]{:S(2)}, u32[]{:S(2)}) collective-permute-start(f32[64,512]{1,0:T(8,128)S(1)} %shard_map.40), channel_id=1, source_target_pairs={{0,16},{4,20},{8,24},{12,28},{16,0},{20,4},{24,8},{28,12},{1,17},{... | collective-permute-start | bytes 393224 | tf_op jit(solution)/shard_map/ppermute | solution.py:292
  13.1 6.7 %collective-permute-start.4 = (f32[64,512]{1,0:T(8,128)S(1)}, f32[64,512]{1,0:T(8,128)S(1)}, u32[]{:S(2)}, u32[]{:S(2)}) collective-permute-start(f32[64,512]{1,0:T(8,128)S(1)} %shard_map.41), channel_id=1, source_target_pairs={{0,16},{4,20},{8,24},{12,28},{16,0},{20,4},{24,8},{28,12},{1,17},{... | collective-permute-start | bytes 393224 | tf_op jit(solution)/shard_map/ppermute | solution.py:292
  15.9 6.7 %collective-permute-start.6 = (f32[64,512]{1,0:T(8,128)S(1)}, f32[64,512]{1,0:T(8,128)S(1)}, u32[]{:S(2)}, u32[]{:S(2)}) collective-permute-start(f32[64,512]{1,0:T(8,128)S(1)} %shard_map.42), channel_id=1, source_target_pairs={{0,16},{4,20},{8,24},{12,28},{16,0},{20,4},{24,8},{28,12},{1,17},{... | collective-permute-start | bytes 393224 | tf_op jit(solution)/shard_map/ppermute | solution.py:292
  17.9 6.2 %collective-permute-start.8 = (f32[64,512]{1,0:T(8,128)S(1)}, f32[64,512]{1,0:T(8,128)S(1)}, u32[]{:S(2)}, u32[]{:S(2)}) collective-permute-start(f32[64,512]{1,0:T(8,128)S(1)} %shard_map.43), channel_id=1, source_target_pairs={{0,16},{4,20},{8,24},{12,28},{16,0},{20,4},{24,8},{28,12},{1,17},{... | collective-permute-start | bytes 393224 | tf_op jit(solution)/shard_map/ppermute | solution.py:292
  18.6 6.3 %collective-permute-start.10 = (f32[256,512]{1,0:T(8,128)S(1)}, f32[256,512]{1,0:T(8,128)S(1)}, u32[]{:S(2)}, u32[]{:S(2)}) collective-permute-start(f32[256,512]{1,0:T(8,128)S(1)} %shard_map.45.near), channel_id=1, source_target_pairs={{0,4},{4,0},{8,12},{12,8},{16,20},{20,16},{24,28},{28,24},{1,5},{5... | collective-permute-start | bytes 1572872 | tf_op jit(solution)/shard_map/ppermute | solution.py:292
  24.1 2.0 %collective-permute-start.9 = (f32[256,512]{1,0:T(8,128)S(1)}, f32[256,512]{1,0:T(8,128)S(1)}, u32[]{:S(2)}, u32[]{:S(2)}) collective-permute-start(f32[256,512]{1,0:T(8,128)S(1)} %shard_map.44.far), channel_id=1, source_target_pairs={{0,4},{4,0},{8,12},{12,8},{16,20},{20,16},{24,28},{28,24},{1,5},{5... | collective-permute-start | bytes 1572872 | tf_op jit(solution)/shard_map/ppermute | solution.py:292
  28.3 13.0 %collective-permute-start.13 = (f32[448,128]{1,0:T(8,128)S(1)}, f32[448,128]{1,0:T(8,128)S(1)}, u32[]{:S(2)}, u32[]{:S(2)}) collective-permute-start(f32[448,128]{1,0:T(8,128)S(1)} %get-tuple-element.28), channel_id=1, source_target_pairs={{0,1},{1,3},{3,2},{2,0},{4,5},{5,7},{7,6},{6,4},{8,9},{9,11},{11,1... | collective-permute-start | bytes 688136 | tf_op jit(solution)/shard_map/ppermute | solution.py:274
  31.6 11.7 %collective-permute-start.11 = (f32[448,128]{1,0:T(8,128)S(1)}, f32[448,128]{1,0:T(8,128)S(1)}, u32[]{:S(2)}, u32[]{:S(2)}) collective-permute-start(f32[448,128]{1,0:T(8,128)S(1)} %get-tuple-element.26), channel_id=1, source_target_pairs={{0,3},{3,0},{4,7},{7,4},{8,11},{11,8},{12,15},{15,12},{16,19},{19,... | collective-permute-start | bytes 688136 | tf_op jit(solution)/shard_map/ppermute | solution.py:274
  32.3 13.8 %collective-permute-start.12 = (f32[448,128]{1,0:T(8,128)S(1)}, f32[448,128]{1,0:T(8,128)S(1)}, u32[]{:S(2)}, u32[]{:S(2)}) collective-permute-start(f32[448,128]{1,0:T(8,128)S(1)} %get-tuple-element.27), channel_id=1, source_target_pairs={{0,1},{1,0},{2,3},{3,2},{4,5},{5,4},{6,7},{7,6},{8,9},{9,8},{10,11... | collective-permute-start | bytes 688136 | tf_op jit(solution)/shard_map/ppermute | solution.py:274
  41.4 8.2 %collective-permute-start.14 = (f32[448,128]{1,0:T(8,128)S(1)}, f32[448,128]{1,0:T(8,128)S(1)}, u32[]{:S(2)}, u32[]{:S(2)}) collective-permute-start(f32[448,128]{1,0:T(8,128)S(1)} %add.3), channel_id=1, source_target_pairs={{1,2},{2,1},{5,6},{6,5},{9,10},{10,9},{13,14},{14,13},{17,18},{18,... | collective-permute-start | bytes 688136 | tf_op jit(solution)/shard_map/ppermute | solution.py:274

commit v6 on v5

--- a/solution.py
+++ b/solution.py
@@ -225,28 +225,43 @@
     return weight[...] * (0.5 - bit(turned_level).astype(f32))
 
 
-def first_block_kernel(turned_level, which_of, far, far_other, left, right, weight, cyclic, block, full, part):
+def first_block_kernel(turned_level, which_of, far, far_other, left, right, weight, half_way, block, full, columns):
     place(full, [far], [far_other])
-    cyclic[...] = product(left[...], product(full[...], right[...]))
-    rows = part.shape[0]
+    half_way[...] = product(full[...], right[...])
+    rows = columns.shape[0]
     which = which_of(lax.axis_index("ens"))
     at = pl.ds(pl.multiple_of(which * rows, LANES), rows)
-    part[...] = sign(turned_level, weight) * (cyclic[at, :] - cyclic[:, at].T)
-    lay_out(block, part, which, True)
-
-
-def blocks_kernel(turned_level, which_of, packed, cyclic, weight, *refs):
+    full[...] = product(left[...], half_way[...])
+    columns[...] = sign(turned_level, weight) * (full[at, :] - full[:, at].T)
+    lay_out(block, columns, which, True)
+
+
+def blocks_kernel(turned_level, which_of, packed, half_way, left, weight, *refs):
     blocks, terms = refs[:-1], refs[-1]
-    terms[...] = sign(turned_level, weight) * (cyclic[...] - cyclic[...].T)
+    cyclic = product(left[...], half_way[...])
+    terms[...] = sign(turned_level, weight) * (cyclic - cyclic.T)
     rows = terms.shape[0] // lax.axis_size("ens")
     here = lax.axis_index("ens")
     for which, block in zip(which_of(here), blocks):
         lay_out(block, terms.at[pl.ds(pl.multiple_of(which * rows, 8), rows), :], which, packed)
 
 
-def cyclic_kernel(far, far_other, left, right, cyclic, full):
+def skew_block(turned_level, which, half_way, left, weight, block, columns):
+    rows = columns.shape[0]
+    at = pl.ds(pl.multiple_of(which * rows, LANES), rows)
+    across = product(left[...], half_way[:, at]).T
+    columns[...] = sign(turned_level, weight) * (product(left[at, :], half_way[...]) - across)
+    lay_out(block, columns, which, True)
+
+
+def later_blocks_kernel(turned_level, which_of, half_way, left, weight, own, *refs):
+    blocks_kernel(turned_level, which_of, True, half_way, left, weight, *refs[:-1])
+    skew_block(turned_level, lax.axis_index("ens"), half_way, left, weight, own, refs[-1])
+
+
+def half_way_kernel(far, far_other, right, half_way, full):
     place(full, [far], [far_other])
-    cyclic[...] = product(left[...], product(full[...], right[...]))
+    half_way[...] = product(full[...], right[...])
 
 
 def sum_kernel(rows, packed, *refs):
@@ -314,19 +329,19 @@
     block = (rows * spread - packed * rows // 2, LANES)
     factors = (far, swap(far, 0), left, right, weights.reshape(1, 1))
     if members == 4 and packed:
-        cyclic, over_two = call(
+        half_way, over_two = call(
             functools.partial(first_block_kernel, top - 1, lambda here: here ^ 2), [square, block], *factors,
             scratch=[square, (rows, order)])
         blocks = call(
-            functools.partial(blocks_kernel, top - 1, lambda here: (here, here ^ 1, here ^ 3), packed), [block] * 3,
-            cyclic, factors[-1], scratch=[square])
+            functools.partial(later_blocks_kernel, top - 1, lambda here: (here ^ 1, here ^ 3)), [block] * 3,
+            half_way, left, factors[-1], scratch=[square, (rows, order)])
         blocks = [blocks[0], blocks[1], over_two, blocks[2]]
     else:
         order_of = (lambda here: [here ^ s for s in range(members)]) if members == 4 else (
             lambda here: [lax.rem(here + s, members) for s in range(members)])
-        cyclic = call(cyclic_kernel, [square], *factors[:4], scratch=[square])[0]
+        half_way = call(half_way_kernel, [square], *factors[:2], right, scratch=[square])[0]
         blocks = call(
-            functools.partial(blocks_kernel, top - 1, order_of, packed), [block] * members, cyclic, factors[-1],
+            functools.partial(blocks_kernel, top - 1, order_of, packed), [block] * members, half_way, left, factors[-1],
             scratch=[square])
     arrived = send_rows(blocks)
     total = call(

time: 50.6 us -> 50.4 us (level)
  the two profiles are of different devices: /device:TPU:14 before, /device:TPU:0 now
where the time goes in v6:
time: 50.4 us; the launch traced here: 50.3 us
  starting transfers between devices  20.9 us (41%)
  waiting for transfers between devices  16.4 us (33%)
  Pallas kernels  10.9 us (22%)
  local copies, waits for them, and re-layouts  1.23 us (2%)
  between operations  0.79 us (2%)
    ppermute x11, starting transfers between devices, swap(): return lax.ppermute(x, 'tm', [(i, i ^ 1 << level) for i in range(slices)])  13.6 us
    ppermute x4, waiting for transfers between devices, move(): return lax.ppermute(x, 'ens', pairs)  11 us
    pallas_call x13, Pallas kernels, call(): pl.pallas_call(kernel, out_shape=[jax.ShapeDtypeStruct(s, f32) for s in o...  10.9 us
    ppermute x4, starting transfers between devices, move(): return lax.ppermute(x, 'ens', pairs)  7.28 us
    ppermute x11, waiting for transfers between devices, swap(): return lax.ppermute(x, 'tm', [(i, i ^ 1 << level) for i in range(slices)])  5.38 us
    unnamed x4, local copies, waits for them, and re-layouts  1.23 us
  transfers between devices with their start and end apart: 15, of which 9 were waited for; matrix products, arithmetic and copies ran while one was open for 0% of the time, Pallas kernels for 14%

profile of v6, /device:TPU:0, one launch (start us, length us, event | category | flops | bytes accessed | tf_op | source)
XLA Modules:
  0.0 50.3 jit_solution(142602326770638216)
XLA Ops:
  0.0 0.5 collective-permute-start
  0.5 0.0 copy-start.1
  0.5 1.2 %copy-done.1 = f32[1,1,512,512]{3,2,1,0:T(8,128)S(1)} copy-done((f32[1,1,512,512]{3,2,1,0:T(8,128)S(1)}, f32[1,1,512,512]{3,2,1,0:T(8,128)}, u32[]{:S(2)}) %copy-start.1) | copy-done | bytes 1048600
  1.7 0.1 shard_map.37.mine
  1.8 0.0 copy-start
  1.8 1.2 %collective-permute-done.other = f32[512,512]{1,0:T(8,128)S(1)} collective-permute-done((f32[512,512]{1,0:T(8,128)}, f32[512,512]{1,0:T(8,128)S(1)}, u32[]{:S(2)}, u32[]{:S(2)}) %collective-permute-start) | collective-permute-done | bytes 1048608 | tf_op jit(solution)/shard_map/ppermute | solution.py:307
  3.0 0.7 %shard_map.38 = (f32[64,512]{1,0:T(8,128)S(1)}, f32[64,512]{1,0:T(8,128)S(1)}, f32[64,512]{1,0:T(8,128)S(1)}, f32[64,512]{1,0:T(8,128)S(1)}) custom-call(f32[512,512]{1,0:T(8,128)S(1)} %shard_map.37.mine, f32[512,512]{1,0:T(8,128)S(1)} %collective-permute-done.other), custom_call_target="tpu_custom_call" | custom-call | tf_op jit(solution)/shard_map/pallas_call | solution.py:32
  3.6 2.9 %collective-permute-start.1 = (f32[64,512]{1,0:T(8,128)S(1)}, f32[64,512]{1,0:T(8,128)S(1)}, u32[]{:S(2)}, u32[]{:S(2)}) collective-permute-start(f32[64,512]{1,0:T(8,128)S(1)} %get-tuple-element.17), channel_id=1, source_target_pairs={{0,8},{4,12},{8,0},{12,4},{16,24},{20,28},{24,16},{28,20},{1,9},{5... | collective-permute-start | bytes 393224 | tf_op jit(solution)/shard_map/ppermute | solution.py:307
  6.5 0.1 collective-permute-start.3
  6.6 1.9 %collective-permute-start.5 = (f32[64,512]{1,0:T(8,128)S(1)}, f32[64,512]{1,0:T(8,128)S(1)}, u32[]{:S(2)}, u32[]{:S(2)}) collective-permute-start(f32[64,512]{1,0:T(8,128)S(1)} %get-tuple-element.20), channel_id=1, source_target_pairs={{0,8},{4,12},{8,0},{12,4},{16,24},{20,28},{24,16},{28,20},{1,9},{5... | collective-permute-start | bytes 393224 | tf_op jit(solution)/shard_map/ppermute | solution.py:307
  8.5 0.1 collective-permute-start.7
  8.6 0.0 copy-done
  8.6 2.3 %shard_map.39 = (f32[512,512]{1,0:T(8,128)S(1)}, f32[512,512]{1,0:T(8,128)S(1)}, f32[512,512]{1,0:T(8,128)S(1)}) custom-call(f32[512,512]{1,0:T(8,128)S(1)} %shard_map.37.mine, f32[512,512]{1,0:T(8,128)S(1)} %collective-permute-done.other, f32[512,512]{1,0:T(8,128)S(1)} %copy-done), custom_call_target="tpu_custom_call" | custom-call | tf_op jit(solution)/shard_map/pallas_call | solution.py:32
  10.9 0.0 collective-permute-done.1.got.refs_0_
  11.0 0.4 shard_map.40
  11.4 2.0 %collective-permute-start.2 = (f32[64,512]{1,0:T(8,128)S(1)}, f32[64,512]{1,0:T(8,128)S(1)}, u32[]{:S(2)}, u32[]{:S(2)}) collective-permute-start(f32[64,512]{1,0:T(8,128)S(1)} %shard_map.40), channel_id=1, source_target_pairs={{0,16},{4,20},{8,24},{12,28},{16,0},{20,4},{24,8},{28,12},{1,17},{... | collective-permute-start | bytes 393224 | tf_op jit(solution)/shard_map/ppermute | solution.py:307
  13.4 0.2 collective-permute-done.3.got.refs_1_
  13.6 0.4 shard_map.41
  14.0 2.2 %collective-permute-start.4 = (f32[64,512]{1,0:T(8,128)S(1)}, f32[64,512]{1,0:T(8,128)S(1)}, u32[]{:S(2)}, u32[]{:S(2)}) collective-permute-start(f32[64,512]{1,0:T(8,128)S(1)} %shard_map.41), channel_id=1, source_target_pairs={{0,16},{4,20},{8,24},{12,28},{16,0},{20,4},{24,8},{28,12},{1,17},{... | collective-permute-start | bytes 393224 | tf_op jit(solution)/shard_map/ppermute | solution.py:307
  16.2 0.2 collective-permute-done.5.got.refs_2_
  16.4 0.4 shard_map.42
  16.8 2.2 %collective-permute-start.6 = (f32[64,512]{1,0:T(8,128)S(1)}, f32[64,512]{1,0:T(8,128)S(1)}, u32[]{:S(2)}, u32[]{:S(2)}) collective-permute-start(f32[64,512]{1,0:T(8,128)S(1)} %shard_map.42), channel_id=1, source_target_pairs={{0,16},{4,20},{8,24},{12,28},{16,0},{20,4},{24,8},{28,12},{1,17},{... | collective-permute-start | bytes 393224 | tf_op jit(solution)/shard_map/ppermute | solution.py:307
  19.0 0.0 collective-permute-done.7.got.refs_3_
  19.0 0.4 shard_map.43
  19.5 1.6 %collective-permute-start.8 = (f32[64,512]{1,0:T(8,128)S(1)}, f32[64,512]{1,0:T(8,128)S(1)}, u32[]{:S(2)}, u32[]{:S(2)}) collective-permute-start(f32[64,512]{1,0:T(8,128)S(1)} %shard_map.43), channel_id=1, source_target_pairs={{0,16},{4,20},{8,24},{12,28},{16,0},{20,4},{24,8},{28,12},{1,17},{... | collective-permute-start | bytes 393224 | tf_op jit(solution)/shard_map/ppermute | solution.py:307
  21.1 0.1 collective-permute-start.10
  21.2 0.0 collective-permute-done.2.refs_0_
  21.2 0.0 collective-permute-done.4.refs_1_
  21.2 1.5 %collective-permute-done.6.refs_2_ = f32[64,512]{1,0:T(8,128)S(1)} collective-permute-done((f32[64,512]{1,0:T(8,128)S(1)}, f32[64,512]{1,0:T(8,128)S(1)}, u32[]{:S(2)}, u32[]{:S(2)}) %collective-permute-start.6) | collective-permute-done | bytes 131104 | tf_op jit(solution)/shard_map/ppermute | solution.py:307
  22.7 2.1 %collective-permute-done.8.refs_3_ = f32[64,512]{1,0:T(8,128)S(1)} collective-permute-done((f32[64,512]{1,0:T(8,128)S(1)}, f32[64,512]{1,0:T(8,128)S(1)}, u32[]{:S(2)}, u32[]{:S(2)}) %collective-permute-start.8) | collective-permute-done | bytes 131104 | tf_op jit(solution)/shard_map/ppermute | solution.py:307
  24.9 0.1 collective-permute-start.9
  25.6 0.0 collective-permute-done.10.near_other
  25.6 1.0 %shard_map.46.right = f32[512,512]{1,0:T(8,128)S(1)} custom-call(f32[256,512]{1,0:T(8,128)S(1)} %shard_map.45.near, f32[256,512]{1,0:T(8,128)S(1)} %collective-permute-done.10.near_other, f32[512,512]{1,0:T(8,128)S(1)} %get-tuple-element.23.right), custom_call_target="tpu_custom_call" | custom-call | tf_op jit(solution)/shard_map/pallas_call | solution.py:32
  26.7 0.2 collective-permute-done.9.far_other
  26.9 2.2 %shard_map.47 = (f32[512,512]{1,0:T(8,128)S(1)}, f32[448,128]{1,0:T(8,128)S(1)}) custom-call(f32[256,512]{1,0:T(8,128)S(1)} %shard_map.44.far, f32[256,512]{1,0:T(8,128)S(1)} %collective-permute-done.9.far_other, f32[512,512]{1,0:T(8,128)S(1)} %get-tuple-element.22.left, f32[512,512]{1,0:T(8,128)S(1)} %shard_map.46.right, f32[1,1]{1,0:T(1,128)} %bitcast.3.weight), custom_call_target="tpu_custom_call" | custom-call | tf_op jit(solution)/shard_map/pallas_call | solution.py:32
  29.1 2.2 %collective-permute-start.13 = (f32[448,128]{1,0:T(8,128)S(1)}, f32[448,128]{1,0:T(8,128)S(1)}, u32[]{:S(2)}, u32[]{:S(2)}) collective-permute-start(f32[448,128]{1,0:T(8,128)S(1)} %get-tuple-element.28), channel_id=1, source_target_pairs={{0,1},{1,3},{3,2},{2,0},{4,5},{5,7},{7,6},{6,4},{8,9},{9,11},{11,1... | collective-permute-start | bytes 688136 | tf_op jit(solution)/shard_map/ppermute | solution.py:289
  31.3 1.9 %shard_map.48 = (f32[448,128]{1,0:T(8,128)S(1)}, f32[448,128]{1,0:T(8,128)S(1)}, f32[448,128]{1,0:T(8,128)S(1)}) custom-call(f32[512,512]{1,0:T(8,128)S(1)} %get-tuple-element.24.half_way, f32[512,512]{1,0:T(8,128)S(1)} %get-tuple-element.22.left, f32[1,1]{1,0:T(1,128)} %bitcast.4.weight), custom_call_target="tpu_custom_call" | custom-call | tf_op jit(solution)/shard_map/pallas_call | solution.py:32
  33.2 4.4 %collective-permute-start.11 = (f32[448,128]{1,0:T(8,128)S(1)}, f32[448,128]{1,0:T(8,128)S(1)}, u32[]{:S(2)}, u32[]{:S(2)}) collective-permute-start(f32[448,128]{1,0:T(8,128)S(1)} %get-tuple-element.26), channel_id=1, source_target_pairs={{0,3},{3,0},{4,7},{7,4},{8,11},{11,8},{12,15},{15,12},{16,19},{19,... | collective-permute-start | bytes 688136 | tf_op jit(solution)/shard_map/ppermute | solution.py:289
  37.6 0.1 collective-permute-start.12
  37.7 0.7 %collective-permute-done.13.refs_4_ = f32[448,128]{1,0:T(8,128)S(1)} collective-permute-done((f32[448,128]{1,0:T(8,128)S(1)}, f32[448,128]{1,0:T(8,128)S(1)}, u32[]{:S(2)}, u32[]{:S(2)}) %collective-permute-start.13) | collective-permute-done | bytes 229408 | tf_op jit(solution)/shard_map/ppermute | solution.py:289
  38.4 0.7 %collective-permute-start.14 = (f32[448,128]{1,0:T(8,128)S(1)}, f32[448,128]{1,0:T(8,128)S(1)}, u32[]{:S(2)}, u32[]{:S(2)}) collective-permute-start(f32[448,128]{1,0:T(8,128)S(1)} %add.3), channel_id=1, source_target_pairs={{1,2},{2,1},{5,6},{6,5},{9,10},{10,9},{13,14},{14,13},{17,18},{18,... | collective-permute-start | bytes 688136 | tf_op jit(solution)/shard_map/ppermute | solution.py:289
  39.1 6.3 %collective-permute-done.11.refs_1_ = f32[448,128]{1,0:T(8,128)S(1)} collective-permute-done((f32[448,128]{1,0:T(8,128)S(1)}, f32[448,128]{1,0:T(8,128)S(1)}, u32[]{:S(2)}, u32[]{:S(2)}) %collective-permute-start.11) | collective-permute-done | bytes 229408 | tf_op jit(solution)/shard_map/ppermute | solution.py:289
  45.3 4.0 %collective-permute-done.12.refs_2_ = f32[448,128]{1,0:T(8,128)S(1)} collective-permute-done((f32[448,128]{1,0:T(8,128)S(1)}, f32[448,128]{1,0:T(8,128)S(1)}, u32[]{:S(2)}, u32[]{:S(2)}) %collective-permute-start.12) | collective-permute-done | bytes 229408 | tf_op jit(solution)/shard_map/ppermute | solution.py:289
  49.4 0.0 collective-permute-done.14.refs_3_
  49.4 0.9 %shard_map.49 = f32[512,128]{1,0:T(8,128)} custom-call(f32[448,128]{1,0:T(8,128)S(1)} %get-tuple-element.25.refs_0_, f32[448,128]{1,0:T(8,128)S(1)} %collective-permute-done.11.refs_1_, f32[448,128]{1,0:T(8,128)S(1)} %collective-permute-done.12.refs_2_, f32[448,128]{1,0:T(8,128)S(1)} %collective-permute-done.14.refs_3_, ...), custom_call_target="tpu_custom_call" | custom-call | tf_op jit(solution)/shard_map/pallas_call | solution.py:32
  (3 shorter events, 0.1 us)
Async XLA Ops:
  0.0 3.0 %collective-permute-start = (f32[512,512]{1,0:T(8,128)}, f32[512,512]{1,0:T(8,128)S(1)}, u32[]{:S(2)}, u32[]{:S(2)}) collective-permute-start(f32[512,512]{1,0:T(8,128)} %bitcast.5), channel_id=1, source_target_pairs={{0,4},{4,0},{8,12},{12,8},{16,20},{20,16},{24,28},{28,24},{1,5},{5... | collective-permute-start | bytes 3145736 | tf_op jit(solution)/shard_map/ppermute | solution.py:307
  0.5 1.2 %copy-start.1 = (f32[1,1,512,512]{3,2,1,0:T(8,128)S(1)}, f32[1,1,512,512]{3,2,1,0:T(8,128)}, u32[]{:S(2)}) copy-start(f32[1,1,512,512]{3,2,1,0:T(8,128)} %param.3) | copy-start | bytes 3145732
  1.8 6.8 %copy-start = (f32[512,512]{1,0:T(8,128)S(1)}, f32[512,512]{1,0:T(8,128)}, u32[]{:S(2)}) copy-start(f32[512,512]{1,0:T(8,128)} %target.1) | copy-start | bytes 3145732
  3.6 7.3 %collective-permute-start.1 = (f32[64,512]{1,0:T(8,128)S(1)}, f32[64,512]{1,0:T(8,128)S(1)}, u32[]{:S(2)}, u32[]{:S(2)}) collective-permute-start(f32[64,512]{1,0:T(8,128)S(1)} %get-tuple-element.17), channel_id=1, source_target_pairs={{0,8},{4,12},{8,0},{12,4},{16,24},{20,28},{24,16},{28,20},{1,9},{5... | collective-permute-start | bytes 393224 | tf_op jit(solution)/shard_map/ppermute | solution.py:307
  6.5 7.1 %collective-permute-start.3 = (f32[64,512]{1,0:T(8,128)S(1)}, f32[64,512]{1,0:T(8,128)S(1)}, u32[]{:S(2)}, u32[]{:S(2)}) collective-permute-start(f32[64,512]{1,0:T(8,128)S(1)} %get-tuple-element.19), channel_id=1, source_target_pairs={{0,8},{4,12},{8,0},{12,4},{16,24},{20,28},{24,16},{28,20},{1,9},{5... | collective-permute-start | bytes 393224 | tf_op jit(solution)/shard_map/ppermute | solution.py:307
  6.6 9.8 %collective-permute-start.5 = (f32[64,512]{1,0:T(8,128)S(1)}, f32[64,512]{1,0:T(8,128)S(1)}, u32[]{:S(2)}, u32[]{:S(2)}) collective-permute-start(f32[64,512]{1,0:T(8,128)S(1)} %get-tuple-element.20), channel_id=1, source_target_pairs={{0,8},{4,12},{8,0},{12,4},{16,24},{20,28},{24,16},{28,20},{1,9},{5... | collective-permute-start | bytes 393224 | tf_op jit(solution)/shard_map/ppermute | solution.py:307
  8.5 10.5 %collective-permute-start.7 = (f32[64,512]{1,0:T(8,128)S(1)}, f32[64,512]{1,0:T(8,128)S(1)}, u32[]{:S(2)}, u32[]{:S(2)}) collective-permute-start(f32[64,512]{1,0:T(8,128)S(1)} %get-tuple-element.21), channel_id=1, source_target_pairs={{0,8},{4,12},{8,0},{12,4},{16,24},{20,28},{24,16},{28,20},{1,9},{5... | collective-permute-start | bytes 393224 | tf_op jit(solution)/shard_map/ppermute | solution.py:307
  11.4 9.8 %collective-permute-start.2 = (f32[64,512]{1,0:T(8,128)S(1)}, f32[64,512]{1,0:T(8,128)S(1)}, u32[]{:S(2)}, u32[]{:S(2)}) collective-permute-start(f32[64,512]{1,0:T(8,128)S(1)} %shard_map.40), channel_id=1, source_target_pairs={{0,16},{4,20},{8,24},{12,28},{16,0},{20,4},{24,8},{28,12},{1,17},{... | collective-permute-start | bytes 393224 | tf_op jit(solution)/shard_map/ppermute | solution.py:307
  14.0 7.2 %collective-permute-start.4 = (f32[64,512]{1,0:T(8,128)S(1)}, f32[64,512]{1,0:T(8,128)S(1)}, u32[]{:S(2)}, u32[]{:S(2)}) collective-permute-start(f32[64,512]{1,0:T(8,128)S(1)} %shard_map.41), channel_id=1, source_target_pairs={{0,16},{4,20},{8,24},{12,28},{16,0},{20,4},{24,8},{28,12},{1,17},{... | collective-permute-start | bytes 393224 | tf_op jit(solution)/shard_map/ppermute | solution.py:307
  16.8 5.9 %collective-permute-start.6 = (f32[64,512]{1,0:T(8,128)S(1)}, f32[64,512]{1,0:T(8,128)S(1)}, u32[]{:S(2)}, u32[]{:S(2)}) collective-permute-start(f32[64,512]{1,0:T(8,128)S(1)} %shard_map.42), channel_id=1, source_target_pairs={{0,16},{4,20},{8,24},{12,28},{16,0},{20,4},{24,8},{28,12},{1,17},{... | collective-permute-start | bytes 393224 | tf_op jit(solution)/shard_map/ppermute | solution.py:307
  19.5 5.4 %collective-permute-start.8 = (f32[64,512]{1,0:T(8,128)S(1)}, f32[64,512]{1,0:T(8,128)S(1)}, u32[]{:S(2)}, u32[]{:S(2)}) collective-permute-start(f32[64,512]{1,0:T(8,128)S(1)} %shard_map.43), channel_id=1, source_target_pairs={{0,16},{4,20},{8,24},{12,28},{16,0},{20,4},{24,8},{28,12},{1,17},{... | collective-permute-start | bytes 393224 | tf_op jit(solution)/shard_map/ppermute | solution.py:307
  21.1 4.5 %collective-permute-start.10 = (f32[256,512]{1,0:T(8,128)S(1)}, f32[256,512]{1,0:T(8,128)S(1)}, u32[]{:S(2)}, u32[]{:S(2)}) collective-permute-start(f32[256,512]{1,0:T(8,128)S(1)} %shard_map.45.near), channel_id=1, source_target_pairs={{0,4},{4,0},{8,12},{12,8},{16,20},{20,16},{24,28},{28,24},{1,5},{5... | collective-permute-start | bytes 1572872 | tf_op jit(solution)/shard_map/ppermute | solution.py:307
  24.9 2.0 %collective-permute-start.9 = (f32[256,512]{1,0:T(8,128)S(1)}, f32[256,512]{1,0:T(8,128)S(1)}, u32[]{:S(2)}, u32[]{:S(2)}) collective-permute-start(f32[256,512]{1,0:T(8,128)S(1)} %shard_map.44.far), channel_id=1, source_target_pairs={{0,4},{4,0},{8,12},{12,8},{16,20},{20,16},{24,28},{28,24},{1,5},{5... | collective-permute-start | bytes 1572872 | tf_op jit(solution)/shard_map/ppermute | solution.py:307
  29.1 9.3 %collective-permute-start.13 = (f32[448,128]{1,0:T(8,128)S(1)}, f32[448,128]{1,0:T(8,128)S(1)}, u32[]{:S(2)}, u32[]{:S(2)}) collective-permute-start(f32[448,128]{1,0:T(8,128)S(1)} %get-tuple-element.28), channel_id=1, source_target_pairs={{0,1},{1,3},{3,2},{2,0},{4,5},{5,7},{7,6},{6,4},{8,9},{9,11},{11,1... | collective-permute-start | bytes 688136 | tf_op jit(solution)/shard_map/ppermute | solution.py:289
  33.2 12.2 %collective-permute-start.11 = (f32[448,128]{1,0:T(8,128)S(1)}, f32[448,128]{1,0:T(8,128)S(1)}, u32[]{:S(2)}, u32[]{:S(2)}) collective-permute-start(f32[448,128]{1,0:T(8,128)S(1)} %get-tuple-element.26), channel_id=1, source_target_pairs={{0,3},{3,0},{4,7},{7,4},{8,11},{11,8},{12,15},{15,12},{16,19},{19,... | collective-permute-start | bytes 688136 | tf_op jit(solution)/shard_map/ppermute | solution.py:289
  37.6 11.8 %collective-permute-start.12 = (f32[448,128]{1,0:T(8,128)S(1)}, f32[448,128]{1,0:T(8,128)S(1)}, u32[]{:S(2)}, u32[]{:S(2)}) collective-permute-start(f32[448,128]{1,0:T(8,128)S(1)} %get-tuple-element.27), channel_id=1, source_target_pairs={{0,1},{1,0},{2,3},{3,2},{4,5},{5,4},{6,7},{7,6},{8,9},{9,8},{10,11... | collective-permute-start | bytes 688136 | tf_op jit(solution)/shard_map/ppermute | solution.py:289
  38.4 11.0 %collective-permute-start.14 = (f32[448,128]{1,0:T(8,128)S(1)}, f32[448,128]{1,0:T(8,128)S(1)}, u32[]{:S(2)}, u32[]{:S(2)}) collective-permute-start(f32[448,128]{1,0:T(8,128)S(1)} %add.3), channel_id=1, source_target_pairs={{1,2},{2,1},{5,6},{6,5},{9,10},{10,9},{13,14},{14,13},{17,18},{18,... | collective-permute-start | bytes 688136 | tf_op jit(solution)/shard_map/ppermute | solution.py:289

commit v7 on v6

--- a/solution.py
+++ b/solution.py
@@ -18,7 +18,11 @@
 
 
 def product(a, b, b_turned=False):
-    (ah, al), (bh, bl) = split(a), split(b)
+    return product_of(split(a), split(b), b_turned)
+
+
+def product_of(a, b, b_turned=False):
+    (ah, al), (bh, bl) = a, b
     dims = (((1,), (1 if b_turned else 0,)), ((), ()))
     dot = functools.partial(lax.dot_general, dimension_numbers=dims, preferred_element_type=f32)
     return dot(ah, bh) + (dot(al, bh) + dot(ah, bl))
@@ -31,7 +35,7 @@
 def call(kernel, outs, *operands, scratch=()):
     return pl.pallas_call(
         kernel,
-        out_shape=[jax.ShapeDtypeStruct(s, f32) for s in outs],
+        out_shape=[jax.ShapeDtypeStruct(s, f32) if isinstance(s[0], int) else jax.ShapeDtypeStruct(*s) for s in outs],
         in_specs=[pl.BlockSpec(memory_space=pltpu.VMEM)] * len(operands),
         out_specs=[pl.BlockSpec(memory_space=pltpu.VMEM)] * len(outs),
         scratch_shapes=[pltpu.VMEM(s, f32) for s in scratch],
@@ -181,9 +185,9 @@
         at += piece.shape[0]
 
 
-def factor_kernel(near, near_other, right, out, full):
+def factor_kernel(near, near_other, right, high, low, full):
     place(full, [near], [near_other])
-    out[...] = product(full[...], right[...])
+    high[...], low[...] = split(product(full[...], right[...]))
 
 
 def corner(rows):
@@ -225,9 +229,9 @@
     return weight[...] * (0.5 - bit(turned_level).astype(f32))
 
 
-def first_block_kernel(turned_level, which_of, far, far_other, left, right, weight, half_way, block, full, columns):
+def first_block_kernel(turned_level, which_of, far, far_other, left, right_high, right_low, weight, half_way, block, full, columns):
     place(full, [far], [far_other])
-    half_way[...] = product(full[...], right[...])
+    half_way[...] = product_of(split(full[...]), (right_high[...], right_low[...]))
     rows = columns.shape[0]
     which = which_of(lax.axis_index("ens"))
     at = pl.ds(pl.multiple_of(which * rows, LANES), rows)
@@ -259,9 +263,9 @@
     skew_block(turned_level, lax.axis_index("ens"), half_way, left, weight, own, refs[-1])
 
 
-def half_way_kernel(far, far_other, right, half_way, full):
+def half_way_kernel(far, far_other, right_high, right_low, half_way, full):
     place(full, [far], [far_other])
-    half_way[...] = product(full[...], right[...])
+    half_way[...] = product_of(split(full[...]), (right_high[...], right_low[...]))
 
 
 def sum_kernel(rows, packed, *refs):
@@ -322,12 +326,12 @@
             (own, left, right), sends = outs[:3], outs[3:]
     far = [swap(p, top) for p in products]
     near = call(join_kernel, [(order // 2, order)], *got)[0]
-    right = call(factor_kernel, [square], near, swap(near, 0), right, scratch=[square])[0]
+    right = call(factor_kernel, [(square, bf16)] * 2, near, swap(near, 0), right, scratch=[square])
     far = call(join_kernel, [(order // 2, order)], *far)[0]
     rows, spread = order // members, order // LANES
     packed = rows == LANES
     block = (rows * spread - packed * rows // 2, LANES)
-    factors = (far, swap(far, 0), left, right, weights.reshape(1, 1))
+    factors = (far, swap(far, 0), left, *right, weights.reshape(1, 1))
     if members == 4 and packed:
         half_way, over_two = call(
             functools.partial(first_block_kernel, top - 1, lambda here: here ^ 2), [square, block], *factors,
@@ -339,7 +343,7 @@
     else:
         order_of = (lambda here: [here ^ s for s in range(members)]) if members == 4 else (
             lambda here: [lax.rem(here + s, members) for s in range(members)])
-        half_way = call(half_way_kernel, [square], *factors[:2], right, scratch=[square])[0]
+        half_way = call(half_way_kernel, [square], *factors[:2], *right, scratch=[square])[0]
         blocks = call(
             functools.partial(blocks_kernel, top - 1, order_of, packed), [block] * members, half_way, left, factors[-1],
             scratch=[square])

time: 50.4 us -> 50.4 us (level)
  no operation moved by 1% of the time
where the time goes in v7:
time: 50.4 us; the launch traced here: 50.2 us
  starting transfers between devices  20.9 us (41%)
  waiting for transfers between devices  16.4 us (33%)
  Pallas kernels  10.9 us (22%)
  local copies, waits for them, and re-layouts  1.23 us (2%)
  between operations  0.8 us (2%)
    ppermute x11, starting transfers between devices, swap(): return lax.ppermute(x, 'tm', [(i, i ^ 1 << level) for i in range(slices)])  13.6 us
    ppermute x4, waiting for transfers between devices, move(): return lax.ppermute(x, 'ens', pairs)  11 us
    pallas_call x13, Pallas kernels, call(): pl.pallas_call(kernel, out_shape=[jax.ShapeDtypeStruct(s, f32) if isinsta...  10.9 us
    ppermute x4, starting transfers between devices, move(): return lax.ppermute(x, 'ens', pairs)  7.29 us
    ppermute x11, waiting for transfers between devices, swap(): return lax.ppermute(x, 'tm', [(i, i ^ 1 << level) for i in range(slices)])  5.37 us
    unnamed x4, local copies, waits for them, and re-layouts  1.23 us
  transfers between devices with their start and end apart: 15, of which 9 were waited for; matrix products, arithmetic and copies ran while one was open for 0% of the time, Pallas kernels for 14%

profile of v7, /device:TPU:0, one launch (start us, length us, event | category | flops | bytes accessed | tf_op | source)
XLA Modules:
  0.0 50.2 jit_solution(16179421759507816709)
XLA Ops:
  0.0 0.5 collective-permute-start
  0.5 0.0 copy-start.1
  0.5 1.2 %copy-done.1 = f32[1,1,512,512]{3,2,1,0:T(8,128)S(1)} copy-done((f32[1,1,512,512]{3,2,1,0:T(8,128)S(1)}, f32[1,1,512,512]{3,2,1,0:T(8,128)}, u32[]{:S(2)}) %copy-start.1) | copy-done | bytes 1048600
  1.7 0.1 shard_map.37.mine
  1.8 0.0 copy-start
  1.8 1.2 %collective-permute-done.other = f32[512,512]{1,0:T(8,128)S(1)} collective-permute-done((f32[512,512]{1,0:T(8,128)}, f32[512,512]{1,0:T(8,128)S(1)}, u32[]{:S(2)}, u32[]{:S(2)}) %collective-permute-start) | collective-permute-done | bytes 1048608 | tf_op jit(solution)/shard_map/ppermute | solution.py:311
  3.0 0.7 %shard_map.38 = (f32[64,512]{1,0:T(8,128)S(1)}, f32[64,512]{1,0:T(8,128)S(1)}, f32[64,512]{1,0:T(8,128)S(1)}, f32[64,512]{1,0:T(8,128)S(1)}) custom-call(f32[512,512]{1,0:T(8,128)S(1)} %shard_map.37.mine, f32[512,512]{1,0:T(8,128)S(1)} %collective-permute-done.other), custom_call_target="tpu_custom_call" | custom-call | tf_op jit(solution)/shard_map/pallas_call | solution.py:36
  3.6 2.9 %collective-permute-start.1 = (f32[64,512]{1,0:T(8,128)S(1)}, f32[64,512]{1,0:T(8,128)S(1)}, u32[]{:S(2)}, u32[]{:S(2)}) collective-permute-start(f32[64,512]{1,0:T(8,128)S(1)} %get-tuple-element.19), channel_id=1, source_target_pairs={{0,8},{4,12},{8,0},{12,4},{16,24},{20,28},{24,16},{28,20},{1,9},{5... | collective-permute-start | bytes 393224 | tf_op jit(solution)/shard_map/ppermute | solution.py:311
  6.5 0.1 collective-permute-start.3
  6.6 1.9 %collective-permute-start.5 = (f32[64,512]{1,0:T(8,128)S(1)}, f32[64,512]{1,0:T(8,128)S(1)}, u32[]{:S(2)}, u32[]{:S(2)}) collective-permute-start(f32[64,512]{1,0:T(8,128)S(1)} %get-tuple-element.22), channel_id=1, source_target_pairs={{0,8},{4,12},{8,0},{12,4},{16,24},{20,28},{24,16},{28,20},{1,9},{5... | collective-permute-start | bytes 393224 | tf_op jit(solution)/shard_map/ppermute | solution.py:311
  8.5 0.1 collective-permute-start.7
  8.6 0.0 copy-done
  8.6 2.3 %shard_map.39 = (f32[512,512]{1,0:T(8,128)S(1)}, f32[512,512]{1,0:T(8,128)S(1)}, f32[512,512]{1,0:T(8,128)S(1)}) custom-call(f32[512,512]{1,0:T(8,128)S(1)} %shard_map.37.mine, f32[512,512]{1,0:T(8,128)S(1)} %collective-permute-done.other, f32[512,512]{1,0:T(8,128)S(1)} %copy-done), custom_call_target="tpu_custom_call" | custom-call | tf_op jit(solution)/shard_map/pallas_call | solution.py:36
  10.9 0.0 collective-permute-done.1.got.refs_0_
  11.0 0.4 shard_map.40
  11.4 2.0 %collective-permute-start.2 = (f32[64,512]{1,0:T(8,128)S(1)}, f32[64,512]{1,0:T(8,128)S(1)}, u32[]{:S(2)}, u32[]{:S(2)}) collective-permute-start(f32[64,512]{1,0:T(8,128)S(1)} %shard_map.40), channel_id=1, source_target_pairs={{0,16},{4,20},{8,24},{12,28},{16,0},{20,4},{24,8},{28,12},{1,17},{... | collective-permute-start | bytes 393224 | tf_op jit(solution)/shard_map/ppermute | solution.py:311
  13.4 0.2 collective-permute-done.3.got.refs_1_
  13.6 0.4 shard_map.41
  14.0 2.2 %collective-permute-start.4 = (f32[64,512]{1,0:T(8,128)S(1)}, f32[64,512]{1,0:T(8,128)S(1)}, u32[]{:S(2)}, u32[]{:S(2)}) collective-permute-start(f32[64,512]{1,0:T(8,128)S(1)} %shard_map.41), channel_id=1, source_target_pairs={{0,16},{4,20},{8,24},{12,28},{16,0},{20,4},{24,8},{28,12},{1,17},{... | collective-permute-start | bytes 393224 | tf_op jit(solution)/shard_map/ppermute | solution.py:311
  16.2 0.2 collective-permute-done.5.got.refs_2_
  16.4 0.4 shard_map.42
  16.8 2.2 %collective-permute-start.6 = (f32[64,512]{1,0:T(8,128)S(1)}, f32[64,512]{1,0:T(8,128)S(1)}, u32[]{:S(2)}, u32[]{:S(2)}) collective-permute-start(f32[64,512]{1,0:T(8,128)S(1)} %shard_map.42), channel_id=1, source_target_pairs={{0,16},{4,20},{8,24},{12,28},{16,0},{20,4},{24,8},{28,12},{1,17},{... | collective-permute-start | bytes 393224 | tf_op jit(solution)/shard_map/ppermute | solution.py:311
  19.0 0.0 collective-permute-done.7.got.refs_3_
  19.0 0.4 shard_map.43
  19.5 1.6 %collective-permute-start.8 = (f32[64,512]{1,0:T(8,128)S(1)}, f32[64,512]{1,0:T(8,128)S(1)}, u32[]{:S(2)}, u32[]{:S(2)}) collective-permute-start(f32[64,512]{1,0:T(8,128)S(1)} %shard_map.43), channel_id=1, source_target_pairs={{0,16},{4,20},{8,24},{12,28},{16,0},{20,4},{24,8},{28,12},{1,17},{... | collective-permute-start | bytes 393224 | tf_op jit(solution)/shard_map/ppermute | solution.py:311
  21.1 0.1 collective-permute-start.10
  21.2 0.0 collective-permute-done.2.refs_0_
  21.2 0.0 collective-permute-done.4.refs_1_
  21.2 1.5 %collective-permute-done.6.refs_2_ = f32[64,512]{1,0:T(8,128)S(1)} collective-permute-done((f32[64,512]{1,0:T(8,128)S(1)}, f32[64,512]{1,0:T(8,128)S(1)}, u32[]{:S(2)}, u32[]{:S(2)}) %collective-permute-start.6) | collective-permute-done | bytes 131104 | tf_op jit(solution)/shard_map/ppermute | solution.py:311
  22.7 2.1 %collective-permute-done.8.refs_3_ = f32[64,512]{1,0:T(8,128)S(1)} collective-permute-done((f32[64,512]{1,0:T(8,128)S(1)}, f32[64,512]{1,0:T(8,128)S(1)}, u32[]{:S(2)}, u32[]{:S(2)}) %collective-permute-start.8) | collective-permute-done | bytes 131104 | tf_op jit(solution)/shard_map/ppermute | solution.py:311
  24.9 0.1 collective-permute-start.9
  25.6 0.0 collective-permute-done.10.near_other
  25.6 1.1 %shard_map.46 = (bf16[512,512]{1,0:T(8,128)(2,1)S(1)}, bf16[512,512]{1,0:T(8,128)(2,1)S(1)}) custom-call(f32[256,512]{1,0:T(8,128)S(1)} %shard_map.45.near, f32[256,512]{1,0:T(8,128)S(1)} %collective-permute-done.10.near_other, f32[512,512]{1,0:T(8,128)S(1)} %get-tuple-element.25.right), custom_call_target="tpu_custom_call" | custom-call | tf_op jit(solution)/shard_map/pallas_call | solution.py:36
  26.7 0.2 collective-permute-done.9.far_other
  26.9 2.2 %shard_map.47 = (f32[512,512]{1,0:T(8,128)S(1)}, f32[448,128]{1,0:T(8,128)S(1)}) custom-call(f32[256,512]{1,0:T(8,128)S(1)} %shard_map.44.far, f32[256,512]{1,0:T(8,128)S(1)} %collective-permute-done.9.far_other, f32[512,512]{1,0:T(8,128)S(1)} %get-tuple-element.24.left, bf16[512,512]{1,0:T(8,128)(2,1)S(1)} %get-tuple-element.26.right_high, ...), custom_call_target="tpu_custom_call" | custom-call | tf_op jit(solution)/shard_map/pallas_call | solution.py:36
  29.1 2.2 %collective-permute-start.13 = (f32[448,128]{1,0:T(8,128)S(1)}, f32[448,128]{1,0:T(8,128)S(1)}, u32[]{:S(2)}, u32[]{:S(2)}) collective-permute-start(f32[448,128]{1,0:T(8,128)S(1)} %get-tuple-element.32), channel_id=1, source_target_pairs={{0,1},{1,3},{3,2},{2,0},{4,5},{5,7},{7,6},{6,4},{8,9},{9,11},{11,1... | collective-permute-start | bytes 688136 | tf_op jit(solution)/shard_map/ppermute | solution.py:293
  31.2 1.9 %shard_map.48 = (f32[448,128]{1,0:T(8,128)S(1)}, f32[448,128]{1,0:T(8,128)S(1)}, f32[448,128]{1,0:T(8,128)S(1)}) custom-call(f32[512,512]{1,0:T(8,128)S(1)} %get-tuple-element.28.half_way, f32[512,512]{1,0:T(8,128)S(1)} %get-tuple-element.24.left, f32[1,1]{1,0:T(1,128)} %bitcast.4.weight), custom_call_target="tpu_custom_call" | custom-call | tf_op jit(solution)/shard_map/pallas_call | solution.py:36
  33.1 4.4 %collective-permute-start.11 = (f32[448,128]{1,0:T(8,128)S(1)}, f32[448,128]{1,0:T(8,128)S(1)}, u32[]{:S(2)}, u32[]{:S(2)}) collective-permute-start(f32[448,128]{1,0:T(8,128)S(1)} %get-tuple-element.30), channel_id=1, source_target_pairs={{0,3},{3,0},{4,7},{7,4},{8,11},{11,8},{12,15},{15,12},{16,19},{19,... | collective-permute-start | bytes 688136 | tf_op jit(solution)/shard_map/ppermute | solution.py:293
  37.5 0.1 collective-permute-start.12
  37.6 0.7 %collective-permute-done.13.refs_4_ = f32[448,128]{1,0:T(8,128)S(1)} collective-permute-done((f32[448,128]{1,0:T(8,128)S(1)}, f32[448,128]{1,0:T(8,128)S(1)}, u32[]{:S(2)}, u32[]{:S(2)}) %collective-permute-start.13) | collective-permute-done | bytes 229408 | tf_op jit(solution)/shard_map/ppermute | solution.py:293
  38.3 0.7 %collective-permute-start.14 = (f32[448,128]{1,0:T(8,128)S(1)}, f32[448,128]{1,0:T(8,128)S(1)}, u32[]{:S(2)}, u32[]{:S(2)}) collective-permute-start(f32[448,128]{1,0:T(8,128)S(1)} %add.3), channel_id=1, source_target_pairs={{1,2},{2,1},{5,6},{6,5},{9,10},{10,9},{13,14},{14,13},{17,18},{18,... | collective-permute-start | bytes 688136 | tf_op jit(solution)/shard_map/ppermute | solution.py:293
  39.0 6.3 %collective-permute-done.11.refs_1_ = f32[448,128]{1,0:T(8,128)S(1)} collective-permute-done((f32[448,128]{1,0:T(8,128)S(1)}, f32[448,128]{1,0:T(8,128)S(1)}, u32[]{:S(2)}, u32[]{:S(2)}) %collective-permute-start.11) | collective-permute-done | bytes 229408 | tf_op jit(solution)/shard_map/ppermute | solution.py:293
  45.3 4.0 %collective-permute-done.12.refs_2_ = f32[448,128]{1,0:T(8,128)S(1)} collective-permute-done((f32[448,128]{1,0:T(8,128)S(1)}, f32[448,128]{1,0:T(8,128)S(1)}, u32[]{:S(2)}, u32[]{:S(2)}) %collective-permute-start.12) | collective-permute-done | bytes 229408 | tf_op jit(solution)/shard_map/ppermute | solution.py:293
  49.3 0.0 collective-permute-done.14.refs_3_
  49.3 0.9 %shard_map.49 = f32[512,128]{1,0:T(8,128)} custom-call(f32[448,128]{1,0:T(8,128)S(1)} %get-tuple-element.29.refs_0_, f32[448,128]{1,0:T(8,128)S(1)} %collective-permute-done.11.refs_1_, f32[448,128]{1,0:T(8,128)S(1)} %collective-permute-done.12.refs_2_, f32[448,128]{1,0:T(8,128)S(1)} %collective-permute-done.14.refs_3_, ...), custom_call_target="tpu_custom_call" | custom-call | tf_op jit(solution)/shard_map/pallas_call | solution.py:36
  (3 shorter events, 0.1 us)
Async XLA Ops:
  0.0 3.0 %collective-permute-start = (f32[512,512]{1,0:T(8,128)}, f32[512,512]{1,0:T(8,128)S(1)}, u32[]{:S(2)}, u32[]{:S(2)}) collective-permute-start(f32[512,512]{1,0:T(8,128)} %bitcast.5), channel_id=1, source_target_pairs={{0,4},{4,0},{8,12},{12,8},{16,20},{20,16},{24,28},{28,24},{1,5},{5... | collective-permute-start | bytes 3145736 | tf_op jit(solution)/shard_map/ppermute | solution.py:311
  0.5 1.2 %copy-start.1 = (f32[1,1,512,512]{3,2,1,0:T(8,128)S(1)}, f32[1,1,512,512]{3,2,1,0:T(8,128)}, u32[]{:S(2)}) copy-start(f32[1,1,512,512]{3,2,1,0:T(8,128)} %param.3) | copy-start | bytes 3145732
  1.8 6.8 %copy-start = (f32[512,512]{1,0:T(8,128)S(1)}, f32[512,512]{1,0:T(8,128)}, u32[]{:S(2)}) copy-start(f32[512,512]{1,0:T(8,128)} %target.1) | copy-start | bytes 3145732
  3.6 7.3 %collective-permute-start.1 = (f32[64,512]{1,0:T(8,128)S(1)}, f32[64,512]{1,0:T(8,128)S(1)}, u32[]{:S(2)}, u32[]{:S(2)}) collective-permute-start(f32[64,512]{1,0:T(8,128)S(1)} %get-tuple-element.19), channel_id=1, source_target_pairs={{0,8},{4,12},{8,0},{12,4},{16,24},{20,28},{24,16},{28,20},{1,9},{5... | collective-permute-start | bytes 393224 | tf_op jit(solution)/shard_map/ppermute | solution.py:311
  6.5 7.1 %collective-permute-start.3 = (f32[64,512]{1,0:T(8,128)S(1)}, f32[64,512]{1,0:T(8,128)S(1)}, u32[]{:S(2)}, u32[]{:S(2)}) collective-permute-start(f32[64,512]{1,0:T(8,128)S(1)} %get-tuple-element.21), channel_id=1, source_target_pairs={{0,8},{4,12},{8,0},{12,4},{16,24},{20,28},{24,16},{28,20},{1,9},{5... | collective-permute-start | bytes 393224 | tf_op jit(solution)/shard_map/ppermute | solution.py:311
  6.6 9.8 %collective-permute-start.5 = (f32[64,512]{1,0:T(8,128)S(1)}, f32[64,512]{1,0:T(8,128)S(1)}, u32[]{:S(2)}, u32[]{:S(2)}) collective-permute-start(f32[64,512]{1,0:T(8,128)S(1)} %get-tuple-element.22), channel_id=1, source_target_pairs={{0,8},{4,12},{8,0},{12,4},{16,24},{20,28},{24,16},{28,20},{1,9},{5... | collective-permute-start | bytes 393224 | tf_op jit(solution)/shard_map/ppermute | solution.py:311
  8.5 10.5 %collective-permute-start.7 = (f32[64,512]{1,0:T(8,128)S(1)}, f32[64,512]{1,0:T(8,128)S(1)}, u32[]{:S(2)}, u32[]{:S(2)}) collective-permute-start(f32[64,512]{1,0:T(8,128)S(1)} %get-tuple-element.23), channel_id=1, source_target_pairs={{0,8},{4,12},{8,0},{12,4},{16,24},{20,28},{24,16},{28,20},{1,9},{5... | collective-permute-start | bytes 393224 | tf_op jit(solution)/shard_map/ppermute | solution.py:311
  11.4 9.8 %collective-permute-start.2 = (f32[64,512]{1,0:T(8,128)S(1)}, f32[64,512]{1,0:T(8,128)S(1)}, u32[]{:S(2)}, u32[]{:S(2)}) collective-permute-start(f32[64,512]{1,0:T(8,128)S(1)} %shard_map.40), channel_id=1, source_target_pairs={{0,16},{4,20},{8,24},{12,28},{16,0},{20,4},{24,8},{28,12},{1,17},{... | collective-permute-start | bytes 393224 | tf_op jit(solution)/shard_map/ppermute | solution.py:311
  14.0 7.2 %collective-permute-start.4 = (f32[64,512]{1,0:T(8,128)S(1)}, f32[64,512]{1,0:T(8,128)S(1)}, u32[]{:S(2)}, u32[]{:S(2)}) collective-permute-start(f32[64,512]{1,0:T(8,128)S(1)} %shard_map.41), channel_id=1, source_target_pairs={{0,16},{4,20},{8,24},{12,28},{16,0},{20,4},{24,8},{28,12},{1,17},{... | collective-permute-start | bytes 393224 | tf_op jit(solution)/shard_map/ppermute | solution.py:311
  16.8 5.9 %collective-permute-start.6 = (f32[64,512]{1,0:T(8,128)S(1)}, f32[64,512]{1,0:T(8,128)S(1)}, u32[]{:S(2)}, u32[]{:S(2)}) collective-permute-start(f32[64,512]{1,0:T(8,128)S(1)} %shard_map.42), channel_id=1, source_target_pairs={{0,16},{4,20},{8,24},{12,28},{16,0},{20,4},{24,8},{28,12},{1,17},{... | collective-permute-start | bytes 393224 | tf_op jit(solution)/shard_map/ppermute | solution.py:311
  19.5 5.4 %collective-permute-start.8 = (f32[64,512]{1,0:T(8,128)S(1)}, f32[64,512]{1,0:T(8,128)S(1)}, u32[]{:S(2)}, u32[]{:S(2)}) collective-permute-start(f32[64,512]{1,0:T(8,128)S(1)} %shard_map.43), channel_id=1, source_target_pairs={{0,16},{4,20},{8,24},{12,28},{16,0},{20,4},{24,8},{28,12},{1,17},{... | collective-permute-start | bytes 393224 | tf_op jit(solution)/shard_map/ppermute | solution.py:311
  21.1 4.5 %collective-permute-start.10 = (f32[256,512]{1,0:T(8,128)S(1)}, f32[256,512]{1,0:T(8,128)S(1)}, u32[]{:S(2)}, u32[]{:S(2)}) collective-permute-start(f32[256,512]{1,0:T(8,128)S(1)} %shard_map.45.near), channel_id=1, source_target_pairs={{0,4},{4,0},{8,12},{12,8},{16,20},{20,16},{24,28},{28,24},{1,5},{5... | collective-permute-start | bytes 1572872 | tf_op jit(solution)/shard_map/ppermute | solution.py:311
  24.9 2.0 %collective-permute-start.9 = (f32[256,512]{1,0:T(8,128)S(1)}, f32[256,512]{1,0:T(8,128)S(1)}, u32[]{:S(2)}, u32[]{:S(2)}) collective-permute-start(f32[256,512]{1,0:T(8,128)S(1)} %shard_map.44.far), channel_id=1, source_target_pairs={{0,4},{4,0},{8,12},{12,8},{16,20},{20,16},{24,28},{28,24},{1,5},{5... | collective-permute-start | bytes 1572872 | tf_op jit(solution)/shard_map/ppermute | solution.py:311
  29.1 9.3 %collective-permute-start.13 = (f32[448,128]{1,0:T(8,128)S(1)}, f32[448,128]{1,0:T(8,128)S(1)}, u32[]{:S(2)}, u32[]{:S(2)}) collective-permute-start(f32[448,128]{1,0:T(8,128)S(1)} %get-tuple-element.32), channel_id=1, source_target_pairs={{0,1},{1,3},{3,2},{2,0},{4,5},{5,7},{7,6},{6,4},{8,9},{9,11},{11,1... | collective-permute-start | bytes 688136 | tf_op jit(solution)/shard_map/ppermute | solution.py:293
  33.1 12.1 %collective-permute-start.11 = (f32[448,128]{1,0:T(8,128)S(1)}, f32[448,128]{1,0:T(8,128)S(1)}, u32[]{:S(2)}, u32[]{:S(2)}) collective-permute-start(f32[448,128]{1,0:T(8,128)S(1)} %get-tuple-element.30), channel_id=1, source_target_pairs={{0,3},{3,0},{4,7},{7,4},{8,11},{11,8},{12,15},{15,12},{16,19},{19,... | collective-permute-start | bytes 688136 | tf_op jit(solution)/shard_map/ppermute | solution.py:293
  37.5 11.8 %collective-permute-start.12 = (f32[448,128]{1,0:T(8,128)S(1)}, f32[448,128]{1,0:T(8,128)S(1)}, u32[]{:S(2)}, u32[]{:S(2)}) collective-permute-start(f32[448,128]{1,0:T(8,128)S(1)} %get-tuple-element.31), channel_id=1, source_target_pairs={{0,1},{1,0},{2,3},{3,2},{4,5},{5,4},{6,7},{7,6},{8,9},{9,8},{10,11... | collective-permute-start | bytes 688136 | tf_op jit(solution)/shard_map/ppermute | solution.py:293
  38.3 11.0 %collective-permute-start.14 = (f32[448,128]{1,0:T(8,128)S(1)}, f32[448,128]{1,0:T(8,128)S(1)}, u32[]{:S(2)}, u32[]{:S(2)}) collective-permute-start(f32[448,128]{1,0:T(8,128)S(1)} %add.3), channel_id=1, source_target_pairs={{1,2},{2,1},{5,6},{6,5},{9,10},{10,9},{13,14},{14,13},{17,18},{18,... | collective-permute-start | bytes 688136 | tf_op jit(solution)/shard_map/ppermute | solution.py:293

commit v8 on v7

--- a/solution.py
+++ b/solution.py
@@ -183,6 +183,12 @@
     for piece in refs[:-1]:
         refs[-1][at:at + piece.shape[0], :] = piece[...]
         at += piece.shape[0]
+
+
+def near_kernel(*refs):
+    left, joined, high, low = refs[-4:]
+    join_kernel(*refs[:-4], joined)
+    high[...], low[...] = split(left[...])
 
 
 def factor_kernel(near, near_other, right, high, low, full):
@@ -229,13 +235,13 @@
     return weight[...] * (0.5 - bit(turned_level).astype(f32))
 
 
-def first_block_kernel(turned_level, which_of, far, far_other, left, right_high, right_low, weight, half_way, block, full, columns):
+def first_block_kernel(turned_level, which_of, far, far_other, left_high, left_low, right_high, right_low, weight, half_way, block, full, columns):
     place(full, [far], [far_other])
     half_way[...] = product_of(split(full[...]), (right_high[...], right_low[...]))
     rows = columns.shape[0]
     which = which_of(lax.axis_index("ens"))
     at = pl.ds(pl.multiple_of(which * rows, LANES), rows)
-    full[...] = product(left[...], half_way[...])
+    full[...] = product_of((left_high[...], left_low[...]), split(half_way[...]))
     columns[...] = sign(turned_level, weight) * (full[at, :] - full[:, at].T)
     lay_out(block, columns, which, True)
 
@@ -325,13 +331,13 @@
                 *[swap(p, 0) for p in products], *got, *[swap(g, 0) for g in got], left, right, target, scratch=[square])
             (own, left, right), sends = outs[:3], outs[3:]
     far = [swap(p, top) for p in products]
-    near = call(join_kernel, [(order // 2, order)], *got)[0]
+    near, *left_parts = call(near_kernel, [(order // 2, order)] + [(square, bf16)] * 2, *got, left)
     right = call(factor_kernel, [(square, bf16)] * 2, near, swap(near, 0), right, scratch=[square])
     far = call(join_kernel, [(order // 2, order)], *far)[0]
     rows, spread = order // members, order // LANES
     packed = rows == LANES
     block = (rows * spread - packed * rows // 2, LANES)
-    factors = (far, swap(far, 0), left, *right, weights.reshape(1, 1))
+    factors = (far, swap(far, 0), *left_parts, *right, weights.reshape(1, 1))
     if members == 4 and packed:
         half_way, over_two = call(
             functools.partial(first_block_kernel, top - 1, lambda here: here ^ 2), [square, block], *factors,

time: 50.4 us -> 50.4 us (level)
  transfers between devices with their start and end apart: 15 -> 15, of which waited for: 9 -> 9; matrix products, arithmetic and copies ran while one was open for 0% -> 0% of each run, Pallas kernels for 14% -> 15%
where the time goes in v8:
time: 50.4 us; the launch traced here: 50.2 us
  starting transfers between devices  20.9 us (41%)
  waiting for transfers between devices  16.2 us (32%)
  Pallas kernels  11 us (22%)
  local copies, waits for them, and re-layouts  1.23 us (2%)
  between operations  0.8 us (2%)
    ppermute x11, starting transfers between devices, swap(): return lax.ppermute(x, 'tm', [(i, i ^ 1 << level) for i in range(slices)])  13.6 us
    pallas_call x13, Pallas kernels, call(): pl.pallas_call(kernel, out_shape=[jax.ShapeDtypeStruct(s, f32) if isinsta...  11 us
    ppermute x4, waiting for transfers between devices, move(): return lax.ppermute(x, 'ens', pairs)  11 us
    ppermute x4, starting transfers between devices, move(): return lax.ppermute(x, 'ens', pairs)  7.29 us
    ppermute x11, waiting for transfers between devices, swap(): return lax.ppermute(x, 'tm', [(i, i ^ 1 << level) for i in range(slices)])  5.23 us
    unnamed x4, local copies, waits for them, and re-layouts  1.23 us
  transfers between devices with their start and end apart: 15, of which 9 were waited for; matrix products, arithmetic and copies ran while one was open for 0% of the time, Pallas kernels for 15%

profile of v8, /device:TPU:0, one launch (start us, length us, event | category | flops | bytes accessed | tf_op | source)
XLA Modules:
  0.0 50.2 jit_solution(1601693262684705422)
XLA Ops:
  0.0 0.5 collective-permute-start
  0.5 0.0 copy-start.1
  0.5 1.2 %copy-done.1 = f32[1,1,512,512]{3,2,1,0:T(8,128)S(1)} copy-done((f32[1,1,512,512]{3,2,1,0:T(8,128)S(1)}, f32[1,1,512,512]{3,2,1,0:T(8,128)}, u32[]{:S(2)}) %copy-start.1) | copy-done | bytes 1048600
  1.7 0.1 shard_map.37.mine
  1.8 0.0 copy-start
  1.8 1.2 %collective-permute-done.other = f32[512,512]{1,0:T(8,128)S(1)} collective-permute-done((f32[512,512]{1,0:T(8,128)}, f32[512,512]{1,0:T(8,128)S(1)}, u32[]{:S(2)}, u32[]{:S(2)}) %collective-permute-start) | collective-permute-done | bytes 1048608 | tf_op jit(solution)/shard_map/ppermute | solution.py:317
  3.0 0.7 %shard_map.38 = (f32[64,512]{1,0:T(8,128)S(1)}, f32[64,512]{1,0:T(8,128)S(1)}, f32[64,512]{1,0:T(8,128)S(1)}, f32[64,512]{1,0:T(8,128)S(1)}) custom-call(f32[512,512]{1,0:T(8,128)S(1)} %shard_map.37.mine, f32[512,512]{1,0:T(8,128)S(1)} %collective-permute-done.other), custom_call_target="tpu_custom_call" | custom-call | tf_op jit(solution)/shard_map/pallas_call | solution.py:36
  3.6 2.9 %collective-permute-start.1 = (f32[64,512]{1,0:T(8,128)S(1)}, f32[64,512]{1,0:T(8,128)S(1)}, u32[]{:S(2)}, u32[]{:S(2)}) collective-permute-start(f32[64,512]{1,0:T(8,128)S(1)} %get-tuple-element.22), channel_id=1, source_target_pairs={{0,8},{4,12},{8,0},{12,4},{16,24},{20,28},{24,16},{28,20},{1,9},{5... | collective-permute-start | bytes 393224 | tf_op jit(solution)/shard_map/ppermute | solution.py:317
  6.5 0.1 collective-permute-start.3
  6.6 1.9 %collective-permute-start.5 = (f32[64,512]{1,0:T(8,128)S(1)}, f32[64,512]{1,0:T(8,128)S(1)}, u32[]{:S(2)}, u32[]{:S(2)}) collective-permute-start(f32[64,512]{1,0:T(8,128)S(1)} %get-tuple-element.25), channel_id=1, source_target_pairs={{0,8},{4,12},{8,0},{12,4},{16,24},{20,28},{24,16},{28,20},{1,9},{5... | collective-permute-start | bytes 393224 | tf_op jit(solution)/shard_map/ppermute | solution.py:317
  8.5 0.1 collective-permute-start.7
  8.6 0.0 copy-done
  8.6 2.3 %shard_map.39 = (f32[512,512]{1,0:T(8,128)S(1)}, f32[512,512]{1,0:T(8,128)S(1)}, f32[512,512]{1,0:T(8,128)S(1)}) custom-call(f32[512,512]{1,0:T(8,128)S(1)} %shard_map.37.mine, f32[512,512]{1,0:T(8,128)S(1)} %collective-permute-done.other, f32[512,512]{1,0:T(8,128)S(1)} %copy-done), custom_call_target="tpu_custom_call" | custom-call | tf_op jit(solution)/shard_map/pallas_call | solution.py:36
  10.9 0.0 collective-permute-done.1.got.refs_0_
  11.0 0.4 shard_map.40
  11.4 2.0 %collective-permute-start.2 = (f32[64,512]{1,0:T(8,128)S(1)}, f32[64,512]{1,0:T(8,128)S(1)}, u32[]{:S(2)}, u32[]{:S(2)}) collective-permute-start(f32[64,512]{1,0:T(8,128)S(1)} %shard_map.40), channel_id=1, source_target_pairs={{0,16},{4,20},{8,24},{12,28},{16,0},{20,4},{24,8},{28,12},{1,17},{... | collective-permute-start | bytes 393224 | tf_op jit(solution)/shard_map/ppermute | solution.py:317
  13.4 0.2 collective-permute-done.3.got.refs_1_
  13.6 0.4 shard_map.41
  14.0 2.2 %collective-permute-start.4 = (f32[64,512]{1,0:T(8,128)S(1)}, f32[64,512]{1,0:T(8,128)S(1)}, u32[]{:S(2)}, u32[]{:S(2)}) collective-permute-start(f32[64,512]{1,0:T(8,128)S(1)} %shard_map.41), channel_id=1, source_target_pairs={{0,16},{4,20},{8,24},{12,28},{16,0},{20,4},{24,8},{28,12},{1,17},{... | collective-permute-start | bytes 393224 | tf_op jit(solution)/shard_map/ppermute | solution.py:317
  16.2 0.2 collective-permute-done.5.got.refs_2_
  16.4 0.4 shard_map.42
  16.8 2.2 %collective-permute-start.6 = (f32[64,512]{1,0:T(8,128)S(1)}, f32[64,512]{1,0:T(8,128)S(1)}, u32[]{:S(2)}, u32[]{:S(2)}) collective-permute-start(f32[64,512]{1,0:T(8,128)S(1)} %shard_map.42), channel_id=1, source_target_pairs={{0,16},{4,20},{8,24},{12,28},{16,0},{20,4},{24,8},{28,12},{1,17},{... | collective-permute-start | bytes 393224 | tf_op jit(solution)/shard_map/ppermute | solution.py:317
  19.0 0.0 collective-permute-done.7.got.refs_3_
  19.0 0.4 shard_map.43
  19.5 1.6 %collective-permute-start.8 = (f32[64,512]{1,0:T(8,128)S(1)}, f32[64,512]{1,0:T(8,128)S(1)}, u32[]{:S(2)}, u32[]{:S(2)}) collective-permute-start(f32[64,512]{1,0:T(8,128)S(1)} %shard_map.43), channel_id=1, source_target_pairs={{0,16},{4,20},{8,24},{12,28},{16,0},{20,4},{24,8},{28,12},{1,17},{... | collective-permute-start | bytes 393224 | tf_op jit(solution)/shard_map/ppermute | solution.py:317
  21.0 0.2 shard_map.45
  21.2 0.1 collective-permute-start.10
  21.3 0.0 collective-permute-done.2.refs_0_
  21.3 0.0 collective-permute-done.4.refs_1_
  21.3 1.4 %collective-permute-done.6.refs_2_ = f32[64,512]{1,0:T(8,128)S(1)} collective-permute-done((f32[64,512]{1,0:T(8,128)S(1)}, f32[64,512]{1,0:T(8,128)S(1)}, u32[]{:S(2)}, u32[]{:S(2)}) %collective-permute-start.6) | collective-permute-done | bytes 131104 | tf_op jit(solution)/shard_map/ppermute | solution.py:317
  22.7 2.1 %collective-permute-done.8.refs_3_ = f32[64,512]{1,0:T(8,128)S(1)} collective-permute-done((f32[64,512]{1,0:T(8,128)S(1)}, f32[64,512]{1,0:T(8,128)S(1)}, u32[]{:S(2)}, u32[]{:S(2)}) %collective-permute-start.8) | collective-permute-done | bytes 131104 | tf_op jit(solution)/shard_map/ppermute | solution.py:317
  24.9 0.1 collective-permute-start.9
  25.6 0.0 collective-permute-done.10.near_other
  25.6 1.1 %shard_map.46 = (bf16[512,512]{1,0:T(8,128)(2,1)S(1)}, bf16[512,512]{1,0:T(8,128)(2,1)S(1)}) custom-call(f32[256,512]{1,0:T(8,128)S(1)} %get-tuple-element.30.near, f32[256,512]{1,0:T(8,128)S(1)} %collective-permute-done.10.near_other, f32[512,512]{1,0:T(8,128)S(1)} %get-tuple-element.31.right), custom_call_target="tpu_custom_call" | custom-call | tf_op jit(solution)/shard_map/pallas_call | solution.py:36
  26.7 0.2 collective-permute-done.9.far_other
  26.9 2.2 %shard_map.47 = (f32[512,512]{1,0:T(8,128)S(1)}, f32[448,128]{1,0:T(8,128)S(1)}) custom-call(f32[256,512]{1,0:T(8,128)S(1)} %shard_map.44.far, f32[256,512]{1,0:T(8,128)S(1)} %collective-permute-done.9.far_other, bf16[512,512]{1,0:T(8,128)(2,1)S(1)} %get-tuple-element.28.left_high, bf16[512,512]{1,0:T(8,128)(2,1)S(1)} %get-tuple-element.29.left_low, ...), custom_call_target="tpu_custom_call" | custom-call | tf_op jit(solution)/shard_map/pallas_call | solution.py:36
  29.1 2.2 %collective-permute-start.13 = (f32[448,128]{1,0:T(8,128)S(1)}, f32[448,128]{1,0:T(8,128)S(1)}, u32[]{:S(2)}, u32[]{:S(2)}) collective-permute-start(f32[448,128]{1,0:T(8,128)S(1)} %get-tuple-element.38), channel_id=1, source_target_pairs={{0,1},{1,3},{3,2},{2,0},{4,5},{5,7},{7,6},{6,4},{8,9},{9,11},{11,1... | collective-permute-start | bytes 688136 | tf_op jit(solution)/shard_map/ppermute | solution.py:299
  31.2 1.9 %shard_map.48 = (f32[448,128]{1,0:T(8,128)S(1)}, f32[448,128]{1,0:T(8,128)S(1)}, f32[448,128]{1,0:T(8,128)S(1)}) custom-call(f32[512,512]{1,0:T(8,128)S(1)} %get-tuple-element.34.half_way, f32[512,512]{1,0:T(8,128)S(1)} %get-tuple-element.27.refs_4_.left, f32[1,1]{1,0:T(1,128)} %bitcast.4.weight), custom_call_target="tpu_custom_call" | custom-call | tf_op jit(solution)/shard_map/pallas_call | solution.py:36
  33.1 4.4 %collective-permute-start.11 = (f32[448,128]{1,0:T(8,128)S(1)}, f32[448,128]{1,0:T(8,128)S(1)}, u32[]{:S(2)}, u32[]{:S(2)}) collective-permute-start(f32[448,128]{1,0:T(8,128)S(1)} %get-tuple-element.36), channel_id=1, source_target_pairs={{0,3},{3,0},{4,7},{7,4},{8,11},{11,8},{12,15},{15,12},{16,19},{19,... | collective-permute-start | bytes 688136 | tf_op jit(solution)/shard_map/ppermute | solution.py:299
  37.5 0.1 collective-permute-start.12
  37.6 0.7 %collective-permute-done.13.refs_4_ = f32[448,128]{1,0:T(8,128)S(1)} collective-permute-done((f32[448,128]{1,0:T(8,128)S(1)}, f32[448,128]{1,0:T(8,128)S(1)}, u32[]{:S(2)}, u32[]{:S(2)}) %collective-permute-start.13) | collective-permute-done | bytes 229408 | tf_op jit(solution)/shard_map/ppermute | solution.py:299
  38.4 0.7 %collective-permute-start.14 = (f32[448,128]{1,0:T(8,128)S(1)}, f32[448,128]{1,0:T(8,128)S(1)}, u32[]{:S(2)}, u32[]{:S(2)}) collective-permute-start(f32[448,128]{1,0:T(8,128)S(1)} %add.3), channel_id=1, source_target_pairs={{1,2},{2,1},{5,6},{6,5},{9,10},{10,9},{13,14},{14,13},{17,18},{18,... | collective-permute-start | bytes 688136 | tf_op jit(solution)/shard_map/ppermute | solution.py:299
  39.0 6.3 %collective-permute-done.11.refs_1_ = f32[448,128]{1,0:T(8,128)S(1)} collective-permute-done((f32[448,128]{1,0:T(8,128)S(1)}, f32[448,128]{1,0:T(8,128)S(1)}, u32[]{:S(2)}, u32[]{:S(2)}) %collective-permute-start.11) | collective-permute-done | bytes 229408 | tf_op jit(solution)/shard_map/ppermute | solution.py:299
  45.3 4.0 %collective-permute-done.12.refs_2_ = f32[448,128]{1,0:T(8,128)S(1)} collective-permute-done((f32[448,128]{1,0:T(8,128)S(1)}, f32[448,128]{1,0:T(8,128)S(1)}, u32[]{:S(2)}, u32[]{:S(2)}) %collective-permute-start.12) | collective-permute-done | bytes 229408 | tf_op jit(solution)/shard_map/ppermute | solution.py:299
  49.3 0.0 collective-permute-done.14.refs_3_
  49.3 0.9 %shard_map.49 = f32[512,128]{1,0:T(8,128)} custom-call(f32[448,128]{1,0:T(8,128)S(1)} %get-tuple-element.35.refs_0_, f32[448,128]{1,0:T(8,128)S(1)} %collective-permute-done.11.refs_1_, f32[448,128]{1,0:T(8,128)S(1)} %collective-permute-done.12.refs_2_, f32[448,128]{1,0:T(8,128)S(1)} %collective-permute-done.14.refs_3_, ...), custom_call_target="tpu_custom_call" | custom-call | tf_op jit(solution)/shard_map/pallas_call | solution.py:36
  (2 shorter events, 0.1 us)
Async XLA Ops:
  0.0 3.0 %collective-permute-start = (f32[512,512]{1,0:T(8,128)}, f32[512,512]{1,0:T(8,128)S(1)}, u32[]{:S(2)}, u32[]{:S(2)}) collective-permute-start(f32[512,512]{1,0:T(8,128)} %bitcast.5), channel_id=1, source_target_pairs={{0,4},{4,0},{8,12},{12,8},{16,20},{20,16},{24,28},{28,24},{1,5},{5... | collective-permute-start | bytes 3145736 | tf_op jit(solution)/shard_map/ppermute | solution.py:317
  0.5 1.2 %copy-start.1 = (f32[1,1,512,512]{3,2,1,0:T(8,128)S(1)}, f32[1,1,512,512]{3,2,1,0:T(8,128)}, u32[]{:S(2)}) copy-start(f32[1,1,512,512]{3,2,1,0:T(8,128)} %param.3) | copy-start | bytes 3145732
  1.8 6.8 %copy-start = (f32[512,512]{1,0:T(8,128)S(1)}, f32[512,512]{1,0:T(8,128)}, u32[]{:S(2)}) copy-start(f32[512,512]{1,0:T(8,128)} %target.1) | copy-start | bytes 3145732
  3.6 7.3 %collective-permute-start.1 = (f32[64,512]{1,0:T(8,128)S(1)}, f32[64,512]{1,0:T(8,128)S(1)}, u32[]{:S(2)}, u32[]{:S(2)}) collective-permute-start(f32[64,512]{1,0:T(8,128)S(1)} %get-tuple-element.22), channel_id=1, source_target_pairs={{0,8},{4,12},{8,0},{12,4},{16,24},{20,28},{24,16},{28,20},{1,9},{5... | collective-permute-start | bytes 393224 | tf_op jit(solution)/shard_map/ppermute | solution.py:317
  6.5 7.1 %collective-permute-start.3 = (f32[64,512]{1,0:T(8,128)S(1)}, f32[64,512]{1,0:T(8,128)S(1)}, u32[]{:S(2)}, u32[]{:S(2)}) collective-permute-start(f32[64,512]{1,0:T(8,128)S(1)} %get-tuple-element.24), channel_id=1, source_target_pairs={{0,8},{4,12},{8,0},{12,4},{16,24},{20,28},{24,16},{28,20},{1,9},{5... | collective-permute-start | bytes 393224 | tf_op jit(solution)/shard_map/ppermute | solution.py:317
  6.6 9.8 %collective-permute-start.5 = (f32[64,512]{1,0:T(8,128)S(1)}, f32[64,512]{1,0:T(8,128)S(1)}, u32[]{:S(2)}, u32[]{:S(2)}) collective-permute-start(f32[64,512]{1,0:T(8,128)S(1)} %get-tuple-element.25), channel_id=1, source_target_pairs={{0,8},{4,12},{8,0},{12,4},{16,24},{20,28},{24,16},{28,20},{1,9},{5... | collective-permute-start | bytes 393224 | tf_op jit(solution)/shard_map/ppermute | solution.py:317
  8.5 10.5 %collective-permute-start.7 = (f32[64,512]{1,0:T(8,128)S(1)}, f32[64,512]{1,0:T(8,128)S(1)}, u32[]{:S(2)}, u32[]{:S(2)}) collective-permute-start(f32[64,512]{1,0:T(8,128)S(1)} %get-tuple-element.26), channel_id=1, source_target_pairs={{0,8},{4,12},{8,0},{12,4},{16,24},{20,28},{24,16},{28,20},{1,9},{5... | collective-permute-start | bytes 393224 | tf_op jit(solution)/shard_map/ppermute | solution.py:317
  11.4 9.9 %collective-permute-start.2 = (f32[64,512]{1,0:T(8,128)S(1)}, f32[64,512]{1,0:T(8,128)S(1)}, u32[]{:S(2)}, u32[]{:S(2)}) collective-permute-start(f32[64,512]{1,0:T(8,128)S(1)} %shard_map.40), channel_id=1, source_target_pairs={{0,16},{4,20},{8,24},{12,28},{16,0},{20,4},{24,8},{28,12},{1,17},{... | collective-permute-start | bytes 393224 | tf_op jit(solution)/shard_map/ppermute | solution.py:317
  14.0 7.3 %collective-permute-start.4 = (f32[64,512]{1,0:T(8,128)S(1)}, f32[64,512]{1,0:T(8,128)S(1)}, u32[]{:S(2)}, u32[]{:S(2)}) collective-permute-start(f32[64,512]{1,0:T(8,128)S(1)} %shard_map.41), channel_id=1, source_target_pairs={{0,16},{4,20},{8,24},{12,28},{16,0},{20,4},{24,8},{28,12},{1,17},{... | collective-permute-start | bytes 393224 | tf_op jit(solution)/shard_map/ppermute | solution.py:317
  16.8 5.9 %collective-permute-start.6 = (f32[64,512]{1,0:T(8,128)S(1)}, f32[64,512]{1,0:T(8,128)S(1)}, u32[]{:S(2)}, u32[]{:S(2)}) collective-permute-start(f32[64,512]{1,0:T(8,128)S(1)} %shard_map.42), channel_id=1, source_target_pairs={{0,16},{4,20},{8,24},{12,28},{16,0},{20,4},{24,8},{28,12},{1,17},{... | collective-permute-start | bytes 393224 | tf_op jit(solution)/shard_map/ppermute | solution.py:317
  19.5 5.4 %collective-permute-start.8 = (f32[64,512]{1,0:T(8,128)S(1)}, f32[64,512]{1,0:T(8,128)S(1)}, u32[]{:S(2)}, u32[]{:S(2)}) collective-permute-start(f32[64,512]{1,0:T(8,128)S(1)} %shard_map.43), channel_id=1, source_target_pairs={{0,16},{4,20},{8,24},{12,28},{16,0},{20,4},{24,8},{28,12},{1,17},{... | collective-permute-start | bytes 393224 | tf_op jit(solution)/shard_map/ppermute | solution.py:317
  21.2 4.4 %collective-permute-start.10 = (f32[256,512]{1,0:T(8,128)S(1)}, f32[256,512]{1,0:T(8,128)S(1)}, u32[]{:S(2)}, u32[]{:S(2)}) collective-permute-start(f32[256,512]{1,0:T(8,128)S(1)} %get-tuple-element.30.near), channel_id=1, source_target_pairs={{0,4},{4,0},{8,12},{12,8},{16,20},{20,16},{24,28},{28,24},{1,5},{5... | collective-permute-start | bytes 1572872 | tf_op jit(solution)/shard_map/ppermute | solution.py:317
  24.9 2.0 %collective-permute-start.9 = (f32[256,512]{1,0:T(8,128)S(1)}, f32[256,512]{1,0:T(8,128)S(1)}, u32[]{:S(2)}, u32[]{:S(2)}) collective-permute-start(f32[256,512]{1,0:T(8,128)S(1)} %shard_map.44.far), channel_id=1, source_target_pairs={{0,4},{4,0},{8,12},{12,8},{16,20},{20,16},{24,28},{28,24},{1,5},{5... | collective-permute-start | bytes 1572872 | tf_op jit(solution)/shard_map/ppermute | solution.py:317
  29.1 9.3 %collective-permute-start.13 = (f32[448,128]{1,0:T(8,128)S(1)}, f32[448,128]{1,0:T(8,128)S(1)}, u32[]{:S(2)}, u32[]{:S(2)}) collective-permute-start(f32[448,128]{1,0:T(8,128)S(1)} %get-tuple-element.38), channel_id=1, source_target_pairs={{0,1},{1,3},{3,2},{2,0},{4,5},{5,7},{7,6},{6,4},{8,9},{9,11},{11,1... | collective-permute-start | bytes 688136 | tf_op jit(solution)/shard_map/ppermute | solution.py:299
  33.1 12.1 %collective-permute-start.11 = (f32[448,128]{1,0:T(8,128)S(1)}, f32[448,128]{1,0:T(8,128)S(1)}, u32[]{:S(2)}, u32[]{:S(2)}) collective-permute-start(f32[448,128]{1,0:T(8,128)S(1)} %get-tuple-element.36), channel_id=1, source_target_pairs={{0,3},{3,0},{4,7},{7,4},{8,11},{11,8},{12,15},{15,12},{16,19},{19,... | collective-permute-start | bytes 688136 | tf_op jit(solution)/shard_map/ppermute | solution.py:299
  37.5 11.8 %collective-permute-start.12 = (f32[448,128]{1,0:T(8,128)S(1)}, f32[448,128]{1,0:T(8,128)S(1)}, u32[]{:S(2)}, u32[]{:S(2)}) collective-permute-start(f32[448,128]{1,0:T(8,128)S(1)} %get-tuple-element.37), channel_id=1, source_target_pairs={{0,1},{1,0},{2,3},{3,2},{4,5},{5,4},{6,7},{7,6},{8,9},{9,8},{10,11... | collective-permute-start | bytes 688136 | tf_op jit(solution)/shard_map/ppermute | solution.py:299
  38.4 11.0 %collective-permute-start.14 = (f32[448,128]{1,0:T(8,128)S(1)}, f32[448,128]{1,0:T(8,128)S(1)}, u32[]{:S(2)}, u32[]{:S(2)}) collective-permute-start(f32[448,128]{1,0:T(8,128)S(1)} %add.3), channel_id=1, source_target_pairs={{1,2},{2,1},{5,6},{6,5},{9,10},{10,9},{13,14},{14,13},{17,18},{18,... | collective-permute-start | bytes 688136 | tf_op jit(solution)/shard_map/ppermute | solution.py:299
